TPU v7x, 32 devices: a whole 2x2x4 slice. The times are simulated.
32 devices in a mesh: tok: 4 (over y, core), feat: 8 (over z, x).
Axes of the slice: x: 2, y: 2, z: 4, core: 2. Of those that a mesh axis runs over, the one named last changes fastest.
Arguments:
- span_input: bfloat16 [768, 16384], P('tok', 'feat'), may hold values from -6 to 6
- span_output: bfloat16 [768, 16384], P('tok', 'feat'), may hold values from -6 to 6
- block_pairs: int32 [384, 2], replicated, may hold values from 0 to 127, as said below
Outputs:
- gram: float32 [384, 128, 128], P(('tok', 'feat'))
- cross: float32 [384, 128, 128], P(('tok', 'feat'))
Inputs may be any that keep to these rules, and one draw needn't show every extreme that they name: `block_pairs`: the pairs are distinct; each of the 128 row blocks appears in exactly 3 pairs, one of them with itself as column block.
All inputs are finite; a program needn't handle non-finite values.
Results may differ from a plain program's by a relative error of at most 0.0003.
Values may be sent and summed in bfloat16 or wider, within the bound.
No kernel may reach another device: no remote copies, remote signals or barrier semaphores. Data moves between devices by JAX's collectives and lax.ppermute only.
A program may use at most 128 MiB of HBM per device.

v0:
```python
import jax
import jax.numpy as jnp
from jax import lax
from jax.sharding import PartitionSpec as P

BLK = 128
PAIR_DEV = 12
NB = 128


def body(span_input, span_output, block_pairs):
    tok_count = lax.axis_size("tok")
    feat_count = lax.axis_size("feat")
    feat_index = lax.axis_index("feat")
    tok_rows = span_input.shape[0]
    inverse = 1.0 / (tok_count * tok_rows)
    gathered_in, gathered_out = (
        lax.all_gather(span_input, "feat", axis=1, tiled=True),
        lax.all_gather(span_output, "feat", axis=1, tiled=True),
    )
    blocks_in = gathered_in.reshape(tok_rows, NB, BLK)
    blocks_out = gathered_out.reshape(tok_rows, NB, BLK)
    slot_ids = (
        (jnp.arange(tok_count, dtype=jnp.int32)[:, None] * feat_count + feat_index) * PAIR_DEV
        + jnp.arange(PAIR_DEV, dtype=jnp.int32)[None, :]
    ).reshape(-1)
    column_pairs = jnp.take(block_pairs, slot_ids, axis=0)
    left_tiles = jnp.take(blocks_in, column_pairs[:, 0], axis=1)
    right_in = jnp.take(blocks_in, column_pairs[:, 1], axis=1)
    right_out = jnp.take(blocks_out, column_pairs[:, 1], axis=1)
    selected = jnp.stack([left_tiles, right_in, right_out], 0).reshape(
        3, tok_rows, tok_count, PAIR_DEV, BLK
    )
    received = lax.all_to_all(selected, "tok", split_axis=2, concat_axis=1, tiled=True)
    gram_tiles = (
        jnp.einsum(
            "tkb,tkc->kbc", received[0, :, 0], received[1, :, 0], preferred_element_type=jnp.float32
        )
        * inverse
    )
    cross_tiles = (
        jnp.einsum(
            "tkb,tkc->kbc", received[0, :, 0], received[2, :, 0], preferred_element_type=jnp.float32
        )
        * inverse
    )
    summed = jnp.stack([gram_tiles, cross_tiles], 1)
    return (summed[:, 0], summed[:, 1])


def solution(mesh):
    return jax.shard_map(
        body,
        mesh=mesh,
        in_specs=(P("tok", "feat"), P("tok", "feat"), P()),
        out_specs=(P(("tok", "feat"), None, None), P(("tok", "feat"), None, None)),
        check_vma=False,
    )
```

profile of v0, /device:TPU:25, one launch (start us, length us, event | category | flops | bytes accessed | tf_op | source)
XLA Modules:
  0.0 328.4 jit_solution(2681167141525791077)
XLA Ops:
  7.2 0.0 all-gather.5.cloned.1.call-start
  7.2 0.7 all-gather.5.cloned.1.call-update
  7.9 0.0 all-gather.3.cloned.1.call-start
  7.9 0.7 all-gather.3.cloned.1.call-update
  8.7 0.1 iota_add_fusion
  8.7 0.1 add.75
  8.8 0.1 add.72
  8.9 0.8 copy.22
  9.8 0.6 gather_fusion
  10.3 0.1 broadcast_select_fusion.3
  10.4 0.2 slice_reduce_fusion.1
  10.7 97.8 %all-gather.5.cloned.1.call-done = bf16[192,16384]{1,0:T(8,128)(2,1)} async-done(((bf16[192,2048]{1,0:T(8,128)(2,1)}), bf16[192,16384]{1,0:T(8,128)(2,1)}) %all-gather.5.cloned.1.call-update) | async-done | bytes 6291472 | tf_op jit(solution)/shard_map/all_gather | solution.py:19
  108.5 7.2 %copy_bitcast_fusion.1 = bf16[192,128,128]{2,0,1:T(8,128)(2,1)} fusion(bf16[192,16384]{1,0:T(8,128)(2,1)} %all-gather.5.cloned.1.call-done), kind=kLoop, calls=%fused_computation.6 | loop fusion | bytes 12582912 | tf_op jit(solution)/shard_map/reshape | solution.py:22
  115.7 5.2 %gather_fusion.3 = bf16[48,192,128]{2,1,0:T(8,128)(2,1)} fusion(bf16[192,128,128]{2,0,1:T(8,128)(2,1)} %copy_bitcast_fusion.1, s32[1024]{0:T(1024)S(1)} %pad_clamp_fusion), kind=kCustom, calls=%fused_computation.2.clone | custom fusion | bytes 4718784 | tf_op jit(solution)/shard_map/jit(_take)/gather | solution.py:30
  120.9 87.0 %all-gather.3.cloned.1.call-done = bf16[192,16384]{1,0:T(8,128)(2,1)} async-done(((bf16[192,2048]{1,0:T(8,128)(2,1)}), bf16[192,16384]{1,0:T(8,128)(2,1)}) %all-gather.3.cloned.1.call-update) | async-done | bytes 6291472 | tf_op jit(solution)/shard_map/all_gather | solution.py:18
  207.9 7.3 %copy_bitcast_fusion.2 = bf16[192,128,128]{2,0,1:T(8,128)(2,1)} fusion(bf16[192,16384]{1,0:T(8,128)(2,1)} %all-gather.3.cloned.1.call-done), kind=kLoop, calls=%fused_computation.7 | loop fusion | bytes 12582912 | tf_op jit(solution)/shard_map/reshape | solution.py:21
  215.2 5.1 %gather_fusion.2 = bf16[48,192,128]{2,1,0:T(8,128)(2,1)} fusion(bf16[192,128,128]{2,0,1:T(8,128)(2,1)} %copy_bitcast_fusion.2, s32[1024]{0:T(1024)S(1)} %pad_clamp_fusion), kind=kCustom, calls=%fused_computation.1.clone | custom fusion | bytes 4718784 | tf_op jit(solution)/shard_map/jit(_take)/gather | solution.py:29
  220.3 3.8 %gather_fusion.1 = bf16[48,192,128]{2,1,0:T(8,128)(2,1)S(1)} fusion(bf16[192,128,128]{2,0,1:T(8,128)(2,1)} %copy_bitcast_fusion.2, s32[1024]{0:T(1024)S(1)} %pad_clamp_fusion.1), kind=kCustom, calls=%fused_computation.clone | custom fusion | bytes 4718784 | tf_op jit(solution)/shard_map/jit(_take)/gather | solution.py:28
  224.1 0.0 copy-start
  224.1 0.0 copy-start.1
  224.2 0.3 broadcast_select_fusion.2
  224.5 1.3 copy-done
  225.8 0.7 copy-done.1
  226.5 0.5 broadcast_select_fusion.1
  227.0 0.8 pad_maximum_fusion
  227.8 1.4 copy.26
  229.3 82.2 %all_to_all.15 = bf16[3,192,4,12,128]{4,1,3,0,2:T(8,128)(2,1)} all-to-all(bf16[3,192,4,12,128]{4,1,3,0,2:T(8,128)(2,1)S(1)} %copy.26), channel_id=1, replica_groups=mesh['tok'=4,'feat'=8] {'tok'}, dimensions={2} | all-to-all | bytes 14155776 | tf_op jit(solution)/shard_map/all_to_all | solution.py:34
  311.5 5.1 %copy.37 = bf16[3,192,4,12,128]{4,1,2,3,0:T(8,128)(2,1)S(1)} copy(bf16[3,192,4,12,128]{4,1,3,0,2:T(8,128)(2,1)} %all_to_all.15) | data formatting | bytes 14155776 | tf_op jit(solution)/shard_map/all_to_all | solution.py:34
  316.6 1.4 fusion.1
  318.0 1.7 convolution_multiply_fusion
  319.8 1.7 convolution_multiply_fusion.1
  (9 shorter events, 0.1 us)
Async XLA Ops:
  7.2 101.3 %all-gather.5.cloned.1.call-start = ((), (), s32[]{:S(2)}) async-start(), calls=%async_computation.2 | async-start | bytes 7077888 | tf_op jit(solution)/shard_map/all_gather | solution.py:19
  7.9 200.0 %all-gather.3.cloned.1.call-start = ((), (), s32[]{:S(2)}) async-start(), calls=%async_computation.1 | async-start | bytes 7077888 | tf_op jit(solution)/shard_map/all_gather | solution.py:18
  224.1 1.7 copy-start
  224.1 2.4 copy-start.1
Sparse Core Ops, SparseCore 0:
  10.2 98.2 all-gather.4
  110.7 97.2 all-gather.2
where the time goes:
time: 333 us; the launch traced here: 328 us
  waiting for transfers between devices  186 us (56%)
  blocking collectives  82.2 us (25%)
  local copies, waits for them, and re-layouts  40.4 us (12%)
  between operations  14.2 us (4%)
  matrix products  3.47 us (1%)
    all_gather x1, waiting for transfers between devices, body(): lax.all_gather(span_output, 'feat', axis=1, tiled=True)  97.8 us
    all_gather x1, waiting for transfers between devices, body(): lax.all_gather(span_input, 'feat', axis=1, tiled=True)  87 us
    all_to_all x1, blocking collectives, body(): lax.all_to_all(selected, 'tok', split_axis=2, concat_axis=1, tiled=True)  82.2 us
    reshape x1, local copies, waits for them, and re-layouts, body(): blocks_in = gathered_in.reshape(tok_rows, NB, BLK)  7.29 us
    reshape x1, local copies, waits for them, and re-layouts, body(): blocks_out = gathered_out.reshape(tok_rows, NB, BLK)  7.19 us
  transfers between devices with their start and end apart: 2, of which 2 were waited for; matrix products, arithmetic and copies ran while one was open for 4% of the time, Pallas kernels for 0%

commit v1 on v0

v1 whole, which is shorter than its diff:
```python
import functools

import jax
import jax.numpy as jnp
from jax import lax
from jax.experimental import pallas as pl
from jax.experimental.pallas import tpu as pltpu
from jax.sharding import PartitionSpec as P

BLK = 128


def select_kernel(line, outs, line_ref, table_ref, *refs):
    pieces = refs[: 2 * line - 1]
    out_refs = refs[2 * line - 1 : 2 * line - 1 + outs]
    held, sems = refs[2 * line - 1 + outs :]
    me = line_ref[0]
    per = held.shape[0] // line

    def copy(piece, place):
        return pltpu.make_async_copy(
            pieces[piece], held.at[pl.ds(place * per, per)], sems.at[place]
        )

    def each(action):
        action(copy(0, me))
        for k in range(1, line):

            @pl.when(me >= k)
            def _(k=k):
                action(copy(k, me - k))

            @pl.when(me + k < line)
            def _(k=k):
                action(copy(line - 1 + k, me + k))

    each(lambda c: c.start())
    each(lambda c: c.wait())
    for o, out_ref in enumerate(out_refs):
        count = out_ref.shape[0]

        @pl.loop(0, count, unroll=4)
        def _(i, o=o, out_ref=out_ref, count=count):
            out_ref[i] = held[table_ref[o * count + i]]


def select_tiles(me, table, pieces, outs, line):
    blocks, rows, blk = pieces[0].shape
    count = table.shape[0] // outs
    return pl.pallas_call(
        functools.partial(select_kernel, line, outs),
        out_shape=[jax.ShapeDtypeStruct((count, rows, blk), pieces[0].dtype)] * outs,
        in_specs=[pl.BlockSpec(memory_space=pltpu.SMEM)] * 2
        + [pl.BlockSpec(memory_space=pl.ANY)] * len(pieces),
        out_specs=[pl.BlockSpec(memory_space=pltpu.VMEM)] * outs,
        scratch_shapes=[
            pltpu.VMEM((line * blocks, rows, blk), pieces[0].dtype),
            pltpu.SemaphoreType.DMA((line,)),
        ],
        compiler_params=pltpu.CompilerParams(vmem_limit_bytes=40 << 20),
        name="select_tiles",
    )(me, table, *pieces)


def gram_kernel(parts, inverse, *refs):
    out_ref = refs[-1]
    total = jnp.zeros(out_ref.shape[1:], jnp.float32)
    for ref in refs[:parts]:
        total += lax.dot_general(
            ref[0], ref[1], (((0,), (0,)), ((), ())), preferred_element_type=jnp.float32
        )
    out_ref[0] = total * inverse


def gram_sum(tiles, pairs, inverse):
    _, rows, blk = tiles[0].shape
    return pl.pallas_call(
        functools.partial(gram_kernel, len(tiles), inverse),
        grid=(pairs,),
        out_shape=jax.ShapeDtypeStruct((pairs, blk, blk), jnp.float32),
        in_specs=[pl.BlockSpec((2, rows, blk), lambda p: (p, 0, 0))] * len(tiles),
        out_specs=pl.BlockSpec((1, blk, blk), lambda p: (p, 0, 0)),
        name="gram_sum",
    )(*tiles)


def cross_kernel(parts, inverse, *refs):
    out_ref = refs[-1]
    total = jnp.zeros(out_ref.shape[1:], jnp.float32)
    for left, right in zip(refs[:parts], refs[parts : 2 * parts]):
        total += lax.dot_general(
            left[0], right[0], (((0,), (0,)), ((), ())), preferred_element_type=jnp.float32
        )
    out_ref[0] = total * inverse


def cross_sum(left, right, pairs, inverse):
    _, rows, blk = left[0].shape
    return pl.pallas_call(
        functools.partial(cross_kernel, len(left), inverse),
        grid=(pairs,),
        out_shape=jax.ShapeDtypeStruct((pairs, blk, blk), jnp.float32),
        in_specs=[pl.BlockSpec((1, rows, blk), lambda p: (2 * p, 0, 0))] * len(left)
        + [pl.BlockSpec((1, rows, blk), lambda p: (p, 0, 0))] * len(left),
        out_specs=pl.BlockSpec((1, blk, blk), lambda p: (p, 0, 0)),
        name="cross_sum",
    )(*left, *right)


def body(span_input, span_output, block_pairs):
    tok_count = lax.axis_size("tok")
    feat_count = lax.axis_size("feat")
    tok = lax.axis_index("tok")
    feat = lax.axis_index("feat")
    rows, width = span_input.shape
    inverse = 1.0 / (tok_count * rows)
    pair_dev = block_pairs.shape[0] // (tok_count * feat_count)
    sides = 2 if feat_count % 2 == 0 and rows % 32 == 0 else 1
    line = feat_count // sides
    place, side = feat // sides, feat % sides
    own_blocks = width // BLK
    half = rows // sides

    def blocks_of(array, which):
        part = lax.dynamic_slice_in_dim(array, which * half, half, 0)
        return part.reshape(half, own_blocks, BLK).transpose(1, 0, 2)

    def unit_of(array):
        pieces = [blocks_of(array, side)]
        for d in range(1, sides):
            sent = blocks_of(array, (side + d) % sides)
            perm = [
                (f, f // sides * sides + (f % sides + d) % sides) for f in range(feat_count)
            ]
            pieces.append(lax.ppermute(sent, "feat", perm))
        return jnp.concatenate(pieces, 0) if sides > 1 else pieces[0]

    def gather_line(unit):
        ups, downs = [], []
        up = down = unit
        for k in range(1, line):
            up = lax.ppermute(
                up, "feat",
                [(p * sides + s, (p + 1) * sides + s) for p in range(k - 1, line - 1) for s in range(sides)],
            )
            down = lax.ppermute(
                down, "feat",
                [((p + 1) * sides + s, p * sides + s) for p in range(0, line - k) for s in range(sides)],
            )
            ups.append(up)
            downs.append(down)
        return [unit] + ups + downs

    deltas = [(dt, ds) for dt in range(tok_count) for ds in range(sides)]
    owner = jnp.stack(
        [((tok + dt) % tok_count) * feat_count + place * sides + (side + ds) % sides for dt, ds in deltas]
    )
    listed = jnp.take(
        block_pairs.reshape(tok_count * feat_count, pair_dev, 2), owner, axis=0
    )
    piece = (side - listed // own_blocks % sides) % sides
    slots = listed // (own_blocks * sides) * (own_blocks * sides) + piece * own_blocks + listed % own_blocks
    me = place.reshape(1).astype(jnp.int32)

    def to_owners(tiles):
        got = []
        for (dt, ds), sent in zip(deltas, tiles):
            if dt == 0 and ds == 0:
                got.append(sent)
                continue
            perm = [
                (
                    t * feat_count + f,
                    (t + dt) % tok_count * feat_count + f // sides * sides + (f % sides + ds) % sides,
                )
                for t in range(tok_count)
                for f in range(feat_count)
            ]
            got.append(lax.ppermute(sent, ("tok", "feat"), perm))
        return got

    outs = len(deltas)
    unit_in = unit_of(span_input)
    unit_out = unit_of(span_output)
    line_in = gather_line(unit_in)
    line_out = gather_line(unit_out)
    tiles_in = to_owners(select_tiles(me, slots.reshape(-1), line_in, outs, line))
    tiles_out = to_owners(select_tiles(me, slots[:, :, 1].reshape(-1), line_out, outs, line))
    gram = gram_sum(tiles_in, pair_dev, inverse)
    cross = cross_sum(tiles_in, tiles_out, pair_dev, inverse)
    return gram, cross


def solution(mesh):
    return jax.shard_map(
        body,
        mesh=mesh,
        in_specs=(P("tok", "feat"), P("tok", "feat"), P()),
        out_specs=(P(("tok", "feat"), None, None), P(("tok", "feat"), None, None)),
        check_vma=False,
    )
```

time: 333 us -> 211 us (0.63)
  blocking collectives: 82.2 us -> 0 us
  waiting for transfers between devices: 186 us -> 128 us
  starting transfers between devices: 0.08 us -> 45.6 us
  local copies, waits for them, and re-layouts: 40.4 us -> 9.49 us
  Pallas kernels: 0 us -> 24.1 us
  between operations: 14.2 us -> 1.13 us
  matrix products: 3.47 us -> 0 us
    all_gather x2 -> x0, waiting for transfers between devices: 185 us -> none  [the longest x1 97.8 us: body(): lax.all_gather(span_output, 'feat', axis=1, tiled=True)]
    ppermute x0 -> x28, waiting for transfers between devices: none -> 128 us  [the longest x14 53.3 us: to_owners(): got.append(lax.ppermute(sent, ('tok', 'feat'), perm))]
    all_to_all x1 -> x0, blocking collectives: 82.2 us -> none  [body(): lax.all_to_all(selected, 'tok', split_axis=2, concat_axis=1, tiled=True)]
    ppermute x0 -> x28, starting transfers between devices: none -> 45.6 us  [the longest x14 24.9 us: to_owners(): got.append(lax.ppermute(sent, ('tok', 'feat'), perm))]
    pallas_call x0 -> x4, Pallas kernels: none -> 24.1 us  [the longest x1 8.85 us: gram_sum(): pl.pallas_call(functools.partial(gram_kernel, len(tiles), inverse), grid=...]
    gather x4 -> x1, local copies, waits for them, and re-layouts: 14.7 us -> 0.58 us  [body(): jnp.take(block_pairs.reshape(tok_count * feat_count, pair_dev, 2), owner,...]
    reshape x2 -> x6, local copies, waits for them, and re-layouts: 14.5 us -> 0.41 us  [the longest x4 0.28 us: blocks_of(): return part.reshape(half, own_blocks, BLK).transpose(1, 0, 2)]
    all_to_all x1 -> x0, local copies, waits for them, and re-layouts: 5.11 us -> none  [body(): lax.all_to_all(selected, 'tok', split_axis=2, concat_axis=1, tiled=True)]
  transfers between devices with their start and end apart: 2 -> 28, of which waited for: 2 -> 13; matrix products, arithmetic and copies ran while one was open for 4% -> 1% of each run, Pallas kernels for 0% -> 7%
where the time goes in v1:
time: 211 us; the launch traced here: 209 us
  waiting for transfers between devices  128 us (61%)
  starting transfers between devices  45.6 us (22%)
  Pallas kernels  24.1 us (11%)
  local copies, waits for them, and re-layouts  9.49 us (4%)
    ppermute x14, waiting for transfers between devices, to_owners(): got.append(lax.ppermute(sent, ('tok', 'feat'), perm))  53.3 us
    ppermute x6, waiting for transfers between devices, gather_line(): lax.ppermute(up, 'feat', [(p * sides + s, (p + 1) * sides + s) for p in r...  46.8 us
    ppermute x14, starting transfers between devices, to_owners(): got.append(lax.ppermute(sent, ('tok', 'feat'), perm))  24.9 us
    ppermute x6, waiting for transfers between devices, gather_line(): lax.ppermute(down, 'feat', [((p + 1) * sides + s, p * sides + s) for p in...  15.1 us
    ppermute x2, waiting for transfers between devices, unit_of(): pieces.append(lax.ppermute(sent, 'feat', perm))  13.2 us
    ppermute x6, starting transfers between devices, gather_line(): lax.ppermute(down, 'feat', [((p + 1) * sides + s, p * sides + s) for p in...  11.4 us
    pallas_call x1, Pallas kernels, gram_sum(): pl.pallas_call(functools.partial(gram_kernel, len(tiles), inverse), grid=...  8.85 us
    pallas_call x1, Pallas kernels, cross_sum(): pl.pallas_call(functools.partial(cross_kernel, len(left), inverse), grid=...  8.78 us
  transfers between devices with their start and end apart: 28, of which 13 were waited for; matrix products, arithmetic and copies ran while one was open for 1% of the time, Pallas kernels for 7%

profile of v1, /device:TPU:25, one launch (start us, length us, event | category | flops | bytes accessed | tf_op | source)
XLA Modules:
  0.0 209.1 jit_solution(375680729498365951)
XLA Ops:
  0.7 1.5 dynamic-slice_bitcast_fusion.1
  2.3 1.3 collective-permute-start
  4.0 8.3 %collective-permute-done = bf16[16,96,128]{2,1,0:T(8,128)(2,1)S(1)} collective-permute-done((bf16[16,96,128]{2,1,0:T(8,128)(2,1)S(1)}, bf16[16,96,128]{2,1,0:T(8,128)(2,1)S(1)}, u32[]{:S(2)}, u32[]{:S(2)}) %collective-permute-start) | collective-permute-done | bytes 393248 | tf_op jit(solution)/shard_map/ppermute | solution.py:135
  12.4 2.1 %collective-permute-start.4 = (bf16[32,96,128]{2,1,0:T(8,128)(2,1)S(1)}, bf16[32,96,128]{2,1,0:T(8,128)(2,1)S(1)}, u32[]{:S(2)}, u32[]{:S(2)}) collective-permute-start(bf16[32,96,128]{2,1,0:T(8,128)(2,1)S(1)} %pad_maximum_fusion.refs_0_), channel_id=1, source_target_pairs={{2,0},{3,1},{4,2},{5,3},{6,4},{7,5},{10,8},{11,9},{12,10},{13,11},... | collective-permute-start | bytes 2359304 | tf_op jit(solution)/shard_map/ppermute | solution.py:146
  14.5 1.3 collective-permute-start.1
  15.9 4.8 %collective-permute-done.14 = bf16[16,96,128]{2,1,0:T(8,128)(2,1)S(1)} collective-permute-done((bf16[16,96,128]{2,1,0:T(8,128)(2,1)S(1)}, bf16[16,96,128]{2,1,0:T(8,128)(2,1)S(1)}, u32[]{:S(2)}, u32[]{:S(2)}) %collective-permute-start.14) | collective-permute-done | bytes 393248 | tf_op jit(solution)/shard_map/ppermute | solution.py:135
  20.8 3.0 %collective-permute-start.18 = (bf16[32,96,128]{2,1,0:T(8,128)(2,1)S(1)}, bf16[32,96,128]{2,1,0:T(8,128)(2,1)}, u32[]{:S(2)}, u32[]{:S(2)}) collective-permute-start(bf16[32,96,128]{2,1,0:T(8,128)(2,1)S(1)} %pad_maximum_fusion.1.refs_0_), channel_id=1, source_target_pairs={{2,0},{3,1},{4,2},{5,3},{6,4},{7,5},{10,8},{11,9},{12,10},{13,11},... | collective-permute-start | bytes 2359304 | tf_op jit(solution)/shard_map/ppermute | solution.py:146
  23.8 1.3 collective-permute-start.15
  25.1 3.5 %collective-permute-done.4.refs_4_ = bf16[32,96,128]{2,1,0:T(8,128)(2,1)S(1)} collective-permute-done((bf16[32,96,128]{2,1,0:T(8,128)(2,1)S(1)}, bf16[32,96,128]{2,1,0:T(8,128)(2,1)S(1)}, u32[]{:S(2)}, u32[]{:S(2)}) %collective-permute-start.4) | collective-permute-done | bytes 786464 | tf_op jit(solution)/shard_map/ppermute | solution.py:146
  28.6 1.6 collective-permute-start.5
  30.1 2.3 %collective-permute-done.1.refs_1_ = bf16[32,96,128]{2,1,0:T(8,128)(2,1)S(1)} collective-permute-done((bf16[32,96,128]{2,1,0:T(8,128)(2,1)S(1)}, bf16[32,96,128]{2,1,0:T(8,128)(2,1)S(1)}, u32[]{:S(2)}, u32[]{:S(2)}) %collective-permute-start.1) | collective-permute-done | bytes 786464 | tf_op jit(solution)/shard_map/ppermute | solution.py:142
  32.5 1.3 collective-permute-start.2
  33.8 11.6 %collective-permute-done.18.refs_4_ = bf16[32,96,128]{2,1,0:T(8,128)(2,1)} collective-permute-done((bf16[32,96,128]{2,1,0:T(8,128)(2,1)S(1)}, bf16[32,96,128]{2,1,0:T(8,128)(2,1)}, u32[]{:S(2)}, u32[]{:S(2)}) %collective-permute-start.18) | collective-permute-done | bytes 786464 | tf_op jit(solution)/shard_map/ppermute | solution.py:146
  45.4 1.6 collective-permute-start.19
  47.0 2.4 %collective-permute-done.15.refs_1_ = bf16[32,96,128]{2,1,0:T(8,128)(2,1)} collective-permute-done((bf16[32,96,128]{2,1,0:T(8,128)(2,1)S(1)}, bf16[32,96,128]{2,1,0:T(8,128)(2,1)}, u32[]{:S(2)}, u32[]{:S(2)}) %collective-permute-start.15) | collective-permute-done | bytes 786464 | tf_op jit(solution)/shard_map/ppermute | solution.py:142
  49.4 1.3 collective-permute-start.16
  51.1 1.6 collective-permute-start.6
  52.7 13.6 %collective-permute-done.2.refs_2_ = bf16[32,96,128]{2,1,0:T(8,128)(2,1)} collective-permute-done((bf16[32,96,128]{2,1,0:T(8,128)(2,1)S(1)}, bf16[32,96,128]{2,1,0:T(8,128)(2,1)}, u32[]{:S(2)}, u32[]{:S(2)}) %collective-permute-start.2) | collective-permute-done | bytes 786464 | tf_op jit(solution)/shard_map/ppermute | solution.py:142
  66.3 1.3 collective-permute-start.3
  68.5 1.6 collective-permute-start.20
  70.1 13.0 %collective-permute-done.16.refs_2_ = bf16[32,96,128]{2,1,0:T(8,128)(2,1)} collective-permute-done((bf16[32,96,128]{2,1,0:T(8,128)(2,1)}, bf16[32,96,128]{2,1,0:T(8,128)(2,1)}, u32[]{:S(2)}, u32[]{:S(2)}) %collective-permute-start.16) | collective-permute-done | bytes 786464 | tf_op jit(solution)/shard_map/ppermute | solution.py:142
  83.1 1.3 collective-permute-start.17
  84.5 15.5 %collective-permute-done.3.refs_3_ = bf16[32,96,128]{2,1,0:T(8,128)(2,1)} collective-permute-done((bf16[32,96,128]{2,1,0:T(8,128)(2,1)}, bf16[32,96,128]{2,1,0:T(8,128)(2,1)}, u32[]{:S(2)}, u32[]{:S(2)}) %collective-permute-start.3) | collective-permute-done | bytes 786464 | tf_op jit(solution)/shard_map/ppermute | solution.py:142
  100.0 3.7 %select_tiles.2 = (bf16[24,96,128]{2,1,0:T(8,128)(2,1)S(1)}, bf16[24,96,128]{2,1,0:T(8,128)(2,1)}, bf16[24,96,128]{2,1,0:T(8,128)(2,1)}, bf16[24,96,128]{2,1,0:T...) custom-call(s32[1]{0:T(128)} %bitcast.line_ref, ...), custom_call_target="tpu_custom_call" | custom-call | tf_op jit(solution)/shard_map/select_tiles/pallas_call | solution.py:50
  103.7 0.8 copy-done
  104.5 0.8 copy-done.2
  105.3 0.9 copy-done.4
  106.2 0.9 copy-done.6
  107.1 0.8 copy-done.8
  107.9 0.8 copy-done.10
  108.7 1.2 collective-permute-start.7
  109.9 8.8 %collective-permute-start.8 = (bf16[24,96,128]{2,1,0:T(8,128)(2,1)}, bf16[24,96,128]{2,1,0:T(8,128)(2,1)}, u32[]{:S(2)}, u32[]{:S(2)}) collective-permute-start(bf16[24,96,128]{2,1,0:T(8,128)(2,1)} %get-tuple-element.20), channel_id=1, source_target_pairs={{0,8},{1,9},{2,10},{3,11},{4,12},{5,13},{6,14},{7,15},{8,16},{9,17... | collective-permute-start | bytes 1769480 | tf_op jit(solution)/shard_map/ppermute | solution.py:179
  118.9 2.8 %select_tiles.3 = (bf16[12,96,128]{2,1,0:T(8,128)(2,1)S(1)}, bf16[12,96,128]{2,1,0:T(8,128)(2,1)S(1)}, bf16[12,96,128]{2,1,0:T(8,128)(2,1)S(1)}, bf16[12,96,128]...) custom-call(s32[1]{0:T(128)} %bitcast.line_ref, ...), custom_call_target="tpu_custom_call" | custom-call | tf_op jit(solution)/shard_map/select_tiles/pallas_call | solution.py:50
  121.7 0.7 copy-done.1
  122.6 4.0 %collective-permute-start.22 = (bf16[12,96,128]{2,1,0:T(8,128)(2,1)S(1)}, bf16[12,96,128]{2,1,0:T(8,128)(2,1)S(1)}, u32[]{:S(2)}, u32[]{:S(2)}) collective-permute-start(bf16[12,96,128]{2,1,0:T(8,128)(2,1)S(1)} %get-tuple-element.28), channel_id=1, source_target_pairs={{0,8},{1,9},{2,10},{3,11},{4,12},{5,13},{6,14},{7,15},{8,16},{9,17... | collective-permute-start | bytes 884744 | tf_op jit(solution)/shard_map/ppermute | solution.py:179
  126.6 4.0 %collective-permute-done.21.refs_9_ = bf16[12,96,128]{2,1,0:T(8,128)(2,1)S(1)} collective-permute-done((bf16[12,96,128]{2,1,0:T(8,128)(2,1)S(1)}, bf16[12,96,128]{2,1,0:T(8,128)(2,1)S(1)}, u32[]{:S(2)}, u32[]{:S(2)}) %collective-permute-start.21) | collective-permute-done | bytes 294944 | tf_op jit(solution)/shard_map/ppermute | solution.py:179
  130.6 1.1 collective-permute-start.10
  131.7 1.3 collective-permute-start.11
  133.0 4.6 %collective-permute-start.12 = (bf16[24,96,128]{2,1,0:T(8,128)(2,1)S(1)}, bf16[24,96,128]{2,1,0:T(8,128)(2,1)S(1)}, u32[]{:S(2)}, u32[]{:S(2)}) collective-permute-start(bf16[24,96,128]{2,1,0:T(8,128)(2,1)S(1)} %copy-done.5), channel_id=1, source_target_pairs={{0,24},{1,25},{2,26},{3,27},{4,28},{5,29},{6,30},{7,31},{8,0},{9,1... | collective-permute-start | bytes 1769480 | tf_op jit(solution)/shard_map/ppermute | solution.py:179
  137.9 8.3 %collective-permute-done.9.refs_3_ = bf16[24,96,128]{2,1,0:T(8,128)(2,1)S(1)} collective-permute-done((bf16[24,96,128]{2,1,0:T(8,128)(2,1)S(1)}, bf16[24,96,128]{2,1,0:T(8,128)(2,1)S(1)}, u32[]{:S(2)}, u32[]{:S(2)}) %collective-permute-start.9) | collective-permute-done | bytes 589856 | tf_op jit(solution)/shard_map/ppermute | solution.py:179
  146.2 0.7 collective-permute-start.23
  146.8 17.2 %collective-permute-done.10.refs_4_ = bf16[24,96,128]{2,1,0:T(8,128)(2,1)S(1)} collective-permute-done((bf16[24,96,128]{2,1,0:T(8,128)(2,1)S(1)}, bf16[24,96,128]{2,1,0:T(8,128)(2,1)S(1)}, u32[]{:S(2)}, u32[]{:S(2)}) %collective-permute-start.10) | collective-permute-done | bytes 589856 | tf_op jit(solution)/shard_map/ppermute | solution.py:179
  164.1 1.1 collective-permute-start.24
  165.2 23.8 %collective-permute-done.12.refs_6_ = bf16[24,96,128]{2,1,0:T(8,128)(2,1)S(1)} collective-permute-done((bf16[24,96,128]{2,1,0:T(8,128)(2,1)S(1)}, bf16[24,96,128]{2,1,0:T(8,128)(2,1)S(1)}, u32[]{:S(2)}, u32[]{:S(2)}) %collective-permute-start.12) | collective-permute-done | bytes 589856 | tf_op jit(solution)/shard_map/ppermute | solution.py:179
  189.0 1.7 collective-permute-start.27
  190.7 8.9 %gram_sum.1 = f32[12,128,128]{2,1,0:T(8,128)} custom-call(bf16[24,96,128]{2,1,0:T(8,128)(2,1)} %copy-done, bf16[24,96,128]{2,1,0:T(8,128)(2,1)} %collective-permute-done.7.refs_1_, bf16[24,96,128]{2,1,0:T(8,128)(2,1)} %collective-permute-done.8.refs_2_, bf16[24,96,128]{2,1,0:T(8,128)(2,1)} %copy-done.12, bf16[24,96,128]{2,1,0:T(8,128)(2,1)} %copy-done.13, ...), custom_call_target="tpu_custom_call" | custom-call | tf_op jit(solution)/shard_map/gram_sum/pallas_call | solution.py:77
  199.6 0.7 copy-done.19
  200.3 8.8 %cross_sum.1 = f32[12,128,128]{2,1,0:T(8,128)} custom-call(bf16[24,96,128]{2,1,0:T(8,128)(2,1)} %copy-done, bf16[24,96,128]{2,1,0:T(8,128)(2,1)} %collective-permute-done.7.refs_1_, bf16[24,96,128]{2,1,0:T(8,128)(2,1)} %collective-permute-done.8.refs_2_, bf16[24,96,128]{2,1,0:T(8,128)(2,1)} %copy-done.12, bf16[24,96,128]{2,1,0:T(8,128)(2,1)} %copy-done.13, ...), custom_call_target="tpu_custom_call" | custom-call | tf_op jit(solution)/shard_map/cross_sum/pallas_call | solution.py:99
  (77 shorter events, 2.9 us)
Async XLA Ops:
  2.3 10.0 %collective-permute-start = (bf16[16,96,128]{2,1,0:T(8,128)(2,1)S(1)}, bf16[16,96,128]{2,1,0:T(8,128)(2,1)S(1)}, u32[]{:S(2)}, u32[]{:S(2)}) collective-permute-start(bf16[16,96,128]{2,1,0:T(8,128)(2,1)S(1)} %bitcast.56), channel_id=1, source_target_pairs={{0,1},{1,0},{2,3},{3,2},{4,5},{5,4},{6,7},{7,6},{8,9},{9,8},{10,11... | collective-permute-start | bytes 1179656 | tf_op jit(solution)/shard_map/ppermute | solution.py:135
  3.6 17.1 %collective-permute-start.14 = (bf16[16,96,128]{2,1,0:T(8,128)(2,1)S(1)}, bf16[16,96,128]{2,1,0:T(8,128)(2,1)S(1)}, u32[]{:S(2)}, u32[]{:S(2)}) collective-permute-start(bf16[16,96,128]{2,1,0:T(8,128)(2,1)S(1)} %bitcast.55), channel_id=1, source_target_pairs={{0,1},{1,0},{2,3},{3,2},{4,5},{5,4},{6,7},{7,6},{8,9},{9,8},{10,11... | collective-permute-start | bytes 1179656 | tf_op jit(solution)/shard_map/ppermute | solution.py:135
  12.4 16.2 %collective-permute-start.4 = (bf16[32,96,128]{2,1,0:T(8,128)(2,1)S(1)}, bf16[32,96,128]{2,1,0:T(8,128)(2,1)S(1)}, u32[]{:S(2)}, u32[]{:S(2)}) collective-permute-start(bf16[32,96,128]{2,1,0:T(8,128)(2,1)S(1)} %pad_maximum_fusion.refs_0_), channel_id=1, source_target_pairs={{2,0},{3,1},{4,2},{5,3},{6,4},{7,5},{10,8},{11,9},{12,10},{13,11},... | collective-permute-start | bytes 2359304 | tf_op jit(solution)/shard_map/ppermute | solution.py:146
  14.5 18.0 %collective-permute-start.1 = (bf16[32,96,128]{2,1,0:T(8,128)(2,1)S(1)}, bf16[32,96,128]{2,1,0:T(8,128)(2,1)S(1)}, u32[]{:S(2)}, u32[]{:S(2)}) collective-permute-start(bf16[32,96,128]{2,1,0:T(8,128)(2,1)S(1)} %pad_maximum_fusion.refs_0_), channel_id=1, source_target_pairs={{0,2},{1,3},{2,4},{3,5},{4,6},{5,7},{8,10},{9,11},{10,12},{11,13},... | collective-permute-start | bytes 2359304 | tf_op jit(solution)/shard_map/ppermute | solution.py:142
  20.8 24.6 %collective-permute-start.18 = (bf16[32,96,128]{2,1,0:T(8,128)(2,1)S(1)}, bf16[32,96,128]{2,1,0:T(8,128)(2,1)}, u32[]{:S(2)}, u32[]{:S(2)}) collective-permute-start(bf16[32,96,128]{2,1,0:T(8,128)(2,1)S(1)} %pad_maximum_fusion.1.refs_0_), channel_id=1, source_target_pairs={{2,0},{3,1},{4,2},{5,3},{6,4},{7,5},{10,8},{11,9},{12,10},{13,11},... | collective-permute-start | bytes 2359304 | tf_op jit(solution)/shard_map/ppermute | solution.py:146
  23.8 25.6 %collective-permute-start.15 = (bf16[32,96,128]{2,1,0:T(8,128)(2,1)S(1)}, bf16[32,96,128]{2,1,0:T(8,128)(2,1)}, u32[]{:S(2)}, u32[]{:S(2)}) collective-permute-start(bf16[32,96,128]{2,1,0:T(8,128)(2,1)S(1)} %pad_maximum_fusion.1.refs_0_), channel_id=1, source_target_pairs={{0,2},{1,3},{2,4},{3,5},{4,6},{5,7},{8,10},{9,11},{10,12},{11,13},... | collective-permute-start | bytes 2359304 | tf_op jit(solution)/shard_map/ppermute | solution.py:142
  28.6 22.5 %collective-permute-start.5 = (bf16[32,96,128]{2,1,0:T(8,128)(2,1)S(1)}, bf16[32,96,128]{2,1,0:T(8,128)(2,1)}, u32[]{:S(2)}, u32[]{:S(2)}) collective-permute-start(bf16[32,96,128]{2,1,0:T(8,128)(2,1)S(1)} %collective-permute-done.4.refs_4_), channel_id=1, source_target_pairs={{2,0},{3,1},{4,2},{5,3},{10,8},{11,9},{12,10},{13,11},{18,16},{19,... | collective-permute-start | bytes 2359304 | tf_op jit(solution)/shard_map/ppermute | solution.py:146
  32.5 33.8 %collective-permute-start.2 = (bf16[32,96,128]{2,1,0:T(8,128)(2,1)S(1)}, bf16[32,96,128]{2,1,0:T(8,128)(2,1)}, u32[]{:S(2)}, u32[]{:S(2)}) collective-permute-start(bf16[32,96,128]{2,1,0:T(8,128)(2,1)S(1)} %collective-permute-done.1.refs_1_), channel_id=1, source_target_pairs={{2,4},{3,5},{4,6},{5,7},{10,12},{11,13},{12,14},{13,15},{18,20},{1... | collective-permute-start | bytes 2359304 | tf_op jit(solution)/shard_map/ppermute | solution.py:142
  33.8 16.9 %copy-start.20 = (s32[384,2]{0,1:T(2,128)S(1)}, s32[384,2]{0,1:T(2,128)}, u32[]{:S(2)}) copy-start(s32[384,2]{0,1:T(2,128)} %param.5) | copy-start | bytes 9220
  45.4 23.1 %collective-permute-start.19 = (bf16[32,96,128]{2,1,0:T(8,128)(2,1)}, bf16[32,96,128]{2,1,0:T(8,128)(2,1)}, u32[]{:S(2)}, u32[]{:S(2)}) collective-permute-start(bf16[32,96,128]{2,1,0:T(8,128)(2,1)} %collective-permute-done.18.refs_4_), channel_id=1, source_target_pairs={{2,0},{3,1},{4,2},{5,3},{10,8},{11,9},{12,10},{13,11},{18,16},{19,... | collective-permute-start | bytes 2359304 | tf_op jit(solution)/shard_map/ppermute | solution.py:146
  49.4 33.7 %collective-permute-start.16 = (bf16[32,96,128]{2,1,0:T(8,128)(2,1)}, bf16[32,96,128]{2,1,0:T(8,128)(2,1)}, u32[]{:S(2)}, u32[]{:S(2)}) collective-permute-start(bf16[32,96,128]{2,1,0:T(8,128)(2,1)} %collective-permute-done.15.refs_1_), channel_id=1, source_target_pairs={{2,4},{3,5},{4,6},{5,7},{10,12},{11,13},{12,14},{13,15},{18,20},{1... | collective-permute-start | bytes 2359304 | tf_op jit(solution)/shard_map/ppermute | solution.py:142
  51.1 33.4 %collective-permute-start.6 = (bf16[32,96,128]{2,1,0:T(8,128)(2,1)}, bf16[32,96,128]{2,1,0:T(8,128)(2,1)}, u32[]{:S(2)}, u32[]{:S(2)}) collective-permute-start(bf16[32,96,128]{2,1,0:T(8,128)(2,1)} %collective-permute-done.5.refs_5_), channel_id=1, source_target_pairs={{2,0},{3,1},{10,8},{11,9},{18,16},{19,17},{26,24},{27,25}} | collective-permute-start | bytes 2359304 | tf_op jit(solution)/shard_map/ppermute | solution.py:146
  66.3 33.7 %collective-permute-start.3 = (bf16[32,96,128]{2,1,0:T(8,128)(2,1)}, bf16[32,96,128]{2,1,0:T(8,128)(2,1)}, u32[]{:S(2)}, u32[]{:S(2)}) collective-permute-start(bf16[32,96,128]{2,1,0:T(8,128)(2,1)} %collective-permute-done.2.refs_2_), channel_id=1, source_target_pairs={{4,6},{5,7},{12,14},{13,15},{20,22},{21,23},{28,30},{29,31}} | collective-permute-start | bytes 2359304 | tf_op jit(solution)/shard_map/ppermute | solution.py:142
  68.5 50.4 %collective-permute-start.20 = (bf16[32,96,128]{2,1,0:T(8,128)(2,1)}, bf16[32,96,128]{2,1,0:T(8,128)(2,1)}, u32[]{:S(2)}, u32[]{:S(2)}) collective-permute-start(bf16[32,96,128]{2,1,0:T(8,128)(2,1)} %collective-permute-done.19.refs_5_), channel_id=1, source_target_pairs={{2,0},{3,1},{10,8},{11,9},{18,16},{19,17},{26,24},{27,25}} | collective-permute-start | bytes 2359304 | tf_op jit(solution)/shard_map/ppermute | solution.py:146
  83.1 35.8 %collective-permute-start.17 = (bf16[32,96,128]{2,1,0:T(8,128)(2,1)}, bf16[32,96,128]{2,1,0:T(8,128)(2,1)}, u32[]{:S(2)}, u32[]{:S(2)}) collective-permute-start(bf16[32,96,128]{2,1,0:T(8,128)(2,1)} %collective-permute-done.16.refs_2_), channel_id=1, source_target_pairs={{4,6},{5,7},{12,14},{13,15},{20,22},{21,23},{28,30},{29,31}} | collective-permute-start | bytes 2359304 | tf_op jit(solution)/shard_map/ppermute | solution.py:142
  103.7 0.8 copy-start
  104.5 0.8 copy-start.2
  105.3 0.9 copy-start.4
  106.2 0.9 copy-start.6
  107.1 0.8 copy-start.8
  107.9 0.8 copy-start.10
  108.7 24.3 %collective-permute-start.7 = (bf16[24,96,128]{2,1,0:T(8,128)(2,1)}, bf16[24,96,128]{2,1,0:T(8,128)(2,1)}, u32[]{:S(2)}, u32[]{:S(2)}) collective-permute-start(bf16[24,96,128]{2,1,0:T(8,128)(2,1)} %get-tuple-element.19), channel_id=1, source_target_pairs={{0,1},{1,0},{2,3},{3,2},{4,5},{5,4},{6,7},{7,6},{8,9},{9,8},{10,11... | collective-permute-start | bytes 1769480 | tf_op jit(solution)/shard_map/ppermute | solution.py:179
  109.9 27.7 %collective-permute-start.8 = (bf16[24,96,128]{2,1,0:T(8,128)(2,1)}, bf16[24,96,128]{2,1,0:T(8,128)(2,1)}, u32[]{:S(2)}, u32[]{:S(2)}) collective-permute-start(bf16[24,96,128]{2,1,0:T(8,128)(2,1)} %get-tuple-element.20), channel_id=1, source_target_pairs={{0,8},{1,9},{2,10},{3,11},{4,12},{5,13},{6,14},{7,15},{8,16},{9,17... | collective-permute-start | bytes 1769480 | tf_op jit(solution)/shard_map/ppermute | solution.py:179
  118.8 7.8 %copy-start.11 = (bf16[24,96,128]{2,1,0:T(8,128)(2,1)S(1)}, bf16[24,96,128]{2,1,0:T(8,128)(2,1)}, u32[]{:S(2)}) copy-start(bf16[24,96,128]{2,1,0:T(8,128)(2,1)} %copy-done.10) | copy-start | bytes 1769476
  118.8 11.8 %copy-start.9 = (bf16[24,96,128]{2,1,0:T(8,128)(2,1)S(1)}, bf16[24,96,128]{2,1,0:T(8,128)(2,1)}, u32[]{:S(2)}) copy-start(bf16[24,96,128]{2,1,0:T(8,128)(2,1)} %copy-done.8) | copy-start | bytes 1769476
  118.8 12.9 %copy-start.7 = (bf16[24,96,128]{2,1,0:T(8,128)(2,1)S(1)}, bf16[24,96,128]{2,1,0:T(8,128)(2,1)}, u32[]{:S(2)}) copy-start(bf16[24,96,128]{2,1,0:T(8,128)(2,1)} %copy-done.6) | copy-start | bytes 1769476
  118.9 14.1 %copy-start.5 = (bf16[24,96,128]{2,1,0:T(8,128)(2,1)S(1)}, bf16[24,96,128]{2,1,0:T(8,128)(2,1)}, u32[]{:S(2)}) copy-start(bf16[24,96,128]{2,1,0:T(8,128)(2,1)} %copy-done.4) | copy-start | bytes 1769476
  118.9 18.7 %copy-start.3 = (bf16[24,96,128]{2,1,0:T(8,128)(2,1)S(1)}, bf16[24,96,128]{2,1,0:T(8,128)(2,1)}, u32[]{:S(2)}) copy-start(bf16[24,96,128]{2,1,0:T(8,128)(2,1)} %copy-done.2) | copy-start | bytes 1769476
  122.4 8.2 %collective-permute-start.21 = (bf16[12,96,128]{2,1,0:T(8,128)(2,1)S(1)}, bf16[12,96,128]{2,1,0:T(8,128)(2,1)S(1)}, u32[]{:S(2)}, u32[]{:S(2)}) collective-permute-start(bf16[12,96,128]{2,1,0:T(8,128)(2,1)S(1)} %get-tuple-element.27), channel_id=1, source_target_pairs={{0,1},{1,0},{2,3},{3,2},{4,5},{5,4},{6,7},{7,6},{8,9},{9,8},{10,11... | collective-permute-start | bytes 884744 | tf_op jit(solution)/shard_map/ppermute | solution.py:179
  122.6 9.1 %collective-permute-start.22 = (bf16[12,96,128]{2,1,0:T(8,128)(2,1)S(1)}, bf16[12,96,128]{2,1,0:T(8,128)(2,1)S(1)}, u32[]{:S(2)}, u32[]{:S(2)}) collective-permute-start(bf16[12,96,128]{2,1,0:T(8,128)(2,1)S(1)} %get-tuple-element.28), channel_id=1, source_target_pairs={{0,8},{1,9},{2,10},{3,11},{4,12},{5,13},{6,14},{7,15},{8,16},{9,17... | collective-permute-start | bytes 884744 | tf_op jit(solution)/shard_map/ppermute | solution.py:179
  126.6 19.6 %collective-permute-start.9 = (bf16[24,96,128]{2,1,0:T(8,128)(2,1)S(1)}, bf16[24,96,128]{2,1,0:T(8,128)(2,1)S(1)}, u32[]{:S(2)}, u32[]{:S(2)}) collective-permute-start(bf16[24,96,128]{2,1,0:T(8,128)(2,1)S(1)} %copy-done.11), channel_id=1, source_target_pairs={{0,9},{1,8},{2,11},{3,10},{4,13},{5,12},{6,15},{7,14},{8,17},{9,16... | collective-permute-start | bytes 1769480 | tf_op jit(solution)/shard_map/ppermute | solution.py:179
  130.6 68.9 %copy-start.17 = (bf16[12,96,128]{2,1,0:T(8,128)(2,1)}, bf16[12,96,128]{2,1,0:T(8,128)(2,1)S(1)}, u32[]{:S(2)}) copy-start(bf16[12,96,128]{2,1,0:T(8,128)(2,1)S(1)} %collective-permute-done.21.refs_9_) | copy-start | bytes 884740
  130.6 33.4 %collective-permute-start.10 = (bf16[24,96,128]{2,1,0:T(8,128)(2,1)S(1)}, bf16[24,96,128]{2,1,0:T(8,128)(2,1)S(1)}, u32[]{:S(2)}, u32[]{:S(2)}) collective-permute-start(bf16[24,96,128]{2,1,0:T(8,128)(2,1)S(1)} %copy-done.9), channel_id=1, source_target_pairs={{0,16},{1,17},{2,18},{3,19},{4,20},{5,21},{6,22},{7,23},{8,24},{9,... | collective-permute-start | bytes 1769480 | tf_op jit(solution)/shard_map/ppermute | solution.py:179
  131.7 67.8 %copy-start.18 = (bf16[12,96,128]{2,1,0:T(8,128)(2,1)}, bf16[12,96,128]{2,1,0:T(8,128)(2,1)S(1)}, u32[]{:S(2)}) copy-start(bf16[12,96,128]{2,1,0:T(8,128)(2,1)S(1)} %collective-permute-done.22.refs_10_) | copy-start | bytes 884740
  131.7 33.4 %collective-permute-start.11 = (bf16[24,96,128]{2,1,0:T(8,128)(2,1)S(1)}, bf16[24,96,128]{2,1,0:T(8,128)(2,1)S(1)}, u32[]{:S(2)}, u32[]{:S(2)}) collective-permute-start(bf16[24,96,128]{2,1,0:T(8,128)(2,1)S(1)} %copy-done.7), channel_id=1, source_target_pairs={{0,17},{1,16},{2,19},{3,18},{4,21},{5,20},{6,23},{7,22},{8,25},{9,... | collective-permute-start | bytes 1769480 | tf_op jit(solution)/shard_map/ppermute | solution.py:179
  133.0 56.0 %collective-permute-start.12 = (bf16[24,96,128]{2,1,0:T(8,128)(2,1)S(1)}, bf16[24,96,128]{2,1,0:T(8,128)(2,1)S(1)}, u32[]{:S(2)}, u32[]{:S(2)}) collective-permute-start(bf16[24,96,128]{2,1,0:T(8,128)(2,1)S(1)} %copy-done.5), channel_id=1, source_target_pairs={{0,24},{1,25},{2,26},{3,27},{4,28},{5,29},{6,30},{7,31},{8,0},{9,1... | collective-permute-start | bytes 1769480 | tf_op jit(solution)/shard_map/ppermute | solution.py:179
  137.6 51.4 %collective-permute-start.13 = (bf16[24,96,128]{2,1,0:T(8,128)(2,1)S(1)}, bf16[24,96,128]{2,1,0:T(8,128)(2,1)S(1)}, u32[]{:S(2)}, u32[]{:S(2)}) collective-permute-start(bf16[24,96,128]{2,1,0:T(8,128)(2,1)S(1)} %copy-done.3), channel_id=1, source_target_pairs={{0,25},{1,24},{2,27},{3,26},{4,29},{5,28},{6,31},{7,30},{8,1},{9,0... | collective-permute-start | bytes 1769480 | tf_op jit(solution)/shard_map/ppermute | solution.py:179
  146.2 44.5 %copy-start.12 = (bf16[24,96,128]{2,1,0:T(8,128)(2,1)}, bf16[24,96,128]{2,1,0:T(8,128)(2,1)S(1)}, u32[]{:S(2)}) copy-start(bf16[24,96,128]{2,1,0:T(8,128)(2,1)S(1)} %collective-permute-done.9.refs_3_) | copy-start | bytes 1769476
  146.2 53.4 %collective-permute-start.23 = (bf16[12,96,128]{2,1,0:T(8,128)(2,1)S(1)}, bf16[12,96,128]{2,1,0:T(8,128)(2,1)}, u32[]{:S(2)}, u32[]{:S(2)}) collective-permute-start(bf16[12,96,128]{2,1,0:T(8,128)(2,1)S(1)} %get-tuple-element.29), channel_id=1, source_target_pairs={{0,9},{1,8},{2,11},{3,10},{4,13},{5,12},{6,15},{7,14},{8,17},{9,16... | collective-permute-start | bytes 884744 | tf_op jit(solution)/shard_map/ppermute | solution.py:179
  164.1 26.6 %copy-start.13 = (bf16[24,96,128]{2,1,0:T(8,128)(2,1)}, bf16[24,96,128]{2,1,0:T(8,128)(2,1)S(1)}, u32[]{:S(2)}) copy-start(bf16[24,96,128]{2,1,0:T(8,128)(2,1)S(1)} %collective-permute-done.10.refs_4_) | copy-start | bytes 1769476
  164.1 35.5 %collective-permute-start.24 = (bf16[12,96,128]{2,1,0:T(8,128)(2,1)S(1)}, bf16[12,96,128]{2,1,0:T(8,128)(2,1)}, u32[]{:S(2)}, u32[]{:S(2)}) collective-permute-start(bf16[12,96,128]{2,1,0:T(8,128)(2,1)S(1)} %get-tuple-element.30), channel_id=1, source_target_pairs={{0,16},{1,17},{2,18},{3,19},{4,20},{5,21},{6,22},{7,23},{8,24},{9,... | collective-permute-start | bytes 884744 | tf_op jit(solution)/shard_map/ppermute | solution.py:179
  165.2 25.5 %copy-start.14 = (bf16[24,96,128]{2,1,0:T(8,128)(2,1)}, bf16[24,96,128]{2,1,0:T(8,128)(2,1)S(1)}, u32[]{:S(2)}) copy-start(bf16[24,96,128]{2,1,0:T(8,128)(2,1)S(1)} %collective-permute-done.11.refs_5_) | copy-start | bytes 1769476
  165.2 34.4 %collective-permute-start.25 = (bf16[12,96,128]{2,1,0:T(8,128)(2,1)S(1)}, bf16[12,96,128]{2,1,0:T(8,128)(2,1)}, u32[]{:S(2)}, u32[]{:S(2)}) collective-permute-start(bf16[12,96,128]{2,1,0:T(8,128)(2,1)S(1)} %get-tuple-element.31), channel_id=1, source_target_pairs={{0,17},{1,16},{2,19},{3,18},{4,21},{5,20},{6,23},{7,22},{8,25},{9,... | collective-permute-start | bytes 884744 | tf_op jit(solution)/shard_map/ppermute | solution.py:179
  189.0 1.7 copy-start.15
  189.0 10.6 %collective-permute-start.26 = (bf16[12,96,128]{2,1,0:T(8,128)(2,1)S(1)}, bf16[12,96,128]{2,1,0:T(8,128)(2,1)}, u32[]{:S(2)}, u32[]{:S(2)}) collective-permute-start(bf16[12,96,128]{2,1,0:T(8,128)(2,1)S(1)} %get-tuple-element.32), channel_id=1, source_target_pairs={{0,24},{1,25},{2,26},{3,27},{4,28},{5,29},{6,30},{7,31},{8,0},{9,1... | collective-permute-start | bytes 884744 | tf_op jit(solution)/shard_map/ppermute | solution.py:179
  189.0 1.7 copy-start.16
  189.0 10.6 %collective-permute-start.27 = (bf16[12,96,128]{2,1,0:T(8,128)(2,1)S(1)}, bf16[12,96,128]{2,1,0:T(8,128)(2,1)S(1)}, u32[]{:S(2)}, u32[]{:S(2)}) collective-permute-start(bf16[12,96,128]{2,1,0:T(8,128)(2,1)S(1)} %get-tuple-element.33), channel_id=1, source_target_pairs={{0,25},{1,24},{2,27},{3,26},{4,29},{5,28},{6,31},{7,30},{8,1},{9,0... | collective-permute-start | bytes 884744 | tf_op jit(solution)/shard_map/ppermute | solution.py:179
  199.6 0.7 copy-start.19
  (1 other events, 0.7 us)

commit v2 on v0

v2 whole, which is shorter than its diff:
```python
import functools

import jax
import jax.numpy as jnp
from jax import lax
from jax.experimental import pallas as pl
from jax.experimental.pallas import tpu as pltpu
from jax.sharding import PartitionSpec as P

BLK = 128
VMEM_LIMIT = 56 << 20


def select_kernel(offsets, outs, places_ref, table_ref, *refs):
    line = len(offsets)
    pieces, out_refs = refs[:line], refs[line : line + outs]
    held, sems = refs[line + outs :]
    per, rows = held.shape[0] // line, held.shape[1]
    copies = [
        pltpu.make_async_copy(
            piece.at[:, pl.ds(offset, rows), :],
            held.at[pl.ds(places_ref[k] * per, per)],
            sems.at[k],
        )
        for k, (piece, offset) in enumerate(zip(pieces, offsets))
    ]
    for copy in copies:
        copy.start()
    for copy in copies:
        copy.wait()
    for o, out_ref in enumerate(out_refs):
        count = out_ref.shape[0]

        @pl.loop(0, count, unroll=4)
        def _(i, o=o, out_ref=out_ref, count=count):
            out_ref[i] = held[table_ref[o * count + i]]


def select_tiles(places, table, pieces, offsets, rows, outs):
    blocks, _, blk = pieces[0].shape
    dtype = pieces[0].dtype
    return pl.pallas_call(
        functools.partial(select_kernel, offsets, outs),
        out_shape=[jax.ShapeDtypeStruct((table.shape[0] // outs, rows, blk), dtype)] * outs,
        in_specs=[pl.BlockSpec(memory_space=pltpu.SMEM)] * 2
        + [pl.BlockSpec(memory_space=pl.ANY)] * len(pieces),
        out_specs=[pl.BlockSpec(memory_space=pltpu.VMEM)] * outs,
        scratch_shapes=[
            pltpu.VMEM((len(pieces) * blocks, rows, blk), dtype),
            pltpu.SemaphoreType.DMA((len(pieces),)),
        ],
        compiler_params=pltpu.CompilerParams(vmem_limit_bytes=VMEM_LIMIT),
        name="select_tiles",
    )(places, table, *pieces)


def rows_of(refs, parts, group, which, p):
    return jnp.concatenate(
        [ref[k * group + which(p)] for ref, held in zip(refs, parts) for k in held], 0
    )


def gram_kernel(parts, inverse, *refs):
    tiles, out_ref, left_ref = refs[: len(parts)], refs[len(parts)], refs[len(parts) + 1]
    pairs = out_ref.shape[0]

    @pl.loop(0, pairs)
    def _(p):
        left = rows_of(tiles, parts, 2 * pairs, lambda p: 2 * p, p).T
        right = rows_of(tiles, parts, 2 * pairs, lambda p: 2 * p + 1, p)
        left_ref[p] = left
        out_ref[p] = jnp.dot(left, right, preferred_element_type=jnp.float32) * inverse


def cross_kernel(parts, inverse, left_ref, *refs):
    tiles, out_ref = refs[: len(parts)], refs[len(parts)]
    pairs = out_ref.shape[0]

    @pl.loop(0, pairs)
    def _(p):
        right = rows_of(tiles, parts, pairs, lambda p: p, p)
        out_ref[p] = jnp.dot(left_ref[p], right, preferred_element_type=jnp.float32) * inverse


def sum_call(kernel, operands, outs, name):
    return pl.pallas_call(
        kernel,
        out_shape=outs,
        in_specs=[pl.BlockSpec(memory_space=pltpu.VMEM)] * len(operands),
        out_specs=[pl.BlockSpec(memory_space=pltpu.VMEM)] * len(outs),
        compiler_params=pltpu.CompilerParams(vmem_limit_bytes=VMEM_LIMIT),
        name=name,
    )(*operands)


def after(values, done):
    return lax.optimization_barrier((values, done))


def body(span_input, span_output, block_pairs):
    tok_count = lax.axis_size("tok")
    feat_count = lax.axis_size("feat")
    tok = lax.axis_index("tok")
    feat = lax.axis_index("feat")
    rows, width = span_input.shape
    inverse = 1.0 / (tok_count * rows)
    pairs = block_pairs.shape[0] // (tok_count * feat_count)
    own_blocks = width // BLK
    sides = 2 if feat_count % 2 == 0 and rows % 64 == 0 else 1
    line = feat_count // sides
    place, side = feat // sides, feat % sides
    chunks = 2 if rows % (32 * sides) == 0 else 1
    half = rows // sides
    chunk = half // chunks
    paired = line & (line - 1) == 0

    def blocks_of(array, which, start, count):
        part = lax.dynamic_slice_in_dim(array, which * half + start, count, 0)
        return part.reshape(count, own_blocks, BLK).transpose(1, 0, 2)

    def from_sides(array, start, count):
        return [
            lax.ppermute(
                blocks_of(array, (side + d) % sides, start, count), "feat",
                [(f, f // sides * sides + (f % sides + d) % sides) for f in range(feat_count)],
            )
            for d in range(1, sides)
        ]

    def at_place(p, k):
        return p ^ k if paired else (p + k) % line

    def hop(piece, k):
        return lax.ppermute(piece, "feat", [
            (f, at_place(f // sides, k) * sides + f % sides) for f in range(feat_count)
        ])

    def far_hops(unit):
        held = {0: unit}
        if not paired:
            held.update({k: hop(unit, k) for k in range(1, line)})
            return held
        k = line // 2
        while k > 1:
            held.update({m ^ k: hop(piece, k) for m, piece in list(held.items())})
            k //= 2
        if line > 1:
            held[1] = hop(unit, 1)
        return held

    def last_hops(held):
        return {m ^ 1: hop(held[m], 1) for m in held if m > 1 and m ^ 1 not in held}

    places = jnp.stack([at_place(place, k) if paired else (place - k) % line for k in range(line)])
    places = places.astype(jnp.int32)

    cores = 2 if tok_count % 2 == 0 else 1
    chips = [(dt, ds) for dt in range(0, tok_count, cores) for ds in range(sides)]

    def other(t, c):
        return t + c * (1 - 2 * (t % 2))

    owner = jnp.stack([
        other((tok + dt) % tok_count, c) * feat_count + place * sides + (side + ds) % sides
        for dt, ds in chips
        for c in range(cores)
    ])
    listed = jnp.take(block_pairs.reshape(tok_count * feat_count, pairs, 2), owner, axis=0)
    stream = (side - listed // own_blocks % sides) % sides
    slots = listed // (own_blocks * sides) * (own_blocks * sides) + stream * own_blocks + listed % own_blocks

    def send(tiles, chip, c):
        dt, ds = chip
        return lax.ppermute(tiles, ("tok", "feat"), [
            (
                t * feat_count + f,
                other((t + dt) % tok_count, c) * feat_count + f // sides * sides + (f % sides + ds) % sides,
            )
            for t in range(tok_count)
            for f in range(feat_count)
        ])

    def to_owners(tiles):
        got = [tiles[0]] + [send(sent, chip, 0) for sent, chip in zip(tiles[1:], chips[1:])]
        if cores > 1:
            own = tiles[0].shape[0] // cores
            got.append(send(jnp.concatenate([g[own:] for g in got], 0), (0, 0), 1))
        return got

    parts = [(0,)] * len(chips) + [tuple(range(len(chips)))] * (cores > 1)

    brought = [from_sides(span_input, i * chunk, chunk) for i in range(chunks)]
    others_out = from_sides(span_output, 0, half)
    own_out = blocks_of(span_output, side, 0, half)
    tiles_in = []
    held = None
    for i in range(chunks):
        unit = jnp.concatenate([blocks_of(span_input, side, i * chunk, chunk)] + brought[i], 0)
        if held:
            unit, held = after(unit, held)
        ahead = held
        held = far_hops(unit)
        if ahead:
            whole = {**ahead, **last_hops(ahead)}
            picked = select_tiles(
                places, slots.reshape(-1), [whole[k] for k in range(line)], (0,) * line, chunk, len(chips)
            )
            tiles_in += to_owners(picked)
    own_out, held = after(own_out, held)
    whole = {**held, **last_hops(held)}
    picked = select_tiles(
        places, slots.reshape(-1), [whole[k] for k in range(line)], (0,) * line, chunk, len(chips)
    )
    tiles_in += to_owners(picked)

    held = far_hops(jnp.concatenate([own_out] + others_out, 0))
    tiles_out = []
    for i in range(chunks):
        last = last_hops({k: h[:, i * chunk : (i + 1) * chunk] for k, h in held.items()})
        pieces = [last[k] if k in last else held[k] for k in range(line)]
        offsets = tuple(0 if k in last else i * chunk for k in range(line))
        picked = select_tiles(places, slots[:, :, 1].reshape(-1), pieces, offsets, chunk, len(chips))
        tiles_out += to_owners(picked)

    gram_shape = jax.ShapeDtypeStruct((pairs, BLK, BLK), jnp.float32)
    gram, left = sum_call(
        functools.partial(gram_kernel, parts * chunks, inverse), tiles_in,
        [gram_shape, jax.ShapeDtypeStruct((pairs, BLK, tok_count * rows), span_input.dtype)],
        "gram_sum",
    )
    (cross,) = sum_call(
        functools.partial(cross_kernel, parts * chunks, inverse), [left] + tiles_out,
        [gram_shape], "cross_sum",
    )
    return gram, cross


def solution(mesh):
    return jax.shard_map(
        body,
        mesh=mesh,
        in_specs=(P("tok", "feat"), P("tok", "feat"), P()),
        out_specs=(P(("tok", "feat"), None, None), P(("tok", "feat"), None, None)),
        check_vma=False,
    )
```

time: 333 us -> 182 us (0.55)
  waiting for transfers between devices: 186 us -> 99.5 us
  blocking collectives: 82.2 us -> 0 us
  starting transfers between devices: 0.08 us -> 31.5 us
  Pallas kernels: 0 us -> 28.1 us
  local copies, waits for them, and re-layouts: 40.4 us -> 16.6 us
  between operations: 14.2 us -> 1.3 us
  matrix products: 3.47 us -> 0 us
    all_gather x2 -> x0, waiting for transfers between devices: 185 us -> none  [the longest x1 97.8 us: body(): lax.all_gather(span_output, 'feat', axis=1, tiled=True)]
    ppermute x0 -> x29, waiting for transfers between devices: none -> 99.5 us  [the longest x10 67.1 us: hop(): lax.ppermute(piece, 'feat', [(f, at_place(f // sides, k) * sides + f % si...]
    all_to_all x1 -> x0, blocking collectives: 82.2 us -> none  [body(): lax.all_to_all(selected, 'tok', split_axis=2, concat_axis=1, tiled=True)]
    ppermute x0 -> x29, starting transfers between devices: none -> 31.5 us  [the longest x16 23.5 us: send(): lax.ppermute(tiles, ('tok', 'feat'), [(t * feat_count + f, other((t + dt)...]
    pallas_call x0 -> x6, Pallas kernels: none -> 28.1 us  [the longest x4 14.5 us: select_tiles(): pl.pallas_call(functools.partial(select_kernel, offsets, outs), out_shape...]
    gather x4 -> x1, local copies, waits for them, and re-layouts: 14.7 us -> 0.58 us  [body(): jnp.take(block_pairs.reshape(tok_count * feat_count, pairs, 2), owner, ax...]
    reshape x2 -> x8, local copies, waits for them, and re-layouts: 14.5 us -> 0.41 us  [the longest x6 0.28 us: blocks_of(): return part.reshape(count, own_blocks, BLK).transpose(1, 0, 2)]
    unnamed x5 -> x61, local copies, waits for them, and re-layouts: 2.88 us -> 8.5 us
  transfers between devices with their start and end apart: 2 -> 29, of which waited for: 2 -> 11; matrix products, arithmetic and copies ran while one was open for 4% -> 6% of each run, Pallas kernels for 0% -> 12%
where the time goes in v2:
time: 182 us; the launch traced here: 180 us
  waiting for transfers between devices  99.5 us (55%)
  starting transfers between devices  31.5 us (17%)
  Pallas kernels  28.1 us (15%)
  local copies, waits for them, and re-layouts  16.6 us (9%)
  other arithmetic  2.83 us (2%)
    ppermute x10, waiting for transfers between devices, hop(): lax.ppermute(piece, 'feat', [(f, at_place(f // sides, k) * sides + f % si...  67.1 us
    ppermute x16, waiting for transfers between devices, send(): lax.ppermute(tiles, ('tok', 'feat'), [(t * feat_count + f, other((t + dt)...  25.5 us
    ppermute x16, starting transfers between devices, send(): lax.ppermute(tiles, ('tok', 'feat'), [(t * feat_count + f, other((t + dt)...  23.5 us
    pallas_call x4, Pallas kernels, select_tiles(): pl.pallas_call(functools.partial(select_kernel, offsets, outs), out_shape...  14.5 us
    pallas_call x2, Pallas kernels, sum_call(): pl.pallas_call(kernel, out_shape=outs, in_specs=[pl.BlockSpec(memory_spac...  13.6 us
    unnamed x61, local copies, waits for them, and re-layouts  8.5 us
    ppermute x3, waiting for transfers between devices, from_sides(): lax.ppermute(blocks_of(array, (side + d) % sides, start, count), 'feat',...  6.83 us
    ppermute x10, starting transfers between devices, hop(): lax.ppermute(piece, 'feat', [(f, at_place(f // sides, k) * sides + f % si...  5.1 us
  transfers between devices with their start and end apart: 29, of which 11 were waited for; matrix products, arithmetic and copies ran while one was open for 6% of the time, Pallas kernels for 12%

profile of v2, /device:TPU:25, one launch (start us, length us, event | category | flops | bytes accessed | tf_op | source)
XLA Modules:
  0.0 179.8 jit_solution(17648709651111364724)
XLA Ops:
  0.7 1.3 dynamic-slice_bitcast_fusion.3
  2.1 1.3 collective-permute-start
  3.9 1.3 collective-permute-start.16
  5.3 6.8 %collective-permute-done.1 = bf16[16,48,128]{2,1,0:T(8,128)(2,1)S(1)} collective-permute-done((bf16[16,48,128]{2,1,0:T(8,128)(2,1)S(1)}, bf16[16,48,128]{2,1,0:T(8,128)(2,1)S(1)}, u32[]{:S(2)}, u32[]{:S(2)}) %collective-permute-start.1) | collective-permute-done | bytes 196640 | tf_op jit(solution)/shard_map/ppermute | solution.py:123
  13.5 16.0 %collective-permute-done.2.refs_1_ = bf16[32,48,128]{2,1,0:T(8,128)(2,1)S(1)} collective-permute-done((bf16[32,48,128]{2,1,0:T(8,128)(2,1)S(1)}, bf16[32,48,128]{2,1,0:T(8,128)(2,1)S(1)}, u32[]{:S(2)}, u32[]{:S(2)}) %collective-permute-start.2) | collective-permute-done | bytes 393248 | tf_op jit(solution)/shard_map/ppermute | solution.py:134
  30.6 1.1 collective-permute-start.4
  33.4 23.8 %collective-permute-done.4.refs_3_ = bf16[32,48,128]{2,1,0:T(8,128)(2,1)S(1)} collective-permute-done((bf16[32,48,128]{2,1,0:T(8,128)(2,1)}, bf16[32,48,128]{2,1,0:T(8,128)(2,1)S(1)}, u32[]{:S(2)}, u32[]{:S(2)}) %collective-permute-start.4) | collective-permute-done | bytes 393248 | tf_op jit(solution)/shard_map/ppermute | solution.py:134
  57.1 0.8 copy-done.24
  57.9 3.9 %select_tiles.4 = (bf16[48,48,128]{2,1,0:T(8,128)(2,1)}, bf16[48,48,128]{2,1,0:T(8,128)(2,1)}, bf16[48,48,128]{2,1,0:T(8,128)(2,1)}, bf16[48,48,128]{2,1,0:T(8,128)(2,1)}) custom-call(s32[4]{0:T(128)} %pad_add_fusion.places_ref, s32[192]{0:T(256)} %fusion.12.table_ref, bf16[32,48,128]{2,1,0:T(8,128)(2,1)} %copy-done.4, bf16[32,48,128]{2,1,0:T(8,128)(2,1)} %copy-done.23, ...), custom_call_target="tpu_custom_call" | custom-call | tf_op jit(solution)/shard_map/select_tiles/pallas_call | solution.py:42
  61.9 1.3 collective-permute-start.5
  63.2 0.8 copy-done.22
  64.2 1.3 collective-permute-start.6
  65.7 22.4 %collective-permute-done.11.refs_3_ = bf16[32,48,128]{2,1,0:T(8,128)(2,1)S(1)} collective-permute-done((bf16[32,48,128]{2,1,0:T(8,128)(2,1)}, bf16[32,48,128]{2,1,0:T(8,128)(2,1)S(1)}, u32[]{:S(2)}, u32[]{:S(2)}) %collective-permute-start.11) | collective-permute-done | bytes 393248 | tf_op jit(solution)/shard_map/ppermute | solution.py:134
  88.1 2.1 %collective-permute-start.17 = (bf16[32,96,128]{2,1,0:T(8,128)(2,1)S(1)}, bf16[32,96,128]{2,1,0:T(8,128)(2,1)S(1)}, u32[]{:S(2)}, u32[]{:S(2)}) collective-permute-start(bf16[32,96,128]{2,1,0:T(8,128)(2,1)S(1)} %constant_dynamic-update-slice_fusion.refs_0_), channel_id=1, source_target_pairs={{0,2},{1,3},{2,0},{3,1},{4,6},{5,7},{6,4},{7,5},{8,10},{9,11},{10,... | collective-permute-start | bytes 2359304 | tf_op jit(solution)/shard_map/ppermute | solution.py:134
  90.2 3.9 %select_tiles.5 = (bf16[48,48,128]{2,1,0:T(8,128)(2,1)}, bf16[48,48,128]{2,1,0:T(8,128)(2,1)}, bf16[48,48,128]{2,1,0:T(8,128)(2,1)}, bf16[48,48,128]{2,1,0:T(8,128)(2,1)}) custom-call(s32[4]{0:T(128)} %pad_add_fusion.places_ref, s32[192]{0:T(256)} %fusion.12.table_ref, bf16[32,48,128]{2,1,0:T(8,128)(2,1)} %copy-done.3, bf16[32,48,128]{2,1,0:T(8,128)(2,1)} %copy-done.21, ...), custom_call_target="tpu_custom_call" | custom-call | tf_op jit(solution)/shard_map/select_tiles/pallas_call | solution.py:42
  94.2 1.2 collective-permute-start.14
  95.4 1.4 collective-permute-start.12
  96.8 3.6 %collective-permute-done.18.refs_2_ = bf16[32,96,128]{2,1,0:T(8,128)(2,1)S(1)} collective-permute-done((bf16[32,96,128]{2,1,0:T(8,128)(2,1)S(1)}, bf16[32,96,128]{2,1,0:T(8,128)(2,1)S(1)}, u32[]{:S(2)}, u32[]{:S(2)}) %collective-permute-start.18) | collective-permute-done | bytes 786464 | tf_op jit(solution)/shard_map/ppermute | solution.py:134
  100.5 1.2 collective-permute-start.13
  101.7 1.0 fusion.17
  102.7 0.8 copy-done.8
  103.5 4.2 %collective-permute-done.14.refs_8_ = bf16[48,48,128]{2,1,0:T(8,128)(2,1)} collective-permute-done((bf16[48,48,128]{2,1,0:T(8,128)(2,1)}, bf16[48,48,128]{2,1,0:T(8,128)(2,1)}, u32[]{:S(2)}, u32[]{:S(2)}) %collective-permute-start.14) | collective-permute-done | bytes 589856 | tf_op jit(solution)/shard_map/ppermute | solution.py:174
  107.7 1.0 collective-permute-start.24
  109.4 1.0 slice.62
  110.7 1.0 slice.84
  111.7 11.7 %collective-permute-done.13.refs_7_ = bf16[48,48,128]{2,1,0:T(8,128)(2,1)} collective-permute-done((bf16[48,48,128]{2,1,0:T(8,128)(2,1)}, bf16[48,48,128]{2,1,0:T(8,128)(2,1)}, u32[]{:S(2)}, u32[]{:S(2)}) %collective-permute-start.13) | collective-permute-done | bytes 589856 | tf_op jit(solution)/shard_map/ppermute | solution.py:174
  123.8 1.0 slice.83
  124.8 1.0 slice.82
  125.9 0.9 copy-done.2
  126.7 3.3 %select_tiles.6 = (bf16[24,48,128]{2,1,0:T(8,128)(2,1)}, bf16[24,48,128]{2,1,0:T(8,128)(2,1)}, bf16[24,48,128]{2,1,0:T(8,128)(2,1)}, bf16[24,48,128]{2,1,0:T(8,128)(2,1)}) custom-call(s32[4]{0:T(128)} %pad_add_fusion.places_ref, s32[96]{0:T(128)} %reshape_squeeze.4.table_ref, bf16[32,96,128]{2,1,0:T(8,128)(2,1)} %copy-done.1, ...), custom_call_target="tpu_custom_call" | custom-call | tf_op jit(solution)/shard_map/select_tiles/pallas_call | solution.py:42
  130.3 1.2 collective-permute-start.21
  131.5 1.2 collective-permute-start.22
  132.9 1.3 collective-permute-done.24.refs_3_
  134.7 3.3 %select_tiles.7 = (bf16[24,48,128]{2,1,0:T(8,128)(2,1)}, bf16[24,48,128]{2,1,0:T(8,128)(2,1)}, bf16[24,48,128]{2,1,0:T(8,128)(2,1)}, bf16[24,48,128]{2,1,0:T(8,128)(2,1)}) custom-call(s32[4]{0:T(128)} %pad_add_fusion.places_ref, s32[96]{0:T(128)} %reshape_squeeze.4.table_ref, bf16[32,96,128]{2,1,0:T(8,128)(2,1)} %copy-done.1, ...), custom_call_target="tpu_custom_call" | custom-call | tf_op jit(solution)/shard_map/select_tiles/pallas_call | solution.py:42
  138.0 0.9 collective-permute-done.20.refs_1_
  139.0 1.1 collective-permute-start.27
  140.3 6.0 %collective-permute-done.22.refs_3_ = bf16[24,48,128]{2,1,0:T(8,128)(2,1)S(1)} collective-permute-done((bf16[24,48,128]{2,1,0:T(8,128)(2,1)}, bf16[24,48,128]{2,1,0:T(8,128)(2,1)S(1)}, u32[]{:S(2)}, u32[]{:S(2)}) %collective-permute-start.22) | collective-permute-done | bytes 294944 | tf_op jit(solution)/shard_map/ppermute | solution.py:174
  146.3 7.7 %collective-permute-start.25 = (bf16[24,48,128]{2,1,0:T(8,128)(2,1)}, bf16[24,48,128]{2,1,0:T(8,128)(2,1)S(1)}, u32[]{:S(2)}, u32[]{:S(2)}) collective-permute-start(bf16[24,48,128]{2,1,0:T(8,128)(2,1)} %get-tuple-element.51), channel_id=1, source_target_pairs={{0,1},{1,0},{2,3},{3,2},{4,5},{5,4},{6,7},{7,6},{8,9},{9,8},{10,11... | collective-permute-start | bytes 884744 | tf_op jit(solution)/shard_map/ppermute | solution.py:174
  154.0 0.9 slice.73
  155.1 1.7 collective-permute-start.23
  156.9 2.7 %collective-permute-done.25.refs_6_ = bf16[24,48,128]{2,1,0:T(8,128)(2,1)S(1)} collective-permute-done((bf16[24,48,128]{2,1,0:T(8,128)(2,1)}, bf16[24,48,128]{2,1,0:T(8,128)(2,1)S(1)}, u32[]{:S(2)}, u32[]{:S(2)}) %collective-permute-start.25) | collective-permute-done | bytes 294944 | tf_op jit(solution)/shard_map/ppermute | solution.py:174
  159.6 0.9 pad_maximum_fusion.3
  160.5 2.5 %collective-permute-start.28 = (bf16[48,48,128]{2,1,0:T(8,128)(2,1)}, bf16[48,48,128]{2,1,0:T(8,128)(2,1)S(1)}, u32[]{:S(2)}, u32[]{:S(2)}) collective-permute-start(bf16[48,48,128]{2,1,0:T(8,128)(2,1)} %pad_maximum_fusion.3), channel_id=1, source_target_pairs={{0,8},{1,9},{2,10},{3,11},{4,12},{5,13},{6,14},{7,15},{8,0},{9,1},... | collective-permute-start | bytes 1769480 | tf_op jit(solution)/shard_map/ppermute | solution.py:174
  163.1 1.0 copy-done.9
  164.1 1.1 copy-done.10
  165.2 7.7 %gram_sum.1 = (f32[12,128,128]{2,1,0:T(8,128)}, bf16[12,128,768]{2,1,0:T(8,128)(2,1)}) custom-call(bf16[48,48,128]{2,1,0:T(8,128)(2,1)} %get-tuple-element.31.refs_0_, bf16[48,48,128]{2,1,0:T(8,128)(2,1)} %copy-done.6, bf16[48,48,128]{2,1,0:T(8,128)(2,1)} %copy-done.7, bf16[48,48,128]{2,1,0:T(8,128)(2,1)} %copy-done.8, bf16[96,48,128]{2,1,0:T(8,128)(2,1)} %copy-done.9, ...), custom_call_target="tpu_custom_call" | custom-call | tf_op jit(solution)/shard_map/gram_sum/pallas_call | solution.py:86
  172.9 0.8 copy-done.19
  173.9 6.0 %cross_sum.1 = f32[12,128,128]{2,1,0:T(8,128)} custom-call(bf16[12,128,768]{2,1,0:T(8,128)(2,1)} %get-tuple-element.44.left_ref, bf16[24,48,128]{2,1,0:T(8,128)(2,1)} %get-tuple-element.46.refs_0_, bf16[24,48,128]{2,1,0:T(8,128)(2,1)} %copy-done.13, bf16[24,48,128]{2,1,0:T(8,128)(2,1)} %copy-done.14, bf16[24,48,128]{2,1,0:T(8,128)(2,1)} %copy-done.15, ...), custom_call_target="tpu_custom_call" | custom-call | tf_op jit(solution)/shard_map/cross_sum/pallas_call | solution.py:86
  (126 shorter events, 8.1 us)
Async XLA Ops:
  0.7 3.0 %copy-start.11 = (bf16[192,2048]{1,0:T(8,128)(2,1)S(1)}, bf16[192,2048]{1,0:T(8,128)(2,1)}, u32[]{:S(2)}) copy-start(bf16[192,2048]{1,0:T(8,128)(2,1)} %param.4) | copy-start | bytes 2359300
  2.1 11.3 %collective-permute-start = (bf16[16,48,128]{2,1,0:T(8,128)(2,1)S(1)}, bf16[16,48,128]{2,1,0:T(8,128)(2,1)S(1)}, u32[]{:S(2)}, u32[]{:S(2)}) collective-permute-start(bf16[16,48,128]{2,1,0:T(8,128)(2,1)S(1)} %bitcast.76), channel_id=1, source_target_pairs={{0,1},{1,0},{2,3},{3,2},{4,5},{5,4},{6,7},{7,6},{8,9},{9,8},{10,11... | collective-permute-start | bytes 589832 | tf_op jit(solution)/shard_map/ppermute | solution.py:123
  3.4 8.7 %collective-permute-start.1 = (bf16[16,48,128]{2,1,0:T(8,128)(2,1)S(1)}, bf16[16,48,128]{2,1,0:T(8,128)(2,1)S(1)}, u32[]{:S(2)}, u32[]{:S(2)}) collective-permute-start(bf16[16,48,128]{2,1,0:T(8,128)(2,1)S(1)} %bitcast.77), channel_id=1, source_target_pairs={{0,1},{1,0},{2,3},{3,2},{4,5},{5,4},{6,7},{7,6},{8,9},{9,8},{10,11... | collective-permute-start | bytes 589832 | tf_op jit(solution)/shard_map/ppermute | solution.py:123
  3.8 8.8 %copy-start.26 = (s32[384,2]{0,1:T(2,128)S(1)}, s32[384,2]{0,1:T(2,128)}, u32[]{:S(2)}) copy-start(s32[384,2]{0,1:T(2,128)} %param.5) | copy-start | bytes 9220
  3.9 59.3 %collective-permute-start.16 = (bf16[16,96,128]{2,1,0:T(8,128)(2,1)S(1)}, bf16[16,96,128]{2,1,0:T(8,128)(2,1)S(1)}, u32[]{:S(2)}, u32[]{:S(2)}) collective-permute-start(bf16[16,96,128]{2,1,0:T(8,128)(2,1)S(1)} %bitcast.75), channel_id=1, source_target_pairs={{0,1},{1,0},{2,3},{3,2},{4,5},{5,4},{6,7},{7,6},{8,9},{9,8},{10,11... | collective-permute-start | bytes 1179656 | tf_op jit(solution)/shard_map/ppermute | solution.py:123
  12.2 20.6 %copy-start.4 = (bf16[32,48,128]{2,1,0:T(8,128)(2,1)}, bf16[32,48,128]{2,1,0:T(8,128)(2,1)S(1)}, u32[]{:S(2)}) copy-start(bf16[32,48,128]{2,1,0:T(8,128)(2,1)S(1)} %pad_maximum_fusion.5.refs_0_) | copy-start | bytes 1179652
  12.2 17.3 %collective-permute-start.2 = (bf16[32,48,128]{2,1,0:T(8,128)(2,1)S(1)}, bf16[32,48,128]{2,1,0:T(8,128)(2,1)S(1)}, u32[]{:S(2)}, u32[]{:S(2)}) collective-permute-start(bf16[32,48,128]{2,1,0:T(8,128)(2,1)S(1)} %pad_maximum_fusion.5.refs_0_), channel_id=1, source_target_pairs={{0,2},{1,3},{2,0},{3,1},{4,6},{5,7},{6,4},{7,5},{8,10},{9,11},{10,... | collective-permute-start | bytes 1179656 | tf_op jit(solution)/shard_map/ppermute | solution.py:134
  12.4 17.0 %collective-permute-start.3 = (bf16[32,48,128]{2,1,0:T(8,128)(2,1)S(1)}, bf16[32,48,128]{2,1,0:T(8,128)(2,1)}, u32[]{:S(2)}, u32[]{:S(2)}) collective-permute-start(bf16[32,48,128]{2,1,0:T(8,128)(2,1)S(1)} %pad_maximum_fusion.5.refs_0_), channel_id=1, source_target_pairs={{0,4},{1,5},{2,6},{3,7},{4,0},{5,1},{6,2},{7,3},{8,12},{9,13},{10,... | collective-permute-start | bytes 1179656 | tf_op jit(solution)/shard_map/ppermute | solution.py:134
  13.5 48.4 %copy-start.3 = (bf16[32,48,128]{2,1,0:T(8,128)(2,1)}, bf16[32,48,128]{2,1,0:T(8,128)(2,1)S(1)}, u32[]{:S(2)}) copy-start(bf16[32,48,128]{2,1,0:T(8,128)(2,1)S(1)} %pad_maximum_fusion.4.refs_0_) | copy-start | bytes 1179652
  30.2 33.0 %collective-permute-start.9 = (bf16[32,48,128]{2,1,0:T(8,128)(2,1)S(1)}, bf16[32,48,128]{2,1,0:T(8,128)(2,1)S(1)}, u32[]{:S(2)}, u32[]{:S(2)}) collective-permute-start(bf16[32,48,128]{2,1,0:T(8,128)(2,1)S(1)} %pad_maximum_fusion.4.refs_0_), channel_id=1, source_target_pairs={{0,2},{1,3},{2,0},{3,1},{4,6},{5,7},{6,4},{7,5},{8,10},{9,11},{10,... | collective-permute-start | bytes 1179656 | tf_op jit(solution)/shard_map/ppermute | solution.py:134
  30.2 33.0 %collective-permute-start.10 = (bf16[32,48,128]{2,1,0:T(8,128)(2,1)S(1)}, bf16[32,48,128]{2,1,0:T(8,128)(2,1)S(1)}, u32[]{:S(2)}, u32[]{:S(2)}) collective-permute-start(bf16[32,48,128]{2,1,0:T(8,128)(2,1)S(1)} %pad_maximum_fusion.4.refs_0_), channel_id=1, source_target_pairs={{0,4},{1,5},{2,6},{3,7},{4,0},{5,1},{6,2},{7,3},{8,12},{9,13},{10,... | collective-permute-start | bytes 1179656 | tf_op jit(solution)/shard_map/ppermute | solution.py:134
  30.6 26.6 %collective-permute-start.4 = (bf16[32,48,128]{2,1,0:T(8,128)(2,1)}, bf16[32,48,128]{2,1,0:T(8,128)(2,1)S(1)}, u32[]{:S(2)}, u32[]{:S(2)}) collective-permute-start(bf16[32,48,128]{2,1,0:T(8,128)(2,1)} %collective-permute-done.3.refs_2_), channel_id=1, source_target_pairs={{0,2},{1,3},{2,0},{3,1},{4,6},{5,7},{6,4},{7,5},{8,10},{9,11},{10,... | collective-permute-start | bytes 1179656 | tf_op jit(solution)/shard_map/ppermute | solution.py:134
  61.9 2.3 %copy-start.28 = (bf16[48,48,128]{2,1,0:T(8,128)(2,1)S(1)}, bf16[48,48,128]{2,1,0:T(8,128)(2,1)}, u32[]{:S(2)}) copy-start(bf16[48,48,128]{2,1,0:T(8,128)(2,1)} %get-tuple-element.33) | copy-start | bytes 1769476
  61.9 3.7 %copy-start.27 = (bf16[48,48,128]{2,1,0:T(8,128)(2,1)S(1)}, bf16[48,48,128]{2,1,0:T(8,128)(2,1)}, u32[]{:S(2)}) copy-start(bf16[48,48,128]{2,1,0:T(8,128)(2,1)} %get-tuple-element.34) | copy-start | bytes 1769476
  61.9 32.3 %collective-permute-start.5 = (bf16[48,48,128]{2,1,0:T(8,128)(2,1)}, bf16[48,48,128]{2,1,0:T(8,128)(2,1)S(1)}, u32[]{:S(2)}, u32[]{:S(2)}) collective-permute-start(bf16[48,48,128]{2,1,0:T(8,128)(2,1)} %get-tuple-element.32), channel_id=1, source_target_pairs={{0,1},{1,0},{2,3},{3,2},{4,5},{5,4},{6,7},{7,6},{8,9},{9,8},{10,11... | collective-permute-start | bytes 1769480 | tf_op jit(solution)/shard_map/ppermute | solution.py:174
  63.2 27.1 %copy-start.21 = (bf16[32,48,128]{2,1,0:T(8,128)(2,1)}, bf16[32,48,128]{2,1,0:T(8,128)(2,1)S(1)}, u32[]{:S(2)}) copy-start(bf16[32,48,128]{2,1,0:T(8,128)(2,1)S(1)} %collective-permute-done.9.refs_1_) | copy-start | bytes 1179652
  64.0 38.6 %copy-start.1 = (bf16[32,96,128]{2,1,0:T(8,128)(2,1)}, bf16[32,96,128]{2,1,0:T(8,128)(2,1)S(1)}, u32[]{:S(2)}) copy-start(bf16[32,96,128]{2,1,0:T(8,128)(2,1)S(1)} %constant_dynamic-update-slice_fusion.refs_0_) | copy-start | bytes 2359300
  64.0 36.4 %collective-permute-start.18 = (bf16[32,96,128]{2,1,0:T(8,128)(2,1)S(1)}, bf16[32,96,128]{2,1,0:T(8,128)(2,1)S(1)}, u32[]{:S(2)}, u32[]{:S(2)}) collective-permute-start(bf16[32,96,128]{2,1,0:T(8,128)(2,1)S(1)} %constant_dynamic-update-slice_fusion.refs_0_), channel_id=1, source_target_pairs={{0,4},{1,5},{2,6},{3,7},{4,0},{5,1},{6,2},{7,3},{8,12},{9,13},{10,... | collective-permute-start | bytes 2359304 | tf_op jit(solution)/shard_map/ppermute | solution.py:134
  64.1 24.0 %collective-permute-start.11 = (bf16[32,48,128]{2,1,0:T(8,128)(2,1)}, bf16[32,48,128]{2,1,0:T(8,128)(2,1)S(1)}, u32[]{:S(2)}, u32[]{:S(2)}) collective-permute-start(bf16[32,48,128]{2,1,0:T(8,128)(2,1)} %copy-done.22), channel_id=1, source_target_pairs={{0,2},{1,3},{2,0},{3,1},{4,6},{5,7},{6,4},{7,5},{8,10},{9,11},{10,... | collective-permute-start | bytes 1179656 | tf_op jit(solution)/shard_map/ppermute | solution.py:134
  64.2 31.2 %collective-permute-start.6 = (bf16[48,48,128]{2,1,0:T(8,128)(2,1)S(1)}, bf16[48,48,128]{2,1,0:T(8,128)(2,1)S(1)}, u32[]{:S(2)}, u32[]{:S(2)}) collective-permute-start(bf16[48,48,128]{2,1,0:T(8,128)(2,1)S(1)} %copy-done.28), channel_id=1, source_target_pairs={{0,16},{1,17},{2,18},{3,19},{4,20},{5,21},{6,22},{7,23},{8,24},{9,... | collective-permute-start | bytes 1769480 | tf_op jit(solution)/shard_map/ppermute | solution.py:174
  65.5 37.1 %collective-permute-start.7 = (bf16[48,48,128]{2,1,0:T(8,128)(2,1)S(1)}, bf16[48,48,128]{2,1,0:T(8,128)(2,1)S(1)}, u32[]{:S(2)}, u32[]{:S(2)}) collective-permute-start(bf16[48,48,128]{2,1,0:T(8,128)(2,1)S(1)} %copy-done.27), channel_id=1, source_target_pairs={{0,17},{1,16},{2,19},{3,18},{4,21},{5,20},{6,23},{7,22},{8,25},{9,... | collective-permute-start | bytes 1769480 | tf_op jit(solution)/shard_map/ppermute | solution.py:174
  88.1 37.7 %collective-permute-start.17 = (bf16[32,96,128]{2,1,0:T(8,128)(2,1)S(1)}, bf16[32,96,128]{2,1,0:T(8,128)(2,1)S(1)}, u32[]{:S(2)}, u32[]{:S(2)}) collective-permute-start(bf16[32,96,128]{2,1,0:T(8,128)(2,1)S(1)} %constant_dynamic-update-slice_fusion.refs_0_), channel_id=1, source_target_pairs={{0,2},{1,3},{2,0},{3,1},{4,6},{5,7},{6,4},{7,5},{8,10},{9,11},{10,... | collective-permute-start | bytes 2359304 | tf_op jit(solution)/shard_map/ppermute | solution.py:134
  94.1 15.2 %copy-start.5 = (bf16[48,48,128]{2,1,0:T(8,128)(2,1)S(1)}, bf16[48,48,128]{2,1,0:T(8,128)(2,1)}, u32[]{:S(2)}) copy-start(bf16[48,48,128]{2,1,0:T(8,128)(2,1)} %get-tuple-element.31.refs_0_) | copy-start | bytes 1769476
  94.2 16.3 %copy-start.6 = (bf16[48,48,128]{2,1,0:T(8,128)(2,1)}, bf16[48,48,128]{2,1,0:T(8,128)(2,1)S(1)}, u32[]{:S(2)}) copy-start(bf16[48,48,128]{2,1,0:T(8,128)(2,1)S(1)} %collective-permute-done.5.refs_1_) | copy-start | bytes 1769476
  94.2 13.5 %collective-permute-start.14 = (bf16[48,48,128]{2,1,0:T(8,128)(2,1)}, bf16[48,48,128]{2,1,0:T(8,128)(2,1)}, u32[]{:S(2)}, u32[]{:S(2)}) collective-permute-start(bf16[48,48,128]{2,1,0:T(8,128)(2,1)} %get-tuple-element.42), channel_id=1, source_target_pairs={{0,17},{1,16},{2,19},{3,18},{4,21},{5,20},{6,23},{7,22},{8,25},{9,... | collective-permute-start | bytes 1769480 | tf_op jit(solution)/shard_map/ppermute | solution.py:174
  95.4 7.2 %copy-start.7 = (bf16[48,48,128]{2,1,0:T(8,128)(2,1)}, bf16[48,48,128]{2,1,0:T(8,128)(2,1)S(1)}, u32[]{:S(2)}) copy-start(bf16[48,48,128]{2,1,0:T(8,128)(2,1)S(1)} %collective-permute-done.6.refs_2_) | copy-start | bytes 1769476
  95.4 29.4 %collective-permute-start.12 = (bf16[48,48,128]{2,1,0:T(8,128)(2,1)}, bf16[48,48,128]{2,1,0:T(8,128)(2,1)}, u32[]{:S(2)}, u32[]{:S(2)}) collective-permute-start(bf16[48,48,128]{2,1,0:T(8,128)(2,1)} %get-tuple-element.40), channel_id=1, source_target_pairs={{0,1},{1,0},{2,3},{3,2},{4,5},{5,4},{6,7},{7,6},{8,9},{9,8},{10,11... | collective-permute-start | bytes 1769480 | tf_op jit(solution)/shard_map/ppermute | solution.py:174
  100.5 10.0 %copy-start = (bf16[32,96,128]{2,1,0:T(8,128)(2,1)}, bf16[32,96,128]{2,1,0:T(8,128)(2,1)S(1)}, u32[]{:S(2)}) copy-start(bf16[32,96,128]{2,1,0:T(8,128)(2,1)S(1)} %collective-permute-done.18.refs_2_) | copy-start | bytes 2359300
  100.5 22.9 %collective-permute-start.13 = (bf16[48,48,128]{2,1,0:T(8,128)(2,1)}, bf16[48,48,128]{2,1,0:T(8,128)(2,1)}, u32[]{:S(2)}, u32[]{:S(2)}) collective-permute-start(bf16[48,48,128]{2,1,0:T(8,128)(2,1)} %get-tuple-element.41), channel_id=1, source_target_pairs={{0,16},{1,17},{2,18},{3,19},{4,20},{5,21},{6,22},{7,23},{8,24},{9,... | collective-permute-start | bytes 1769480 | tf_op jit(solution)/shard_map/ppermute | solution.py:174
  103.5 22.4 %collective-permute-start.19 = (bf16[32,48,128]{2,1,0:T(8,128)(2,1)}, bf16[32,48,128]{2,1,0:T(8,128)(2,1)}, u32[]{:S(2)}, u32[]{:S(2)}) collective-permute-start(bf16[32,48,128]{2,1,0:T(8,128)(2,1)} %get-tuple-element.61), channel_id=1, source_target_pairs={{0,2},{1,3},{2,0},{3,1},{4,6},{5,7},{6,4},{7,5},{8,10},{9,11},{10,... | collective-permute-start | bytes 1179656 | tf_op jit(solution)/shard_map/ppermute | solution.py:134
  107.7 26.5 %collective-permute-start.24 = (bf16[32,48,128]{2,1,0:T(8,128)(2,1)}, bf16[32,48,128]{2,1,0:T(8,128)(2,1)}, u32[]{:S(2)}, u32[]{:S(2)}) collective-permute-start(bf16[32,48,128]{2,1,0:T(8,128)(2,1)} %get-tuple-element.60), channel_id=1, source_target_pairs={{0,2},{1,3},{2,0},{3,1},{4,6},{5,7},{6,4},{7,5},{8,10},{9,11},{10,... | collective-permute-start | bytes 1179656 | tf_op jit(solution)/shard_map/ppermute | solution.py:134
  123.3 39.7 %collective-permute-start.8 = (bf16[96,48,128]{2,1,0:T(8,128)(2,1)S(1)}, bf16[96,48,128]{2,1,0:T(8,128)(2,1)S(1)}, u32[]{:S(2)}, u32[]{:S(2)}) collective-permute-start(bf16[96,48,128]{2,1,0:T(8,128)(2,1)S(1)} %pad_maximum_fusion), channel_id=1, source_target_pairs={{0,8},{1,9},{2,10},{3,11},{4,12},{5,13},{6,14},{7,15},{8,0},{9,1},... | collective-permute-start | bytes 3538952 | tf_op jit(solution)/shard_map/ppermute | solution.py:174
  130.0 8.9 %collective-permute-start.20 = (bf16[24,48,128]{2,1,0:T(8,128)(2,1)}, bf16[24,48,128]{2,1,0:T(8,128)(2,1)S(1)}, u32[]{:S(2)}, u32[]{:S(2)}) collective-permute-start(bf16[24,48,128]{2,1,0:T(8,128)(2,1)} %get-tuple-element.47), channel_id=1, source_target_pairs={{0,1},{1,0},{2,3},{3,2},{4,5},{5,4},{6,7},{7,6},{8,9},{9,8},{10,11... | collective-permute-start | bytes 884744 | tf_op jit(solution)/shard_map/ppermute | solution.py:174
  130.3 9.8 %collective-permute-start.21 = (bf16[24,48,128]{2,1,0:T(8,128)(2,1)}, bf16[24,48,128]{2,1,0:T(8,128)(2,1)S(1)}, u32[]{:S(2)}, u32[]{:S(2)}) collective-permute-start(bf16[24,48,128]{2,1,0:T(8,128)(2,1)} %get-tuple-element.48), channel_id=1, source_target_pairs={{0,16},{1,17},{2,18},{3,19},{4,20},{5,21},{6,22},{7,23},{8,24},{9,... | collective-permute-start | bytes 884744 | tf_op jit(solution)/shard_map/ppermute | solution.py:174
  131.5 14.8 %collective-permute-start.22 = (bf16[24,48,128]{2,1,0:T(8,128)(2,1)}, bf16[24,48,128]{2,1,0:T(8,128)(2,1)S(1)}, u32[]{:S(2)}, u32[]{:S(2)}) collective-permute-start(bf16[24,48,128]{2,1,0:T(8,128)(2,1)} %get-tuple-element.49), channel_id=1, source_target_pairs={{0,17},{1,16},{2,19},{3,18},{4,21},{5,20},{6,23},{7,22},{8,25},{9,... | collective-permute-start | bytes 884744 | tf_op jit(solution)/shard_map/ppermute | solution.py:174
  132.9 21.1 %copy-start.12 = (bf16[24,48,128]{2,1,0:T(8,128)(2,1)S(1)}, bf16[24,48,128]{2,1,0:T(8,128)(2,1)}, u32[]{:S(2)}) copy-start(bf16[24,48,128]{2,1,0:T(8,128)(2,1)} %get-tuple-element.46.refs_0_) | copy-start | bytes 884740
  134.2 28.9 %collective-permute-start.15 = (bf16[96,48,128]{2,1,0:T(8,128)(2,1)S(1)}, bf16[96,48,128]{2,1,0:T(8,128)(2,1)S(1)}, u32[]{:S(2)}, u32[]{:S(2)}) collective-permute-start(bf16[96,48,128]{2,1,0:T(8,128)(2,1)S(1)} %pad_maximum_fusion.1), channel_id=1, source_target_pairs={{0,8},{1,9},{2,10},{3,11},{4,12},{5,13},{6,14},{7,15},{8,0},{9,1},... | collective-permute-start | bytes 3538952 | tf_op jit(solution)/shard_map/ppermute | solution.py:174
  138.9 16.1 %copy-start.13 = (bf16[24,48,128]{2,1,0:T(8,128)(2,1)}, bf16[24,48,128]{2,1,0:T(8,128)(2,1)S(1)}, u32[]{:S(2)}) copy-start(bf16[24,48,128]{2,1,0:T(8,128)(2,1)S(1)} %collective-permute-done.20.refs_1_) | copy-start | bytes 884740
  139.0 16.2 %collective-permute-start.27 = (bf16[24,48,128]{2,1,0:T(8,128)(2,1)}, bf16[24,48,128]{2,1,0:T(8,128)(2,1)S(1)}, u32[]{:S(2)}, u32[]{:S(2)}) collective-permute-start(bf16[24,48,128]{2,1,0:T(8,128)(2,1)} %get-tuple-element.53), channel_id=1, source_target_pairs={{0,17},{1,16},{2,19},{3,18},{4,21},{5,20},{6,23},{7,22},{8,25},{9,... | collective-permute-start | bytes 884744 | tf_op jit(solution)/shard_map/ppermute | solution.py:174
  140.1 15.0 %copy-start.14 = (bf16[24,48,128]{2,1,0:T(8,128)(2,1)}, bf16[24,48,128]{2,1,0:T(8,128)(2,1)S(1)}, u32[]{:S(2)}) copy-start(bf16[24,48,128]{2,1,0:T(8,128)(2,1)S(1)} %collective-permute-done.21.refs_2_) | copy-start | bytes 884740
  140.1 16.8 %collective-permute-start.26 = (bf16[24,48,128]{2,1,0:T(8,128)(2,1)}, bf16[24,48,128]{2,1,0:T(8,128)(2,1)S(1)}, u32[]{:S(2)}, u32[]{:S(2)}) collective-permute-start(bf16[24,48,128]{2,1,0:T(8,128)(2,1)} %get-tuple-element.52), channel_id=1, source_target_pairs={{0,16},{1,17},{2,18},{3,19},{4,20},{5,21},{6,22},{7,23},{8,24},{9,... | collective-permute-start | bytes 884744 | tf_op jit(solution)/shard_map/ppermute | solution.py:174
  146.3 8.8 %copy-start.15 = (bf16[24,48,128]{2,1,0:T(8,128)(2,1)}, bf16[24,48,128]{2,1,0:T(8,128)(2,1)S(1)}, u32[]{:S(2)}) copy-start(bf16[24,48,128]{2,1,0:T(8,128)(2,1)S(1)} %collective-permute-done.22.refs_3_) | copy-start | bytes 884740
  146.3 13.4 %collective-permute-start.25 = (bf16[24,48,128]{2,1,0:T(8,128)(2,1)}, bf16[24,48,128]{2,1,0:T(8,128)(2,1)S(1)}, u32[]{:S(2)}, u32[]{:S(2)}) collective-permute-start(bf16[24,48,128]{2,1,0:T(8,128)(2,1)} %get-tuple-element.51), channel_id=1, source_target_pairs={{0,1},{1,0},{2,3},{3,2},{4,5},{5,4},{6,7},{7,6},{8,9},{9,8},{10,11... | collective-permute-start | bytes 884744 | tf_op jit(solution)/shard_map/ppermute | solution.py:174
  155.1 17.7 %copy-start.16 = (bf16[24,48,128]{2,1,0:T(8,128)(2,1)}, bf16[24,48,128]{2,1,0:T(8,128)(2,1)S(1)}, u32[]{:S(2)}) copy-start(bf16[24,48,128]{2,1,0:T(8,128)(2,1)S(1)} %collective-permute-done.27.refs_8_) | copy-start | bytes 884740
  155.1 17.7 %collective-permute-start.23 = (bf16[48,48,128]{2,1,0:T(8,128)(2,1)S(1)}, bf16[48,48,128]{2,1,0:T(8,128)(2,1)S(1)}, u32[]{:S(2)}, u32[]{:S(2)}) collective-permute-start(bf16[48,48,128]{2,1,0:T(8,128)(2,1)S(1)} %pad_maximum_fusion.2), channel_id=1, source_target_pairs={{0,8},{1,9},{2,10},{3,11},{4,12},{5,13},{6,14},{7,15},{8,0},{9,1},... | collective-permute-start | bytes 1769480 | tf_op jit(solution)/shard_map/ppermute | solution.py:174
  156.9 15.9 %copy-start.17 = (bf16[24,48,128]{2,1,0:T(8,128)(2,1)}, bf16[24,48,128]{2,1,0:T(8,128)(2,1)S(1)}, u32[]{:S(2)}) copy-start(bf16[24,48,128]{2,1,0:T(8,128)(2,1)S(1)} %collective-permute-done.26.refs_7_) | copy-start | bytes 884740
  159.6 13.2 %copy-start.18 = (bf16[24,48,128]{2,1,0:T(8,128)(2,1)}, bf16[24,48,128]{2,1,0:T(8,128)(2,1)S(1)}, u32[]{:S(2)}) copy-start(bf16[24,48,128]{2,1,0:T(8,128)(2,1)S(1)} %collective-permute-done.25.refs_6_) | copy-start | bytes 884740
  160.5 12.3 %collective-permute-start.28 = (bf16[48,48,128]{2,1,0:T(8,128)(2,1)}, bf16[48,48,128]{2,1,0:T(8,128)(2,1)S(1)}, u32[]{:S(2)}, u32[]{:S(2)}) collective-permute-start(bf16[48,48,128]{2,1,0:T(8,128)(2,1)} %pad_maximum_fusion.3), channel_id=1, source_target_pairs={{0,8},{1,9},{2,10},{3,11},{4,12},{5,13},{6,14},{7,15},{8,0},{9,1},... | collective-permute-start | bytes 1769480 | tf_op jit(solution)/shard_map/ppermute | solution.py:174
  (12 other events, 12.2 us)

commit v3 on v2

v3 whole, which is shorter than its diff:
```python
import functools

import jax
import jax.numpy as jnp
from jax import lax
from jax.experimental import pallas as pl
from jax.experimental.pallas import tpu as pltpu
from jax.sharding import PartitionSpec as P

BLK = 128
VMEM_LIMIT = 56 << 20
CROSS_LIMIT = 24 << 20


def select_kernel(line, groups, places_ref, table_ref, *refs):
    pieces, (out_ref, held, stage, sems, out_sems) = refs[:-5], refs[-5:]
    streams = len(pieces) // line
    per = held.shape[0] // len(pieces)
    copies = [
        pltpu.make_async_copy(
            piece, held.at[pl.ds((places_ref[n % line] * streams + n // line) * per, per)], sems.at[n]
        )
        for n, piece in enumerate(pieces)
    ]
    for copy in copies:
        copy.start()
    for copy in copies:
        copy.wait()
    count = stage.shape[0] // groups
    copies = []
    for g in range(groups):

        @pl.loop(0, count, unroll=4)
        def _(i, g=g):
            stage[g * count + i] = held[table_ref[g * count + i]]

        part = pl.ds(g * count, count)
        copies.append(pltpu.make_async_copy(stage.at[part], out_ref.at[part], out_sems.at[g]))
        copies[-1].start()
    for copy in copies:
        copy.wait()


def select_tiles(places, table, streams, groups):
    pieces = [piece for stream in streams for piece in stream]
    blocks, rows, blk = pieces[0].shape
    dtype = pieces[0].dtype
    out_shape = (table.shape[0], rows, blk)
    return pl.pallas_call(
        functools.partial(select_kernel, len(streams[0]), groups),
        out_shape=jax.ShapeDtypeStruct(out_shape, dtype),
        in_specs=[pl.BlockSpec(memory_space=pltpu.SMEM)] * 2
        + [pl.BlockSpec(memory_space=pl.ANY)] * len(pieces),
        out_specs=pl.BlockSpec(memory_space=pl.ANY),
        scratch_shapes=[
            pltpu.VMEM((len(pieces) * blocks, rows, blk), dtype),
            pltpu.VMEM(out_shape, dtype),
            pltpu.SemaphoreType.DMA((len(pieces),)),
            pltpu.SemaphoreType.DMA((groups,)),
        ],
        compiler_params=pltpu.CompilerParams(vmem_limit_bytes=VMEM_LIMIT),
        name="select_tiles",
    )(places, table, *pieces)


def rows_of(ref, group, which):
    return jnp.concatenate([ref[k + which] for k in range(0, ref.shape[0], group)], 0)


def gram_kernel(inverse, tiles, out_ref, left_ref):
    pairs = out_ref.shape[0]

    @pl.loop(0, pairs, unroll=2)
    def _(p):
        left = rows_of(tiles, 2 * pairs, 2 * p).T
        right = rows_of(tiles, 2 * pairs, 2 * p + 1)
        left_ref[p] = left
        out_ref[p] = jnp.dot(left, right, preferred_element_type=jnp.float32) * inverse


def cross_kernel(inverse, left_ref, tiles, out_ref):
    pairs = out_ref.shape[0]

    @pl.loop(0, pairs, unroll=4)
    def _(p):
        right = rows_of(tiles, pairs, p)
        out_ref[p] = jnp.dot(left_ref[p], right, preferred_element_type=jnp.float32) * inverse


def sum_call(kernel, operands, outs, name, vmem):
    return pl.pallas_call(
        kernel,
        out_shape=outs,
        in_specs=[pl.BlockSpec(memory_space=pltpu.VMEM)] * len(operands),
        out_specs=[pl.BlockSpec(memory_space=pltpu.VMEM)] * len(outs),
        compiler_params=pltpu.CompilerParams(vmem_limit_bytes=vmem),
        name=name,
    )(*operands)


def after(values, done):
    return lax.optimization_barrier((values, done))


def body(span_input, span_output, block_pairs):
    tok_count = lax.axis_size("tok")
    feat_count = lax.axis_size("feat")
    feat = lax.axis_index("feat")
    rows, width = span_input.shape
    inverse = 1.0 / (tok_count * rows)
    pairs = block_pairs.shape[0] // (tok_count * feat_count)
    own_blocks = width // BLK
    sides = 2 if feat_count % 2 == 0 and rows % 32 == 0 else 1
    line = feat_count // sides
    place, side = feat // sides, feat % sides
    part = rows // sides
    paired = line & (line - 1) == 0

    def blocks_of(array, which):
        taken = lax.dynamic_slice_in_dim(array, which * part, part, 0)
        return taken.reshape(part, own_blocks, BLK).transpose(1, 0, 2)

    def from_sides(array):
        return [
            lax.ppermute(
                blocks_of(array, (side + d) % sides), "feat",
                [(f, f // sides * sides + (f % sides + d) % sides) for f in range(feat_count)],
            )
            for d in range(1, sides)
        ]

    def at_place(p, k):
        return p ^ k if paired else (p + k) % line

    def hop(piece, k):
        return lax.ppermute(piece, "feat", [
            (f, at_place(f // sides, k) * sides + f % sides) for f in range(feat_count)
        ])

    def far_hops(unit):
        held = {0: unit}
        if not paired:
            held.update({k: hop(unit, k) for k in range(1, line)})
            return held
        k = line // 2
        while k > 1:
            held.update({m ^ k: hop(piece, k) for m, piece in list(held.items())})
            k //= 2
        if line > 1:
            held[1] = hop(unit, 1)
        return held

    def last_hops(held):
        return {m ^ 1: hop(held[m], 1) for m in held if m > 1 and m ^ 1 not in held}

    def in_order(held):
        return [held[k] for k in range(line)]

    places = jnp.stack([at_place(place, k) if paired else (place - k) % line for k in range(line)])
    places = places.astype(jnp.int32)

    owners = [(t, s) for t in range(tok_count) for s in range(sides)]
    groups = [[t * feat_count + p * sides + s for t, s in owners] for p in range(line)]
    listed = block_pairs.reshape(tok_count, line, sides * pairs, 2)
    listed = lax.dynamic_index_in_dim(listed, place, 1, keepdims=False).reshape(-1, 2)
    stream = (side - listed // own_blocks % sides) % sides
    slots = listed // (own_blocks * sides) * (own_blocks * sides) + stream * own_blocks + listed % own_blocks

    def to_owners(tiles):
        return lax.all_to_all(
            tiles, ("tok", "feat"), split_axis=0, concat_axis=0, axis_index_groups=groups, tiled=True
        )

    own_out = blocks_of(span_output, side)
    others_in, others_out = from_sides(span_input), from_sides(span_output)
    streams_in = [far_hops(blocks_of(span_input, side))]
    if sides > 1:
        others_in, streams_in[0][1] = after(others_in, streams_in[0][1])
        streams_in += [far_hops(other) for other in others_in]
    streams_in[0].update(last_hops(streams_in[0]))
    (own_out, others_out), streams_in[-1] = after((own_out, others_out), streams_in[-1])
    for held in streams_in[1:]:
        held.update(last_hops(held))
    streams_out = [far_hops(unit) for unit in [own_out] + others_out]
    picked = select_tiles(places, slots.reshape(-1), [in_order(h) for h in streams_in], len(owners))
    tiles_in = to_owners(picked)
    for held in streams_out:
        held.update(last_hops(held))
    picked = select_tiles(places, slots[:, 1], [in_order(h) for h in streams_out], len(owners))
    tiles_out = to_owners(picked)

    gram_shape = jax.ShapeDtypeStruct((pairs, BLK, BLK), jnp.float32)
    left_shape = jax.ShapeDtypeStruct((pairs, BLK, tok_count * rows), span_input.dtype)
    gram, left = sum_call(
        functools.partial(gram_kernel, inverse), [tiles_in], [gram_shape, left_shape], "gram_sum", VMEM_LIMIT
    )
    (cross,) = sum_call(
        functools.partial(cross_kernel, inverse), [left, tiles_out], [gram_shape], "cross_sum", CROSS_LIMIT
    )
    return gram, cross


def solution(mesh):
    return jax.shard_map(
        body,
        mesh=mesh,
        in_specs=(P("tok", "feat"), P("tok", "feat"), P()),
        out_specs=(P(("tok", "feat"), None, None), P(("tok", "feat"), None, None)),
        check_vma=False,
    )
```

time: 182 us -> 166 us (0.912)
  waiting for transfers between devices: 99.5 us -> 122 us
  starting transfers between devices: 31.5 us -> 17.8 us
  Pallas kernels: 28.1 us -> 16.6 us
  local copies, waits for them, and re-layouts: 16.6 us -> 6.01 us
    ppermute x19 -> x2, waiting for transfers between devices: 32.3 us -> 7.38 us  [from_sides(): lax.ppermute(blocks_of(array, (side + d) % sides), 'feat', [(f, f // side...]
    ppermute x10 -> x12, waiting for transfers between devices: 67.1 us -> 92.1 us  [hop(): lax.ppermute(piece, 'feat', [(f, at_place(f // sides, k) * sides + f % si...]
    ppermute x19 -> x2, starting transfers between devices: 26.4 us -> 1.48 us  [from_sides(): lax.ppermute(blocks_of(array, (side + d) % sides), 'feat', [(f, f // side...]
    all_to_all x0 -> x2, waiting for transfers between devices: none -> 22.5 us  [to_owners(): lax.all_to_all(tiles, ('tok', 'feat'), split_axis=0, concat_axis=0, axis_...]
    all_to_all x0 -> x2, starting transfers between devices: none -> 10.6 us  [to_owners(): lax.all_to_all(tiles, ('tok', 'feat'), split_axis=0, concat_axis=0, axis_...]
    slice x19 -> x0, local copies, waits for them, and re-layouts: 6.02 us -> none  [the longest x18 5.05 us: to_owners(): got.append(send(jnp.concatenate([g[own:] for g in got], 0), (0, 0), 1))]
    pallas_call x2, Pallas kernels: 13.6 us -> 7.66 us  [sum_call(): pl.pallas_call(kernel, out_shape=outs, in_specs=[pl.BlockSpec(memory_spac...]
    pallas_call x4 -> x2, Pallas kernels: 14.5 us -> 8.9 us  [select_tiles(): pl.pallas_call(functools.partial(select_kernel, len(streams[0]), groups),...]
  transfers between devices with their start and end apart: 29 -> 16, of which waited for: 11 -> 11; matrix products, arithmetic and copies ran while one was open for 6% -> 2% of each run, Pallas kernels for 12% -> 6%
where the time goes in v3:
time: 166 us; the launch traced here: 164 us
  waiting for transfers between devices  122 us (73%)
  starting transfers between devices  17.8 us (11%)
  Pallas kernels  16.6 us (10%)
  local copies, waits for them, and re-layouts  6.01 us (4%)
    ppermute x12, waiting for transfers between devices, hop(): lax.ppermute(piece, 'feat', [(f, at_place(f // sides, k) * sides + f % si...  92.1 us
    all_to_all x2, waiting for transfers between devices, to_owners(): lax.all_to_all(tiles, ('tok', 'feat'), split_axis=0, concat_axis=0, axis_...  22.5 us
    all_to_all x2, starting transfers between devices, to_owners(): lax.all_to_all(tiles, ('tok', 'feat'), split_axis=0, concat_axis=0, axis_...  10.6 us
    pallas_call x2, Pallas kernels, select_tiles(): pl.pallas_call(functools.partial(select_kernel, len(streams[0]), groups),...  8.9 us
    pallas_call x2, Pallas kernels, sum_call(): pl.pallas_call(kernel, out_shape=outs, in_specs=[pl.BlockSpec(memory_spac...  7.66 us
    ppermute x2, waiting for transfers between devices, from_sides(): lax.ppermute(blocks_of(array, (side + d) % sides), 'feat', [(f, f // side...  7.38 us
    ppermute x12, starting transfers between devices, hop(): lax.ppermute(piece, 'feat', [(f, at_place(f // sides, k) * sides + f % si...  5.74 us
    unnamed x34, local copies, waits for them, and re-layouts  4.04 us
  transfers between devices with their start and end apart: 16, of which 11 were waited for; matrix products, arithmetic and copies ran while one was open for 2% of the time, Pallas kernels for 6%

profile of v3, /device:TPU:25, one launch (start us, length us, event | category | flops | bytes accessed | tf_op | source)
XLA Modules:
  0.0 164.5 jit_solution(1538691023092251271)
XLA Ops:
  0.7 1.5 dynamic-slice_bitcast_fusion
  2.2 0.1 copy.23
  2.2 1.3 collective-permute-start
  3.5 0.1 copy.24
  3.6 0.0 copy-start.1
  3.6 0.2 collective-permute-start.1
  3.8 0.1 collective-permute-start.2
  3.9 0.8 copy.21
  4.7 0.2 collective-permute-start.4
  4.9 7.4 %collective-permute-done.refs_4_ = bf16[16,96,128]{2,1,0:T(8,128)(2,1)S(1)} collective-permute-done((bf16[16,96,128]{2,1,0:T(8,128)(2,1)S(1)}, bf16[16,96,128]{2,1,0:T(8,128)(2,1)S(1)}, u32[]{:S(2)}, u32[]{:S(2)}) %collective-permute-start) | collective-permute-done | bytes 393248 | tf_op jit(solution)/shard_map/ppermute | solution.py:125
  12.3 8.6 %collective-permute-done.1.refs_1_ = bf16[16,96,128]{2,1,0:T(8,128)(2,1)S(1)} collective-permute-done((bf16[16,96,128]{2,1,0:T(8,128)(2,1)S(1)}, bf16[16,96,128]{2,1,0:T(8,128)(2,1)S(1)}, u32[]{:S(2)}, u32[]{:S(2)}) %collective-permute-start.1) | collective-permute-done | bytes 393248 | tf_op jit(solution)/shard_map/ppermute | solution.py:136
  20.9 0.0 collective-permute-start.5
  20.9 1.1 collective-permute-start.6
  22.0 0.1 reshape.27
  22.1 0.1 copy.22
  22.1 0.0 collective-permute-done.2.refs_2_
  22.2 0.5 collective-permute-start.3
  22.6 18.4 %collective-permute-done.5.refs_5_ = bf16[16,96,128]{2,1,0:T(8,128)(2,1)S(1)} collective-permute-done((bf16[16,96,128]{2,1,0:T(8,128)(2,1)S(1)}, bf16[16,96,128]{2,1,0:T(8,128)(2,1)S(1)}, u32[]{:S(2)}, u32[]{:S(2)}) %collective-permute-start.5) | collective-permute-done | bytes 393248 | tf_op jit(solution)/shard_map/ppermute | solution.py:136
  41.0 0.1 collective-permute-start.7
  41.1 0.1 copy.12
  41.2 0.1 reshape.28
  41.3 0.7 pad_add_fusion.places_ref
  42.0 0.6 fusion.3.table_ref
  42.6 6.8 %collective-permute-done.3.refs_3_ = bf16[16,96,128]{2,1,0:T(8,128)(2,1)S(1)} collective-permute-done((bf16[16,96,128]{2,1,0:T(8,128)(2,1)S(1)}, bf16[16,96,128]{2,1,0:T(8,128)(2,1)S(1)}, u32[]{:S(2)}, u32[]{:S(2)}) %collective-permute-start.3) | collective-permute-done | bytes 393248 | tf_op jit(solution)/shard_map/ppermute | solution.py:136
  49.4 8.5 %collective-permute-done.7.refs_7_ = bf16[16,96,128]{2,1,0:T(8,128)(2,1)} collective-permute-done((bf16[16,96,128]{2,1,0:T(8,128)(2,1)S(1)}, bf16[16,96,128]{2,1,0:T(8,128)(2,1)}, u32[]{:S(2)}, u32[]{:S(2)}) %collective-permute-start.7) | collective-permute-done | bytes 393248 | tf_op jit(solution)/shard_map/ppermute | solution.py:136
  58.0 4.9 %select_tiles.2 = bf16[192,96,128]{2,1,0:T(8,128)(2,1)} custom-call(s32[4]{0:T(128)} %pad_add_fusion.places_ref, s32[192]{0:T(256)} %fusion.3.table_ref, bf16[16,96,128]{2,1,0:T(8,128)(2,1)} %bitcast.47, bf16[16,96,128]{2,1,0:T(8,128)(2,1)} %copy-done.4, bf16[16,96,128]{2,1,0:T(8,128)(2,1)} %copy-done.5, bf16[16,96,128]{2,1,0:T(8,128)(2,1)} %copy-done.8, ...), custom_call_target="tpu_custom_call" | custom-call | tf_op jit(solution)/shard_map/select_tiles/pallas_call | solution.py:49
  62.9 5.1 %all-to-all-start = ((bf16[192,96,128]{2,1,0:T(8,128)(2,1)}), bf16[192,96,128]{2,1,0:T(8,128)(2,1)}, u32[]{:S(2)}, u32[]{:S(2)}) async-start(bf16[192,96,128]{2,1,0:T(8,128)(2,1)} %select_tiles.2), calls=%async_computation | async-start | bytes 9437184 | tf_op jit(solution)/shard_map/all_to_all | solution.py:170
  68.0 2.4 %collective-permute-start.12 = (bf16[16,96,128]{2,1,0:T(8,128)(2,1)}, bf16[16,96,128]{2,1,0:T(8,128)(2,1)S(1)}, u32[]{:S(2)}, u32[]{:S(2)}) collective-permute-start(bf16[16,96,128]{2,1,0:T(8,128)(2,1)} %collective-permute-done.4.refs_4_), channel_id=1, source_target_pairs={{0,4},{1,5},{2,6},{3,7},{4,0},{5,1},{6,2},{7,3},{8,12},{9,13},{10,... | collective-permute-start | bytes 1179656 | tf_op jit(solution)/shard_map/ppermute | solution.py:136
  70.3 0.1 copy.11
  70.4 0.0 collective-permute-start.8
  70.5 1.5 collective-permute-start.11
  71.9 24.1 %collective-permute-done.9.refs_2_ = bf16[16,96,128]{2,1,0:T(8,128)(2,1)S(1)} collective-permute-done((bf16[16,96,128]{2,1,0:T(8,128)(2,1)S(1)}, bf16[16,96,128]{2,1,0:T(8,128)(2,1)S(1)}, u32[]{:S(2)}, u32[]{:S(2)}) %collective-permute-start.9) | collective-permute-done | bytes 393248 | tf_op jit(solution)/shard_map/ppermute | solution.py:136
  96.0 0.0 collective-permute-start.10
  96.0 8.3 %collective-permute-done.12.refs_6_ = bf16[16,96,128]{2,1,0:T(8,128)(2,1)S(1)} collective-permute-done((bf16[16,96,128]{2,1,0:T(8,128)(2,1)}, bf16[16,96,128]{2,1,0:T(8,128)(2,1)S(1)}, u32[]{:S(2)}, u32[]{:S(2)}) %collective-permute-start.12) | collective-permute-done | bytes 393248 | tf_op jit(solution)/shard_map/ppermute | solution.py:136
  104.3 0.0 collective-permute-start.13
  104.3 0.7 slice_bitcast_fusion.table_ref
  105.0 0.0 collective-permute-done.8.refs_1_
  105.0 0.6 collective-permute-done.11.refs_5_
  105.6 8.4 %collective-permute-done.10.refs_3_ = bf16[16,96,128]{2,1,0:T(8,128)(2,1)S(1)} collective-permute-done((bf16[16,96,128]{2,1,0:T(8,128)(2,1)S(1)}, bf16[16,96,128]{2,1,0:T(8,128)(2,1)S(1)}, u32[]{:S(2)}, u32[]{:S(2)}) %collective-permute-start.10) | collective-permute-done | bytes 393248 | tf_op jit(solution)/shard_map/ppermute | solution.py:136
  114.0 8.3 %collective-permute-done.13.refs_7_ = bf16[16,96,128]{2,1,0:T(8,128)(2,1)S(1)} collective-permute-done((bf16[16,96,128]{2,1,0:T(8,128)(2,1)S(1)}, bf16[16,96,128]{2,1,0:T(8,128)(2,1)S(1)}, u32[]{:S(2)}, u32[]{:S(2)}) %collective-permute-start.13) | collective-permute-done | bytes 393248 | tf_op jit(solution)/shard_map/ppermute | solution.py:136
  122.4 0.7 copy-done.14
  123.1 4.0 %select_tiles.3 = bf16[96,96,128]{2,1,0:T(8,128)(2,1)} custom-call(s32[4]{0:T(128)} %pad_add_fusion.places_ref, s32[96]{0:T(128)} %slice_bitcast_fusion.table_ref, bf16[16,96,128]{2,1,0:T(8,128)(2,1)} %bitcast.50, bf16[16,96,128]{2,1,0:T(8,128)(2,1)} %copy-done.11, bf16[16,96,128]{2,1,0:T(8,128)(2,1)} %copy-done.9, bf16[16,96,128]{2,1,0:T(8,128)(2,1)} %copy-done.13, ...), custom_call_target="tpu_custom_call" | custom-call | tf_op jit(solution)/shard_map/select_tiles/pallas_call | solution.py:49
  127.2 0.0 all-to-all-done.tiles
  127.2 5.5 %all-to-all-start.1 = ((bf16[96,96,128]{2,1,0:T(8,128)(2,1)}), bf16[96,96,128]{2,1,0:T(8,128)(2,1)S(1)}, u32[]{:S(2)}, u32[]{:S(2)}) async-start(bf16[96,96,128]{2,1,0:T(8,128)(2,1)} %select_tiles.3), calls=%async_computation.1 | async-start | bytes 4718592 | tf_op jit(solution)/shard_map/all_to_all | solution.py:170
  132.7 5.7 %gram_sum.1 = (f32[12,128,128]{2,1,0:T(8,128)}, bf16[12,128,768]{2,1,0:T(8,128)(2,1)}) custom-call(bf16[192,96,128]{2,1,0:T(8,128)(2,1)} %all-to-all-done.tiles), custom_call_target="tpu_custom_call" | custom-call | tf_op jit(solution)/shard_map/gram_sum/pallas_call | solution.py:91
  138.4 22.5 %all-to-all-done.1.tiles = bf16[96,96,128]{2,1,0:T(8,128)(2,1)S(1)} async-done(((bf16[96,96,128]{2,1,0:T(8,128)(2,1)}), bf16[96,96,128]{2,1,0:T(8,128)(2,1)S(1)}, u32[]{:S(2)}, u32[]{:S(2)}) %all-to-all-start.1) | async-done | bytes 2359328 | tf_op jit(solution)/shard_map/all_to_all | solution.py:170
  160.9 1.7 %copy-done = bf16[12,128,768]{2,1,0:T(8,128)(2,1)S(1)} copy-done((bf16[12,128,768]{2,1,0:T(8,128)(2,1)S(1)}, bf16[12,128,768]{2,1,0:T(8,128)(2,1)}, u32[]{:S(2)}) %copy-start) | copy-done | bytes 2359320
  162.5 2.0 %cross_sum.1 = f32[12,128,128]{2,1,0:T(8,128)} custom-call(bf16[12,128,768]{2,1,0:T(8,128)(2,1)S(1)} %copy-done, bf16[96,96,128]{2,1,0:T(8,128)(2,1)S(1)} %all-to-all-done.1.tiles), custom_call_target="tpu_custom_call" | custom-call | tf_op jit(solution)/shard_map/cross_sum/pallas_call | solution.py:91
  (34 shorter events, 0.1 us)
Async XLA Ops:
  0.7 21.3 %copy-start.15 = (s32[384,2]{0,1:T(2,128)S(1)}, s32[384,2]{0,1:T(2,128)}, u32[]{:S(2)}) copy-start(s32[384,2]{0,1:T(2,128)} %param.5) | copy-start | bytes 9220
  2.2 10.0 %collective-permute-start = (bf16[16,96,128]{2,1,0:T(8,128)(2,1)S(1)}, bf16[16,96,128]{2,1,0:T(8,128)(2,1)S(1)}, u32[]{:S(2)}, u32[]{:S(2)}) collective-permute-start(bf16[16,96,128]{2,1,0:T(8,128)(2,1)S(1)} %bitcast.52), channel_id=1, source_target_pairs={{0,1},{1,0},{2,3},{3,2},{4,5},{5,4},{6,7},{7,6},{8,9},{9,8},{10,11... | collective-permute-start | bytes 1179656 | tf_op jit(solution)/shard_map/ppermute | solution.py:125
  3.6 54.4 %copy-start.1 = (bf16[12,16,8,128]{3,2,0,1:T(8,128)(2,1)}, bf16[12,16,8,128]{3,2,0,1:T(8,128)(2,1)S(1)}, u32[]{:S(2)}) copy-start(bf16[12,16,8,128]{3,2,0,1:T(8,128)(2,1)S(1)} %copy.24) | copy-start | bytes 1179652
  3.6 17.3 %collective-permute-start.1 = (bf16[16,96,128]{2,1,0:T(8,128)(2,1)S(1)}, bf16[16,96,128]{2,1,0:T(8,128)(2,1)S(1)}, u32[]{:S(2)}, u32[]{:S(2)}) collective-permute-start(bf16[16,96,128]{2,1,0:T(8,128)(2,1)S(1)} %bitcast.45), channel_id=1, source_target_pairs={{0,2},{1,3},{2,0},{3,1},{4,6},{5,7},{6,4},{7,5},{8,10},{9,11},{10,... | collective-permute-start | bytes 1179656 | tf_op jit(solution)/shard_map/ppermute | solution.py:136
  3.8 18.3 %collective-permute-start.2 = (bf16[16,96,128]{2,1,0:T(8,128)(2,1)S(1)}, bf16[16,96,128]{2,1,0:T(8,128)(2,1)S(1)}, u32[]{:S(2)}, u32[]{:S(2)}) collective-permute-start(bf16[16,96,128]{2,1,0:T(8,128)(2,1)S(1)} %bitcast.46), channel_id=1, source_target_pairs={{0,4},{1,5},{2,6},{3,7},{4,0},{5,1},{6,2},{7,3},{8,12},{9,13},{10,... | collective-permute-start | bytes 1179656 | tf_op jit(solution)/shard_map/ppermute | solution.py:136
  4.7 17.9 %collective-permute-start.4 = (bf16[16,96,128]{2,1,0:T(8,128)(2,1)}, bf16[16,96,128]{2,1,0:T(8,128)(2,1)}, u32[]{:S(2)}, u32[]{:S(2)}) collective-permute-start(bf16[16,96,128]{2,1,0:T(8,128)(2,1)} %bitcast.38), channel_id=1, source_target_pairs={{0,1},{1,0},{2,3},{3,2},{4,5},{5,4},{6,7},{7,6},{8,9},{9,8},{10,11... | collective-permute-start | bytes 1179656 | tf_op jit(solution)/shard_map/ppermute | solution.py:125
  12.3 45.7 %copy-start.3 = (bf16[16,96,128]{2,1,0:T(8,128)(2,1)}, bf16[16,96,128]{2,1,0:T(8,128)(2,1)S(1)}, u32[]{:S(2)}) copy-start(bf16[16,96,128]{2,1,0:T(8,128)(2,1)S(1)} %collective-permute-done.refs_4_) | copy-start | bytes 1179652
  20.9 37.1 %copy-start.4 = (bf16[16,96,128]{2,1,0:T(8,128)(2,1)}, bf16[16,96,128]{2,1,0:T(8,128)(2,1)S(1)}, u32[]{:S(2)}) copy-start(bf16[16,96,128]{2,1,0:T(8,128)(2,1)S(1)} %collective-permute-done.1.refs_1_) | copy-start | bytes 1179652
  20.9 20.1 %collective-permute-start.5 = (bf16[16,96,128]{2,1,0:T(8,128)(2,1)S(1)}, bf16[16,96,128]{2,1,0:T(8,128)(2,1)S(1)}, u32[]{:S(2)}, u32[]{:S(2)}) collective-permute-start(bf16[16,96,128]{2,1,0:T(8,128)(2,1)S(1)} %collective-permute-done.refs_4_), channel_id=1, source_target_pairs={{0,2},{1,3},{2,0},{3,1},{4,6},{5,7},{6,4},{7,5},{8,10},{9,11},{10,... | collective-permute-start | bytes 1179656 | tf_op jit(solution)/shard_map/ppermute | solution.py:136
  20.9 20.1 %collective-permute-start.6 = (bf16[16,96,128]{2,1,0:T(8,128)(2,1)S(1)}, bf16[16,96,128]{2,1,0:T(8,128)(2,1)S(1)}, u32[]{:S(2)}, u32[]{:S(2)}) collective-permute-start(bf16[16,96,128]{2,1,0:T(8,128)(2,1)S(1)} %collective-permute-done.refs_4_), channel_id=1, source_target_pairs={{0,4},{1,5},{2,6},{3,7},{4,0},{5,1},{6,2},{7,3},{8,12},{9,13},{10,... | collective-permute-start | bytes 1179656 | tf_op jit(solution)/shard_map/ppermute | solution.py:136
  22.1 48.3 %copy-start.2 = (bf16[12,16,8,128]{3,2,0,1:T(8,128)(2,1)}, bf16[12,16,8,128]{3,2,0,1:T(8,128)(2,1)S(1)}, u32[]{:S(2)}) copy-start(bf16[12,16,8,128]{3,2,0,1:T(8,128)(2,1)S(1)} %copy.22) | copy-start | bytes 1179652
  22.2 35.8 %copy-start.5 = (bf16[16,96,128]{2,1,0:T(8,128)(2,1)}, bf16[16,96,128]{2,1,0:T(8,128)(2,1)S(1)}, u32[]{:S(2)}) copy-start(bf16[16,96,128]{2,1,0:T(8,128)(2,1)S(1)} %collective-permute-done.2.refs_2_) | copy-start | bytes 1179652
  22.2 27.3 %collective-permute-start.3 = (bf16[16,96,128]{2,1,0:T(8,128)(2,1)S(1)}, bf16[16,96,128]{2,1,0:T(8,128)(2,1)S(1)}, u32[]{:S(2)}, u32[]{:S(2)}) collective-permute-start(bf16[16,96,128]{2,1,0:T(8,128)(2,1)S(1)} %collective-permute-done.2.refs_2_), channel_id=1, source_target_pairs={{0,2},{1,3},{2,0},{3,1},{4,6},{5,7},{6,4},{7,5},{8,10},{9,11},{10,... | collective-permute-start | bytes 1179656 | tf_op jit(solution)/shard_map/ppermute | solution.py:136
  41.0 17.0 %copy-start.6 = (bf16[16,96,128]{2,1,0:T(8,128)(2,1)}, bf16[16,96,128]{2,1,0:T(8,128)(2,1)S(1)}, u32[]{:S(2)}) copy-start(bf16[16,96,128]{2,1,0:T(8,128)(2,1)S(1)} %collective-permute-done.5.refs_5_) | copy-start | bytes 1179652
  41.0 17.0 %copy-start.7 = (bf16[16,96,128]{2,1,0:T(8,128)(2,1)}, bf16[16,96,128]{2,1,0:T(8,128)(2,1)S(1)}, u32[]{:S(2)}) copy-start(bf16[16,96,128]{2,1,0:T(8,128)(2,1)S(1)} %collective-permute-done.6.refs_6_) | copy-start | bytes 1179652
  41.0 17.0 %collective-permute-start.7 = (bf16[16,96,128]{2,1,0:T(8,128)(2,1)S(1)}, bf16[16,96,128]{2,1,0:T(8,128)(2,1)}, u32[]{:S(2)}, u32[]{:S(2)}) collective-permute-start(bf16[16,96,128]{2,1,0:T(8,128)(2,1)S(1)} %collective-permute-done.6.refs_6_), channel_id=1, source_target_pairs={{0,2},{1,3},{2,0},{3,1},{4,6},{5,7},{6,4},{7,5},{8,10},{9,11},{10,... | collective-permute-start | bytes 1179656 | tf_op jit(solution)/shard_map/ppermute | solution.py:136
  49.4 8.6 %copy-start.8 = (bf16[16,96,128]{2,1,0:T(8,128)(2,1)}, bf16[16,96,128]{2,1,0:T(8,128)(2,1)S(1)}, u32[]{:S(2)}) copy-start(bf16[16,96,128]{2,1,0:T(8,128)(2,1)S(1)} %collective-permute-done.3.refs_3_) | copy-start | bytes 1179652
  62.9 64.3 %all-to-all-start = ((bf16[192,96,128]{2,1,0:T(8,128)(2,1)}), bf16[192,96,128]{2,1,0:T(8,128)(2,1)}, u32[]{:S(2)}, u32[]{:S(2)}) async-start(bf16[192,96,128]{2,1,0:T(8,128)(2,1)} %select_tiles.2), calls=%async_computation | async-start | bytes 9437184 | tf_op jit(solution)/shard_map/all_to_all | solution.py:170
  68.0 28.0 %collective-permute-start.9 = (bf16[16,96,128]{2,1,0:T(8,128)(2,1)S(1)}, bf16[16,96,128]{2,1,0:T(8,128)(2,1)S(1)}, u32[]{:S(2)}, u32[]{:S(2)}) collective-permute-start(bf16[16,96,128]{2,1,0:T(8,128)(2,1)S(1)} %bitcast.48), channel_id=1, source_target_pairs={{0,4},{1,5},{2,6},{3,7},{4,0},{5,1},{6,2},{7,3},{8,12},{9,13},{10,... | collective-permute-start | bytes 1179656 | tf_op jit(solution)/shard_map/ppermute | solution.py:136
  68.0 36.3 %collective-permute-start.12 = (bf16[16,96,128]{2,1,0:T(8,128)(2,1)}, bf16[16,96,128]{2,1,0:T(8,128)(2,1)S(1)}, u32[]{:S(2)}, u32[]{:S(2)}) collective-permute-start(bf16[16,96,128]{2,1,0:T(8,128)(2,1)} %collective-permute-done.4.refs_4_), channel_id=1, source_target_pairs={{0,4},{1,5},{2,6},{3,7},{4,0},{5,1},{6,2},{7,3},{8,12},{9,13},{10,... | collective-permute-start | bytes 1179656 | tf_op jit(solution)/shard_map/ppermute | solution.py:136
  70.4 34.6 %collective-permute-start.8 = (bf16[16,96,128]{2,1,0:T(8,128)(2,1)S(1)}, bf16[16,96,128]{2,1,0:T(8,128)(2,1)S(1)}, u32[]{:S(2)}, u32[]{:S(2)}) collective-permute-start(bf16[16,96,128]{2,1,0:T(8,128)(2,1)S(1)} %bitcast.49), channel_id=1, source_target_pairs={{0,2},{1,3},{2,0},{3,1},{4,6},{5,7},{6,4},{7,5},{8,10},{9,11},{10,... | collective-permute-start | bytes 1179656 | tf_op jit(solution)/shard_map/ppermute | solution.py:136
  70.5 35.2 %collective-permute-start.11 = (bf16[16,96,128]{2,1,0:T(8,128)(2,1)}, bf16[16,96,128]{2,1,0:T(8,128)(2,1)S(1)}, u32[]{:S(2)}, u32[]{:S(2)}) collective-permute-start(bf16[16,96,128]{2,1,0:T(8,128)(2,1)} %collective-permute-done.4.refs_4_), channel_id=1, source_target_pairs={{0,2},{1,3},{2,0},{3,1},{4,6},{5,7},{6,4},{7,5},{8,10},{9,11},{10,... | collective-permute-start | bytes 1179656 | tf_op jit(solution)/shard_map/ppermute | solution.py:136
  96.0 26.4 %copy-start.9 = (bf16[16,96,128]{2,1,0:T(8,128)(2,1)}, bf16[16,96,128]{2,1,0:T(8,128)(2,1)S(1)}, u32[]{:S(2)}) copy-start(bf16[16,96,128]{2,1,0:T(8,128)(2,1)S(1)} %collective-permute-done.9.refs_2_) | copy-start | bytes 1179652
  96.0 18.1 %collective-permute-start.10 = (bf16[16,96,128]{2,1,0:T(8,128)(2,1)S(1)}, bf16[16,96,128]{2,1,0:T(8,128)(2,1)S(1)}, u32[]{:S(2)}, u32[]{:S(2)}) collective-permute-start(bf16[16,96,128]{2,1,0:T(8,128)(2,1)S(1)} %collective-permute-done.9.refs_2_), channel_id=1, source_target_pairs={{0,2},{1,3},{2,0},{3,1},{4,6},{5,7},{6,4},{7,5},{8,10},{9,11},{10,... | collective-permute-start | bytes 1179656 | tf_op jit(solution)/shard_map/ppermute | solution.py:136
  104.3 18.1 %copy-start.10 = (bf16[16,96,128]{2,1,0:T(8,128)(2,1)}, bf16[16,96,128]{2,1,0:T(8,128)(2,1)S(1)}, u32[]{:S(2)}) copy-start(bf16[16,96,128]{2,1,0:T(8,128)(2,1)S(1)} %collective-permute-done.12.refs_6_) | copy-start | bytes 1179652
  104.3 18.1 %collective-permute-start.13 = (bf16[16,96,128]{2,1,0:T(8,128)(2,1)S(1)}, bf16[16,96,128]{2,1,0:T(8,128)(2,1)S(1)}, u32[]{:S(2)}, u32[]{:S(2)}) collective-permute-start(bf16[16,96,128]{2,1,0:T(8,128)(2,1)S(1)} %collective-permute-done.12.refs_6_), channel_id=1, source_target_pairs={{0,2},{1,3},{2,0},{3,1},{4,6},{5,7},{6,4},{7,5},{8,10},{9,11},{10,... | collective-permute-start | bytes 1179656 | tf_op jit(solution)/shard_map/ppermute | solution.py:136
  105.0 17.4 %copy-start.11 = (bf16[16,96,128]{2,1,0:T(8,128)(2,1)}, bf16[16,96,128]{2,1,0:T(8,128)(2,1)S(1)}, u32[]{:S(2)}) copy-start(bf16[16,96,128]{2,1,0:T(8,128)(2,1)S(1)} %collective-permute-done.8.refs_1_) | copy-start | bytes 1179652
  105.6 16.8 %copy-start.12 = (bf16[16,96,128]{2,1,0:T(8,128)(2,1)}, bf16[16,96,128]{2,1,0:T(8,128)(2,1)S(1)}, u32[]{:S(2)}) copy-start(bf16[16,96,128]{2,1,0:T(8,128)(2,1)S(1)} %collective-permute-done.11.refs_5_) | copy-start | bytes 1179652
  114.0 8.3 %copy-start.13 = (bf16[16,96,128]{2,1,0:T(8,128)(2,1)}, bf16[16,96,128]{2,1,0:T(8,128)(2,1)S(1)}, u32[]{:S(2)}) copy-start(bf16[16,96,128]{2,1,0:T(8,128)(2,1)S(1)} %collective-permute-done.10.refs_3_) | copy-start | bytes 1179652
  122.4 0.7 copy-start.14
  127.2 33.7 %all-to-all-start.1 = ((bf16[96,96,128]{2,1,0:T(8,128)(2,1)}), bf16[96,96,128]{2,1,0:T(8,128)(2,1)S(1)}, u32[]{:S(2)}, u32[]{:S(2)}) async-start(bf16[96,96,128]{2,1,0:T(8,128)(2,1)} %select_tiles.3), calls=%async_computation.1 | async-start | bytes 4718592 | tf_op jit(solution)/shard_map/all_to_all | solution.py:170
  160.9 1.7 %copy-start = (bf16[12,128,768]{2,1,0:T(8,128)(2,1)S(1)}, bf16[12,128,768]{2,1,0:T(8,128)(2,1)}, u32[]{:S(2)}) copy-start(bf16[12,128,768]{2,1,0:T(8,128)(2,1)} %get-tuple-element.17.left_ref) | copy-start | bytes 7077892

commit v4 on v3

v4 whole, which is shorter than its diff:
```python
import functools

import jax
import jax.numpy as jnp
from jax import lax
from jax.experimental import pallas as pl
from jax.experimental.pallas import tpu as pltpu
from jax.sharding import PartitionSpec as P

BLK = 128
SELECT_LIMIT = 56 << 20
SUM_LIMIT = 20 << 20


def select_kernel(where, groups, outs, places_ref, table_ref, *refs):
    pieces, out_refs, (held, stage, sems, out_sems) = refs[: -4 - outs], refs[-4 - outs : -4], refs[-4:]
    per = held.shape[0] // places_ref.shape[0]
    copies = [
        pltpu.make_async_copy(
            piece, held.at[pl.ds(places_ref[k] * per + first, piece.shape[0])], sems.at[n]
        )
        for n, (piece, (k, first)) in enumerate(zip(pieces, where))
    ]
    for copy in copies:
        copy.start()
    for copy in copies:
        copy.wait()
    count = stage.shape[0] // groups
    copies = []
    for g in range(groups):

        @pl.loop(0, count, unroll=4)
        def _(i, g=g):
            stage[g * count + i] = held[table_ref[g * count + i]]

        part = pl.ds(g * count, count)
        out = out_refs[g] if outs > 1 else out_refs[0].at[part]
        copies.append(pltpu.make_async_copy(stage.at[part], out, out_sems.at[g]))
        copies[-1].start()
    for copy in copies:
        copy.wait()


def late_kernel(k, first, per, outs, places_ref, table_ref, piece, *refs):
    out_refs, (held, sem, out_sem) = refs[outs:-3], refs[-3:]
    load = pltpu.make_async_copy(piece, held, sem)
    load.start()
    blocks = held.shape[0]
    begin = places_ref[k] * per + first
    load.wait()
    sent = 0
    for g, out_ref in enumerate(out_refs):
        count = out_ref.shape[0]

        def put(i, sent, g=g, out_ref=out_ref, count=count):
            slot = table_ref[g * count + i] - begin
            mine = jnp.logical_and(slot >= 0, slot < blocks)

            @pl.when(mine)
            def _():
                pltpu.make_async_copy(held.at[slot], out_ref.at[i], out_sem).start()

            return sent + mine.astype(jnp.int32)

        sent = lax.fori_loop(0, count, put, sent)

    @pl.loop(0, sent)
    def _(i):
        pltpu.make_async_copy(held.at[0], out_refs[0].at[0], out_sem).wait()


def select_tiles(places, table, pieces, groups, apart, late=None):
    early = pieces[:-1] if late else pieces
    where, arrays = [w for w, _ in early], [array for _, array in early]
    _, rows, blk = arrays[0].shape
    dtype = arrays[0].dtype
    count = table.shape[0]
    outs = groups if apart else 1
    shapes = [jax.ShapeDtypeStruct((count // outs, rows, blk), dtype)] * outs
    total = sum(array.shape[0] for _, array in pieces)
    picked = pl.pallas_call(
        functools.partial(select_kernel, where, groups, outs),
        out_shape=shapes,
        in_specs=[pl.BlockSpec(memory_space=pltpu.SMEM)] * 2
        + [pl.BlockSpec(memory_space=pl.ANY)] * len(arrays),
        out_specs=[pl.BlockSpec(memory_space=pl.ANY)] * outs,
        scratch_shapes=[
            pltpu.VMEM((total, rows, blk), dtype),
            pltpu.VMEM((count, rows, blk), dtype),
            pltpu.SemaphoreType.DMA((len(arrays),)),
            pltpu.SemaphoreType.DMA((groups,)),
        ],
        compiler_params=pltpu.CompilerParams(vmem_limit_bytes=SELECT_LIMIT),
        name="select_tiles",
    )(places, table, *arrays)
    if not late:
        return picked
    (k, first), piece = pieces[-1]
    return pl.pallas_call(
        functools.partial(late_kernel, k, first, total // places.shape[0], outs),
        out_shape=shapes,
        in_specs=[pl.BlockSpec(memory_space=pltpu.SMEM)] * 2
        + [pl.BlockSpec(memory_space=pl.ANY)] * (1 + outs),
        out_specs=[pl.BlockSpec(memory_space=pl.ANY)] * outs,
        scratch_shapes=[
            pltpu.VMEM(piece.shape, dtype),
            pltpu.SemaphoreType.DMA,
            pltpu.SemaphoreType.DMA,
        ],
        input_output_aliases={3 + i: i for i in range(outs)},
        compiler_params=pltpu.CompilerParams(vmem_limit_bytes=SELECT_LIMIT),
        name="late_tiles",
    )(places, table, piece, *picked)


def rows_in_order(order_ref, tiles, group, which, rows):
    return jnp.concatenate(
        [tiles[order_ref[d] * group + which, rows] for d in range(order_ref.shape[0])], 0
    )


def left_kernel(chunks, order_ref, tiles, *left_refs):
    pairs = left_refs[0].shape[0]
    chunk = tiles.shape[1] // chunks

    @pl.loop(0, pairs, unroll=2)
    def _(p):
        for c, left_ref in enumerate(left_refs):
            rows = slice(c * chunk, (c + 1) * chunk)
            left_ref[p] = rows_in_order(order_ref, tiles, 2 * pairs, 2 * p, rows).T


def gram_kernel(inverse, chunks, order_ref, *refs):
    lefts, (tiles, out_ref) = refs[:chunks], refs[chunks:]
    pairs = out_ref.shape[0]
    chunk = tiles.shape[1] // chunks

    @pl.loop(0, pairs, unroll=2)
    def _(p):
        total = jnp.zeros(out_ref.shape[1:], jnp.float32)
        for c, left_ref in enumerate(lefts):
            rows = slice(c * chunk, (c + 1) * chunk)
            right = rows_in_order(order_ref, tiles, 2 * pairs, 2 * p + 1, rows)
            total += jnp.dot(left_ref[p], right, preferred_element_type=jnp.float32)
        out_ref[p] = total * inverse


def cross_kernel(inverse, parts, left_ref, *refs):
    tiles, before, out_ref = refs[:parts], refs[parts:-1], refs[-1]
    pairs = out_ref.shape[0]

    @pl.loop(0, pairs, unroll=4)
    def _(p):
        right = jnp.concatenate([ref[p] for ref in tiles], 0)
        total = jnp.dot(left_ref[p], right, preferred_element_type=jnp.float32) * inverse
        out_ref[p] = total + before[0][p] if before else total


def sum_call(kernel, operands, outs, name):
    return pl.pallas_call(
        kernel,
        out_shape=outs,
        in_specs=[
            pl.BlockSpec(memory_space=pltpu.SMEM if operand.ndim == 1 else pltpu.VMEM)
            for operand in operands
        ],
        out_specs=[pl.BlockSpec(memory_space=pltpu.VMEM)] * len(outs),
        compiler_params=pltpu.CompilerParams(vmem_limit_bytes=SUM_LIMIT),
        name=name,
    )(*operands)


def after(values, done):
    return lax.optimization_barrier((values, done))


def body(span_input, span_output, block_pairs):
    tok_count = lax.axis_size("tok")
    feat_count = lax.axis_size("feat")
    tok = lax.axis_index("tok")
    feat = lax.axis_index("feat")
    rows, width = span_input.shape
    inverse = 1.0 / (tok_count * rows)
    pairs = block_pairs.shape[0] // (tok_count * feat_count)
    own_blocks = width // BLK
    sides = 2 if feat_count % 2 == 0 and rows % 32 == 0 else 1
    line = feat_count // sides
    place, side = feat // sides, feat % sides
    part = rows // sides
    chunks = 2 if part % 32 == 0 else 1
    chunk = part // chunks
    paired = line & (line - 1) == 0

    def blocks_of(array, which):
        taken = lax.dynamic_slice_in_dim(array, which * part, part, 0)
        return taken.reshape(part, own_blocks, BLK).transpose(1, 0, 2)

    def from_sides(array):
        return [
            lax.ppermute(
                blocks_of(array, (side + d) % sides), "feat",
                [(f, f // sides * sides + (f % sides + d) % sides) for f in range(feat_count)],
            )
            for d in range(1, sides)
        ]

    def at_place(p, k):
        return p ^ k if paired else (p + k) % line

    def hop(piece, k):
        return lax.ppermute(piece, "feat", [
            (f, at_place(f // sides, k) * sides + f % sides) for f in range(feat_count)
        ])

    def far_hops(unit):
        held = {0: unit}
        if not paired:
            held.update({k: hop(unit, k) for k in range(1, line)})
            return held
        k = line // 2
        while k > 1:
            held.update({m ^ k: hop(piece, k) for m, piece in list(held.items())})
            k //= 2
        if line > 1:
            held[1] = hop(unit, 1)
        return held

    def last_hops(held):
        return {m ^ 1: hop(held[m], 1) for m in held if m > 1 and m ^ 1 not in held}

    def pieces_of(streams):
        pieces, first = [], 0
        for held in streams:
            pieces += [((k, first), held[k]) for k in range(line)]
            first += held[0].shape[0]
        return pieces

    places = jnp.stack([at_place(place, k) if paired else (place - k) % line for k in range(line)])
    places = places.astype(jnp.int32)

    owners = [(t, s) for t in range(tok_count) for s in range(sides)]
    groups = [[t * feat_count + p * sides + s for t, s in owners] for p in range(line)]
    listed = block_pairs.reshape(tok_count, line, sides * pairs, 2)
    listed = lax.dynamic_index_in_dim(listed, place, 1, keepdims=False).reshape(len(owners), pairs, 2)
    stream = (side - listed // own_blocks % sides) % sides
    slots = listed // (own_blocks * sides) * (own_blocks * sides) + stream * own_blocks + listed % own_blocks
    away = jnp.stack([
        (tok + d // sides) % tok_count * sides + (side + d) % sides for d in range(len(owners))
    ])
    right_slots = jnp.take(slots[:, :, 1], away, axis=0).reshape(-1)
    sources = jnp.stack([
        (tok - d // sides) % tok_count * sides + (side - d) % sides for d in range(len(owners))
    ]).astype(jnp.int32)

    def to_owners(tiles):
        return lax.all_to_all(
            tiles, ("tok", "feat"), split_axis=0, concat_axis=0, axis_index_groups=groups, tiled=True
        )

    def to_owner(tiles, d):
        if d == 0:
            return tiles
        perm = []
        for t, s in owners:
            to_t, to_s = (t + d // sides) % tok_count, (s + d) % sides
            perm += [
                (t * feat_count + p * sides + s, to_t * feat_count + p * sides + to_s) for p in range(line)
            ]
        return lax.ppermute(tiles, ("tok", "feat"), perm)

    own_out = blocks_of(span_output, side)
    others_in, others_out = from_sides(span_input), from_sides(span_output)
    streams_in = [far_hops(blocks_of(span_input, side))]
    if sides > 1:
        others_in, streams_in[0][1] = after(others_in, streams_in[0][1])
        streams_in += [far_hops(other) for other in others_in]
    streams_in[0].update(last_hops(streams_in[0]))
    unit = jnp.concatenate([own_out] + others_out, 0)
    units = [unit[:, c * chunk : (c + 1) * chunk] for c in range(chunks)]
    units, streams_in[-1] = after(units, streams_in[-1])
    for held in streams_in[1:]:
        held.update(last_hops(held))
    chunks_out = [far_hops(unit) for unit in units]
    (picked,) = select_tiles(places, slots.reshape(-1), pieces_of(streams_in), len(owners), False, True)
    tiles_in = to_owners(picked)
    for held in chunks_out:
        held.update(last_hops(held))

    gram_shape = jax.ShapeDtypeStruct((pairs, BLK, BLK), jnp.float32)
    left_shape = jax.ShapeDtypeStruct((pairs, BLK, len(owners) * chunk), span_input.dtype)
    lefts = sum_call(
        functools.partial(left_kernel, chunks), [sources, tiles_in], [left_shape] * chunks, "left_tiles"
    )
    cross = []
    for c, held in enumerate(chunks_out):
        final = c + 1 == chunks
        picked = select_tiles(places, right_slots, pieces_of([held]), len(owners), True, not final)
        if final:
            picked, lefts = after(picked, lefts)
        got = [to_owner(tiles, d) for d, tiles in enumerate(picked)]
        if final:
            (gram,) = sum_call(
                functools.partial(gram_kernel, inverse, chunks), [sources] + list(lefts) + [tiles_in],
                [gram_shape], "gram_sum",
            )
            cross, gram = after(list(cross), gram)
        cross = sum_call(
            functools.partial(cross_kernel, inverse, len(got)), [lefts[c]] + got + list(cross),
            [gram_shape], "cross_sum",
        )
    (cross,) = cross
    return gram, cross


def solution(mesh):
    return jax.shard_map(
        body,
        mesh=mesh,
        in_specs=(P("tok", "feat"), P("tok", "feat"), P()),
        out_specs=(P(("tok", "feat"), None, None), P(("tok", "feat"), None, None)),
        check_vma=False,
    )
```

time: 166 us -> 154 us (0.928)
  waiting for transfers between devices: 122 us -> 85 us
  starting transfers between devices: 17.8 us -> 28.6 us
  Pallas kernels: 16.6 us -> 27 us
  local copies, waits for them, and re-layouts: 6.01 us -> 8.73 us
    all_to_all x2 -> x1, waiting for transfers between devices: 22.5 us -> 0.01 us  [to_owners(): lax.all_to_all(tiles, ('tok', 'feat'), split_axis=0, concat_axis=0, axis_...]
    ppermute x12, waiting for transfers between devices: 92.1 us -> 70.6 us  [hop(): lax.ppermute(piece, 'feat', [(f, at_place(f // sides, k) * sides + f % si...]
    ppermute x0 -> x14, starting transfers between devices: none -> 16.1 us  [to_owner(): return lax.ppermute(tiles, ('tok', 'feat'), perm)]
    pallas_call x2 -> x5, Pallas kernels: 8.9 us -> 16.3 us  [the longest x3 11 us: select_tiles(): pl.pallas_call(functools.partial(select_kernel, where, groups, outs), out...]
    ppermute x0 -> x14, waiting for transfers between devices: none -> 6.35 us  [to_owner(): return lax.ppermute(tiles, ('tok', 'feat'), perm)]
    all_to_all x2 -> x1, starting transfers between devices: 10.6 us -> 5.1 us  [to_owners(): lax.all_to_all(tiles, ('tok', 'feat'), split_axis=0, concat_axis=0, axis_...]
    pallas_call x2 -> x4, Pallas kernels: 7.66 us -> 10.7 us  [sum_call(): pl.pallas_call(kernel, out_shape=outs, in_specs=[pl.BlockSpec(memory_spac...]
    unnamed x34 -> x56, local copies, waits for them, and re-layouts: 4.04 us -> 4.55 us
  transfers between devices with their start and end apart: 16 -> 29, of which waited for: 11 -> 13; matrix products, arithmetic and copies ran while one was open for 2% -> 5% of each run, Pallas kernels for 6% -> 15%
where the time goes in v4:
time: 154 us; the launch traced here: 153 us
  waiting for transfers between devices  85 us (55%)
  starting transfers between devices  28.6 us (19%)
  Pallas kernels  27 us (18%)
  local copies, waits for them, and re-layouts  8.73 us (6%)
  other arithmetic  2.35 us (2%)
    ppermute x12, waiting for transfers between devices, hop(): lax.ppermute(piece, 'feat', [(f, at_place(f // sides, k) * sides + f % si...  70.6 us
    ppermute x14, starting transfers between devices, to_owner(): return lax.ppermute(tiles, ('tok', 'feat'), perm)  16.1 us
    pallas_call x3, Pallas kernels, select_tiles(): pl.pallas_call(functools.partial(select_kernel, where, groups, outs), out...  11 us
    pallas_call x4, Pallas kernels, sum_call(): pl.pallas_call(kernel, out_shape=outs, in_specs=[pl.BlockSpec(memory_spac...  10.7 us
    ppermute x2, waiting for transfers between devices, from_sides(): lax.ppermute(blocks_of(array, (side + d) % sides), 'feat', [(f, f // side...  8.06 us
    ppermute x14, waiting for transfers between devices, to_owner(): return lax.ppermute(tiles, ('tok', 'feat'), perm)  6.35 us
    ppermute x12, starting transfers between devices, hop(): lax.ppermute(piece, 'feat', [(f, at_place(f // sides, k) * sides + f % si...  5.83 us
    pallas_call x2, Pallas kernels, select_tiles(): pl.pallas_call(functools.partial(late_kernel, k, first, total // places.s...  5.26 us
  transfers between devices with their start and end apart: 29, of which 13 were waited for; matrix products, arithmetic and copies ran while one was open for 5% of the time, Pallas kernels for 15%

profile of v4, /device:TPU:25, one launch (start us, length us, event | category | flops | bytes accessed | tf_op | source)
XLA Modules:
  0.0 152.7 jit_solution(5811488850946356326)
XLA Ops:
  0.7 1.5 dynamic-slice_bitcast_fusion
  2.3 1.3 collective-permute-start.1
  4.2 8.1 %collective-permute-done.1.refs_4_ = bf16[16,96,128]{2,1,0:T(8,128)(2,1)S(1)} collective-permute-done((bf16[16,96,128]{2,1,0:T(8,128)(2,1)S(1)}, bf16[16,96,128]{2,1,0:T(8,128)(2,1)S(1)}, u32[]{:S(2)}, u32[]{:S(2)}) %collective-permute-start.1) | collective-permute-done | bytes 393248 | tf_op jit(solution)/shard_map/ppermute | solution.py:200
  12.3 8.6 %collective-permute-done.2.refs_1_ = bf16[16,96,128]{2,1,0:T(8,128)(2,1)S(1)} collective-permute-done((bf16[16,96,128]{2,1,0:T(8,128)(2,1)S(1)}, bf16[16,96,128]{2,1,0:T(8,128)(2,1)S(1)}, u32[]{:S(2)}, u32[]{:S(2)}) %collective-permute-start.2) | collective-permute-done | bytes 393248 | tf_op jit(solution)/shard_map/ppermute | solution.py:211
  20.9 1.1 collective-permute-start.4
  22.0 0.7 reshape.381
  22.8 0.5 collective-permute-start.7
  23.2 1.1 pad_maximum_fusion
  24.3 16.7 %collective-permute-done.3.refs_5_ = bf16[16,96,128]{2,1,0:T(8,128)(2,1)S(1)} collective-permute-done((bf16[16,96,128]{2,1,0:T(8,128)(2,1)S(1)}, bf16[16,96,128]{2,1,0:T(8,128)(2,1)S(1)}, u32[]{:S(2)}, u32[]{:S(2)}) %collective-permute-start.3) | collective-permute-done | bytes 393248 | tf_op jit(solution)/shard_map/ppermute | solution.py:211
  41.1 0.8 constant_dynamic-slice_fusion
  41.9 0.7 copy.21
  42.6 0.9 reshape.382
  43.5 0.6 pad_add_fusion.places_ref
  44.1 0.6 fusion.13.table_ref
  44.7 4.9 %collective-permute-done.7.refs_3_ = bf16[16,96,128]{2,1,0:T(8,128)(2,1)} collective-permute-done((bf16[16,96,128]{2,1,0:T(8,128)(2,1)S(1)}, bf16[16,96,128]{2,1,0:T(8,128)(2,1)}, u32[]{:S(2)}, u32[]{:S(2)}) %collective-permute-start.7) | collective-permute-done | bytes 393248 | tf_op jit(solution)/shard_map/ppermute | solution.py:211
  49.6 4.8 %select_tiles.3.refs_0_ = bf16[192,96,128]{2,1,0:T(8,128)(2,1)} custom-call(s32[4]{0:T(128)} %pad_add_fusion.places_ref, s32[192]{0:T(256)} %fusion.13.table_ref, bf16[16,96,128]{2,1,0:T(8,128)(2,1)} %bitcast.74, bf16[16,96,128]{2,1,0:T(8,128)(2,1)} %copy-done.6, bf16[16,96,128]{2,1,0:T(8,128)(2,1)} %copy-done.7, ...), custom_call_target="tpu_custom_call" | custom-call | tf_op jit(solution)/shard_map/select_tiles/pallas_call | solution.py:81
  54.4 3.5 %collective-permute-done.5.piece = bf16[16,96,128]{2,1,0:T(8,128)(2,1)S(1)} collective-permute-done((bf16[16,96,128]{2,1,0:T(8,128)(2,1)S(1)}, bf16[16,96,128]{2,1,0:T(8,128)(2,1)S(1)}, u32[]{:S(2)}, u32[]{:S(2)}) %collective-permute-start.5) | collective-permute-done | bytes 393248 | tf_op jit(solution)/shard_map/ppermute | solution.py:211
  57.9 0.7 copy-done.16
  58.6 2.9 %late_tiles.2 = bf16[192,96,128]{2,1,0:T(8,128)(2,1)} custom-call(s32[4]{0:T(128)} %pad_add_fusion.places_ref, s32[192]{0:T(256)} %fusion.13.table_ref, bf16[16,96,128]{2,1,0:T(8,128)(2,1)} %copy-done.16, bf16[192,96,128]{2,1,0:T(8,128)(2,1)} %select_tiles.3.refs_0_), custom_call_target="tpu_custom_call", output_to_operand_aliasing={{}: (3, {})} | custom-call | tf_op jit(solution)/shard_map/late_tiles/pallas_call | solution.py:99
  61.5 5.1 %all-to-all-start = ((bf16[192,96,128]{2,1,0:T(8,128)(2,1)}), bf16[192,96,128]{2,1,0:T(8,128)(2,1)}, u32[]{:S(2)}, u32[]{:S(2)}) async-start(bf16[192,96,128]{2,1,0:T(8,128)(2,1)} %late_tiles.2), calls=%async_computation | async-start | bytes 9437184 | tf_op jit(solution)/shard_map/all_to_all | solution.py:256
  67.0 2.4 %collective-permute-start.19 = (bf16[32,48,128]{2,1,0:T(8,128)(2,1)S(1)}, bf16[32,48,128]{2,1,0:T(8,128)(2,1)S(1)}, u32[]{:S(2)}, u32[]{:S(2)}) collective-permute-start(bf16[32,48,128]{2,1,0:T(8,128)(2,1)S(1)} %get-tuple-element.70.refs_0_), channel_id=1, source_target_pairs={{0,4},{1,5},{2,6},{3,7},{4,0},{5,1},{6,2},{7,3},{8,12},{9,13},{10,... | collective-permute-start | bytes 1179656 | tf_op jit(solution)/shard_map/ppermute | solution.py:211
  69.4 1.5 collective-permute-start.18
  70.9 24.2 %collective-permute-done.8.refs_2_ = bf16[32,48,128]{2,1,0:T(8,128)(2,1)S(1)} collective-permute-done((bf16[32,48,128]{2,1,0:T(8,128)(2,1)S(1)}, bf16[32,48,128]{2,1,0:T(8,128)(2,1)S(1)}, u32[]{:S(2)}, u32[]{:S(2)}) %collective-permute-start.8) | collective-permute-done | bytes 393248 | tf_op jit(solution)/shard_map/ppermute | solution.py:211
  95.1 8.3 %collective-permute-done.19.refs_2_ = bf16[32,48,128]{2,1,0:T(8,128)(2,1)S(1)} collective-permute-done((bf16[32,48,128]{2,1,0:T(8,128)(2,1)S(1)}, bf16[32,48,128]{2,1,0:T(8,128)(2,1)S(1)}, u32[]{:S(2)}, u32[]{:S(2)}) %collective-permute-start.19) | collective-permute-done | bytes 393248 | tf_op jit(solution)/shard_map/ppermute | solution.py:211
  103.4 0.6 gather_fusion
  104.0 0.6 select_n.236.table_ref
  104.7 0.7 copy-done.15
  105.4 3.1 %select_tiles.4 = (bf16[12,48,128]{2,1,0:T(8,128)(2,1)}, bf16[12,48,128]{2,1,0:T(8,128)(2,1)}, bf16[12,48,128]{2,1,0:T(8,128)(2,1)}, bf16[12,48,128]{2,1,0:T(8,1...) custom-call(s32[4]{0:T(128)} %pad_add_fusion.places_ref, ...), custom_call_target="tpu_custom_call" | custom-call | tf_op jit(solution)/shard_map/select_tiles/pallas_call | solution.py:81
  108.5 4.5 %collective-permute-done.9.piece = bf16[32,48,128]{2,1,0:T(8,128)(2,1)S(1)} collective-permute-done((bf16[32,48,128]{2,1,0:T(8,128)(2,1)S(1)}, bf16[32,48,128]{2,1,0:T(8,128)(2,1)S(1)}, u32[]{:S(2)}, u32[]{:S(2)}) %collective-permute-start.9) | collective-permute-done | bytes 393248 | tf_op jit(solution)/shard_map/ppermute | solution.py:211
  113.0 0.7 copy-done.14
  113.7 2.4 %late_tiles.3 = (bf16[12,48,128]{2,1,0:T(8,128)(2,1)}, bf16[12,48,128]{2,1,0:T(8,128)(2,1)}, bf16[12,48,128]{2,1,0:T(8,128)(2,1)}, bf16[12,48,128]{2,1,0:T(8,128...) custom-call(s32[4]{0:T(128)} %pad_add_fusion.places_ref, ...), custom_call_target="tpu_custom_call", output_to_operand_aliasing={{0}: (3, {}), {1}: (4, {}), {2}: (5, {}), {3}: (6, {}), {4}... | custom-call | tf_op jit(solution)/shard_map/late_tiles/pallas_call | solution.py:99
  116.1 1.3 collective-permute-start.11
  117.5 4.5 %collective-permute-start.12 = (bf16[12,48,128]{2,1,0:T(8,128)(2,1)}, bf16[12,48,128]{2,1,0:T(8,128)(2,1)S(1)}, u32[]{:S(2)}, u32[]{:S(2)}) collective-permute-start(bf16[12,48,128]{2,1,0:T(8,128)(2,1)} %get-tuple-element.64), channel_id=1, source_target_pairs={{0,8},{2,10},{4,12},{6,14},{1,9},{3,11},{5,13},{7,15},{8,16},{10,1... | collective-permute-start | bytes 442376 | tf_op jit(solution)/shard_map/ppermute | solution.py:269
  122.5 2.0 %collective-permute-start.15 = (bf16[12,48,128]{2,1,0:T(8,128)(2,1)}, bf16[12,48,128]{2,1,0:T(8,128)(2,1)S(1)}, u32[]{:S(2)}, u32[]{:S(2)}) collective-permute-start(bf16[12,48,128]{2,1,0:T(8,128)(2,1)} %get-tuple-element.67), channel_id=1, source_target_pairs={{0,17},{2,19},{4,21},{6,23},{1,16},{3,18},{5,20},{7,22},{8,25},{10... | collective-permute-start | bytes 442376 | tf_op jit(solution)/shard_map/ppermute | solution.py:269
  124.5 3.2 %select_tiles.5 = (bf16[12,48,128]{2,1,0:T(8,128)(2,1)}, bf16[12,48,128]{2,1,0:T(8,128)(2,1)}, bf16[12,48,128]{2,1,0:T(8,128)(2,1)}, bf16[12,48,128]{2,1,0:T(8,1...) custom-call(s32[4]{0:T(128)} %pad_add_fusion.places_ref, ...), custom_call_target="tpu_custom_call" | custom-call | tf_op jit(solution)/shard_map/select_tiles/pallas_call | solution.py:81
  127.8 3.4 %left_tiles.1 = (bf16[12,128,384]{2,1,0:T(8,128)(2,1)S(1)}, bf16[12,128,384]{2,1,0:T(8,128)(2,1)S(1)}) custom-call(s32[8]{0:T(128)S(1)} %stack.93.order_ref, bf16[192,96,128]{2,1,0:T(8,128)(2,1)} %all-to-all-done.tiles.refs_2_), custom_call_target="tpu_custom_call" | custom-call | tf_op jit(solution)/shard_map/left_tiles/pallas_call | solution.py:160
  131.2 1.3 collective-permute-start.16
  132.8 1.2 collective-permute-start.21
  134.0 1.8 %collective-permute-start.22 = (bf16[12,48,128]{2,1,0:T(8,128)(2,1)S(1)}, bf16[12,48,128]{2,1,0:T(8,128)(2,1)S(1)}, u32[]{:S(2)}, u32[]{:S(2)}) collective-permute-start(bf16[12,48,128]{2,1,0:T(8,128)(2,1)S(1)} %copy-done.25), channel_id=1, source_target_pairs={{0,8},{2,10},{4,12},{6,14},{1,9},{3,11},{5,13},{7,15},{8,16},{10,1... | collective-permute-start | bytes 442376 | tf_op jit(solution)/shard_map/ppermute | solution.py:269
  136.2 0.8 collective-permute-start.24
  137.0 2.7 %collective-permute-done.17.refs_7_ = bf16[12,48,128]{2,1,0:T(8,128)(2,1)S(1)} collective-permute-done((bf16[12,48,128]{2,1,0:T(8,128)(2,1)S(1)}, bf16[12,48,128]{2,1,0:T(8,128)(2,1)S(1)}, u32[]{:S(2)}, u32[]{:S(2)}) %collective-permute-start.17) | collective-permute-done | bytes 147488 | tf_op jit(solution)/shard_map/ppermute | solution.py:269
  140.0 0.9 collective-permute-done.21.refs_1_
  140.9 1.7 %collective-permute-start.26 = (bf16[12,48,128]{2,1,0:T(8,128)(2,1)S(1)}, bf16[12,48,128]{2,1,0:T(8,128)(2,1)S(1)}, u32[]{:S(2)}, u32[]{:S(2)}) collective-permute-start(bf16[12,48,128]{2,1,0:T(8,128)(2,1)S(1)} %copy-done.21), channel_id=1, source_target_pairs={{0,24},{2,26},{4,28},{6,30},{1,25},{3,27},{5,29},{7,31},{8,0},{10,... | collective-permute-start | bytes 442376 | tf_op jit(solution)/shard_map/ppermute | solution.py:269
  142.9 4.8 %gram_sum.1 = f32[12,128,128]{2,1,0:T(8,128)} custom-call(s32[8]{0:T(128)S(1)} %stack.93.order_ref, bf16[12,128,384]{2,1,0:T(8,128)(2,1)S(1)} %get-tuple-element.80.left_ref.refs_0_, bf16[12,128,384]{2,1,0:T(8,128)(2,1)S(1)} %get-tuple-element.81.refs_1_.left_ref, bf16[192,96,128]{2,1,0:T(8,128)(2,1)} %all-to-all-done.tiles.refs_2_), custom_call_target="tpu_custom_call" | custom-call | tf_op jit(solution)/shard_map/gram_sum/pallas_call | solution.py:160
  147.7 0.8 cross_sum.2.refs_8_
  148.5 1.5 collective-permute-done.26.refs_6_
  150.0 1.0 collective-permute-done.27.refs_7_
  151.0 1.7 %cross_sum.3 = f32[12,128,128]{2,1,0:T(8,128)} custom-call(bf16[12,128,384]{2,1,0:T(8,128)(2,1)S(1)} %get-tuple-element.81.refs_1_.left_ref, bf16[12,48,128]{2,1,0:T(8,128)(2,1)S(1)} %copy-done.1, bf16[12,48,128]{2,1,0:T(8,128)(2,1)S(1)} %collective-permute-done.21.refs_1_, bf16[12,48,128]{2,1,0:T(8,128)(2,1)S(1)} %collective-permute-done.22.refs_2_, ...), custom_call_target="tpu_custom_call" | custom-call | tf_op jit(solution)/shard_map/cross_sum/pallas_call | solution.py:160
  (98 shorter events, 3.2 us)
Async XLA Ops:
  0.6 21.3 %copy-start.19 = (s32[384,2]{0,1:T(2,128)S(1)}, s32[384,2]{0,1:T(2,128)}, u32[]{:S(2)}) copy-start(s32[384,2]{0,1:T(2,128)} %param.5) | copy-start | bytes 9220
  2.3 10.0 %collective-permute-start.1 = (bf16[16,96,128]{2,1,0:T(8,128)(2,1)S(1)}, bf16[16,96,128]{2,1,0:T(8,128)(2,1)S(1)}, u32[]{:S(2)}, u32[]{:S(2)}) collective-permute-start(bf16[16,96,128]{2,1,0:T(8,128)(2,1)S(1)} %bitcast.77), channel_id=1, source_target_pairs={{0,1},{1,0},{2,3},{3,2},{4,5},{5,4},{6,7},{7,6},{8,9},{9,8},{10,11... | collective-permute-start | bytes 1179656 | tf_op jit(solution)/shard_map/ppermute | solution.py:200
  3.6 45.9 %copy-start.2 = (bf16[12,16,8,128]{3,2,0,1:T(8,128)(2,1)}, bf16[12,16,8,128]{3,2,0,1:T(8,128)(2,1)S(1)}, u32[]{:S(2)}) copy-start(bf16[12,16,8,128]{3,2,0,1:T(8,128)(2,1)S(1)} %copy.31) | copy-start | bytes 1179652
  3.6 17.3 %collective-permute-start.2 = (bf16[16,96,128]{2,1,0:T(8,128)(2,1)S(1)}, bf16[16,96,128]{2,1,0:T(8,128)(2,1)S(1)}, u32[]{:S(2)}, u32[]{:S(2)}) collective-permute-start(bf16[16,96,128]{2,1,0:T(8,128)(2,1)S(1)} %bitcast.72), channel_id=1, source_target_pairs={{0,2},{1,3},{2,0},{3,1},{4,6},{5,7},{6,4},{7,5},{8,10},{9,11},{10,... | collective-permute-start | bytes 1179656 | tf_op jit(solution)/shard_map/ppermute | solution.py:211
  3.8 18.9 %collective-permute-start.6 = (bf16[16,96,128]{2,1,0:T(8,128)(2,1)S(1)}, bf16[16,96,128]{2,1,0:T(8,128)(2,1)S(1)}, u32[]{:S(2)}, u32[]{:S(2)}) collective-permute-start(bf16[16,96,128]{2,1,0:T(8,128)(2,1)S(1)} %bitcast.73), channel_id=1, source_target_pairs={{0,4},{1,5},{2,6},{3,7},{4,0},{5,1},{6,2},{7,3},{8,12},{9,13},{10,... | collective-permute-start | bytes 1179656 | tf_op jit(solution)/shard_map/ppermute | solution.py:211
  4.0 19.2 %collective-permute-start = (bf16[16,96,128]{2,1,0:T(8,128)(2,1)S(1)}, bf16[16,96,128]{2,1,0:T(8,128)(2,1)}, u32[]{:S(2)}, u32[]{:S(2)}) collective-permute-start(bf16[16,96,128]{2,1,0:T(8,128)(2,1)S(1)} %bitcast.76), channel_id=1, source_target_pairs={{0,1},{1,0},{2,3},{3,2},{4,5},{5,4},{6,7},{7,6},{8,9},{9,8},{10,11... | collective-permute-start | bytes 1179656 | tf_op jit(solution)/shard_map/ppermute | solution.py:200
  12.3 37.2 %copy-start.5 = (bf16[16,96,128]{2,1,0:T(8,128)(2,1)}, bf16[16,96,128]{2,1,0:T(8,128)(2,1)S(1)}, u32[]{:S(2)}) copy-start(bf16[16,96,128]{2,1,0:T(8,128)(2,1)S(1)} %collective-permute-done.1.refs_4_) | copy-start | bytes 1179652
  20.9 28.7 %copy-start.6 = (bf16[16,96,128]{2,1,0:T(8,128)(2,1)}, bf16[16,96,128]{2,1,0:T(8,128)(2,1)S(1)}, u32[]{:S(2)}) copy-start(bf16[16,96,128]{2,1,0:T(8,128)(2,1)S(1)} %collective-permute-done.2.refs_1_) | copy-start | bytes 1179652
  20.9 20.1 %collective-permute-start.3 = (bf16[16,96,128]{2,1,0:T(8,128)(2,1)S(1)}, bf16[16,96,128]{2,1,0:T(8,128)(2,1)S(1)}, u32[]{:S(2)}, u32[]{:S(2)}) collective-permute-start(bf16[16,96,128]{2,1,0:T(8,128)(2,1)S(1)} %collective-permute-done.1.refs_4_), channel_id=1, source_target_pairs={{0,2},{1,3},{2,0},{3,1},{4,6},{5,7},{6,4},{7,5},{8,10},{9,11},{10,... | collective-permute-start | bytes 1179656 | tf_op jit(solution)/shard_map/ppermute | solution.py:211
  20.9 20.1 %collective-permute-start.4 = (bf16[16,96,128]{2,1,0:T(8,128)(2,1)S(1)}, bf16[16,96,128]{2,1,0:T(8,128)(2,1)S(1)}, u32[]{:S(2)}, u32[]{:S(2)}) collective-permute-start(bf16[16,96,128]{2,1,0:T(8,128)(2,1)S(1)} %collective-permute-done.1.refs_4_), channel_id=1, source_target_pairs={{0,4},{1,5},{2,6},{3,7},{4,0},{5,1},{6,2},{7,3},{8,12},{9,13},{10,... | collective-permute-start | bytes 1179656 | tf_op jit(solution)/shard_map/ppermute | solution.py:211
  22.7 26.8 %copy-start.7 = (bf16[16,96,128]{2,1,0:T(8,128)(2,1)}, bf16[16,96,128]{2,1,0:T(8,128)(2,1)S(1)}, u32[]{:S(2)}) copy-start(bf16[16,96,128]{2,1,0:T(8,128)(2,1)S(1)} %collective-permute-done.6.refs_2_) | copy-start | bytes 1179652
  22.8 26.8 %collective-permute-start.7 = (bf16[16,96,128]{2,1,0:T(8,128)(2,1)S(1)}, bf16[16,96,128]{2,1,0:T(8,128)(2,1)}, u32[]{:S(2)}, u32[]{:S(2)}) collective-permute-start(bf16[16,96,128]{2,1,0:T(8,128)(2,1)S(1)} %collective-permute-done.6.refs_2_), channel_id=1, source_target_pairs={{0,2},{1,3},{2,0},{3,1},{4,6},{5,7},{6,4},{7,5},{8,10},{9,11},{10,... | collective-permute-start | bytes 1179656 | tf_op jit(solution)/shard_map/ppermute | solution.py:211
  24.3 45.1 %copy-start.4 = (bf16[32,48,128]{2,1,0:T(8,128)(2,1)}, bf16[32,48,128]{2,1,0:T(8,128)(2,1)S(1)}, u32[]{:S(2)}) copy-start(bf16[32,48,128]{2,1,0:T(8,128)(2,1)S(1)} %get-tuple-element.53.refs_0_) | copy-start | bytes 1179652
  24.3 45.1 %copy-start.3 = (bf16[32,48,128]{2,1,0:T(8,128)(2,1)}, bf16[32,48,128]{2,1,0:T(8,128)(2,1)S(1)}, u32[]{:S(2)}) copy-start(bf16[32,48,128]{2,1,0:T(8,128)(2,1)S(1)} %get-tuple-element.70.refs_0_) | copy-start | bytes 1179652
  41.0 8.6 %copy-start.8 = (bf16[16,96,128]{2,1,0:T(8,128)(2,1)}, bf16[16,96,128]{2,1,0:T(8,128)(2,1)S(1)}, u32[]{:S(2)}) copy-start(bf16[16,96,128]{2,1,0:T(8,128)(2,1)S(1)} %collective-permute-done.3.refs_5_) | copy-start | bytes 1179652
  41.0 8.6 %copy-start.9 = (bf16[16,96,128]{2,1,0:T(8,128)(2,1)}, bf16[16,96,128]{2,1,0:T(8,128)(2,1)S(1)}, u32[]{:S(2)}) copy-start(bf16[16,96,128]{2,1,0:T(8,128)(2,1)S(1)} %collective-permute-done.4.refs_6_) | copy-start | bytes 1179652
  41.0 16.8 %collective-permute-start.5 = (bf16[16,96,128]{2,1,0:T(8,128)(2,1)S(1)}, bf16[16,96,128]{2,1,0:T(8,128)(2,1)S(1)}, u32[]{:S(2)}, u32[]{:S(2)}) collective-permute-start(bf16[16,96,128]{2,1,0:T(8,128)(2,1)S(1)} %collective-permute-done.4.refs_6_), channel_id=1, source_target_pairs={{0,2},{1,3},{2,0},{3,1},{4,6},{5,7},{6,4},{7,5},{8,10},{9,11},{10,... | collective-permute-start | bytes 1179656 | tf_op jit(solution)/shard_map/ppermute | solution.py:211
  61.5 66.3 %all-to-all-start = ((bf16[192,96,128]{2,1,0:T(8,128)(2,1)}), bf16[192,96,128]{2,1,0:T(8,128)(2,1)}, u32[]{:S(2)}, u32[]{:S(2)}) async-start(bf16[192,96,128]{2,1,0:T(8,128)(2,1)} %late_tiles.2), calls=%async_computation | async-start | bytes 9437184 | tf_op jit(solution)/shard_map/all_to_all | solution.py:256
  66.9 28.2 %collective-permute-start.8 = (bf16[32,48,128]{2,1,0:T(8,128)(2,1)S(1)}, bf16[32,48,128]{2,1,0:T(8,128)(2,1)S(1)}, u32[]{:S(2)}, u32[]{:S(2)}) collective-permute-start(bf16[32,48,128]{2,1,0:T(8,128)(2,1)S(1)} %get-tuple-element.53.refs_0_), channel_id=1, source_target_pairs={{0,4},{1,5},{2,6},{3,7},{4,0},{5,1},{6,2},{7,3},{8,12},{9,13},{10,... | collective-permute-start | bytes 1179656 | tf_op jit(solution)/shard_map/ppermute | solution.py:211
  67.0 36.4 %collective-permute-start.19 = (bf16[32,48,128]{2,1,0:T(8,128)(2,1)S(1)}, bf16[32,48,128]{2,1,0:T(8,128)(2,1)S(1)}, u32[]{:S(2)}, u32[]{:S(2)}) collective-permute-start(bf16[32,48,128]{2,1,0:T(8,128)(2,1)S(1)} %get-tuple-element.70.refs_0_), channel_id=1, source_target_pairs={{0,4},{1,5},{2,6},{3,7},{4,0},{5,1},{6,2},{7,3},{8,12},{9,13},{10,... | collective-permute-start | bytes 1179656 | tf_op jit(solution)/shard_map/ppermute | solution.py:211
  69.4 35.2 %collective-permute-start.10 = (bf16[32,48,128]{2,1,0:T(8,128)(2,1)S(1)}, bf16[32,48,128]{2,1,0:T(8,128)(2,1)S(1)}, u32[]{:S(2)}, u32[]{:S(2)}) collective-permute-start(bf16[32,48,128]{2,1,0:T(8,128)(2,1)S(1)} %get-tuple-element.53.refs_0_), channel_id=1, source_target_pairs={{0,2},{1,3},{2,0},{3,1},{4,6},{5,7},{6,4},{7,5},{8,10},{9,11},{10,... | collective-permute-start | bytes 1179656 | tf_op jit(solution)/shard_map/ppermute | solution.py:211
  69.4 52.6 %collective-permute-start.18 = (bf16[32,48,128]{2,1,0:T(8,128)(2,1)S(1)}, bf16[32,48,128]{2,1,0:T(8,128)(2,1)S(1)}, u32[]{:S(2)}, u32[]{:S(2)}) collective-permute-start(bf16[32,48,128]{2,1,0:T(8,128)(2,1)S(1)} %get-tuple-element.70.refs_0_), channel_id=1, source_target_pairs={{0,2},{1,3},{2,0},{3,1},{4,6},{5,7},{6,4},{7,5},{8,10},{9,11},{10,... | collective-permute-start | bytes 1179656 | tf_op jit(solution)/shard_map/ppermute | solution.py:211
  95.1 9.6 %copy-start.13 = (bf16[32,48,128]{2,1,0:T(8,128)(2,1)}, bf16[32,48,128]{2,1,0:T(8,128)(2,1)S(1)}, u32[]{:S(2)}) copy-start(bf16[32,48,128]{2,1,0:T(8,128)(2,1)S(1)} %collective-permute-done.8.refs_2_) | copy-start | bytes 1179652
  95.1 17.9 %collective-permute-start.9 = (bf16[32,48,128]{2,1,0:T(8,128)(2,1)S(1)}, bf16[32,48,128]{2,1,0:T(8,128)(2,1)S(1)}, u32[]{:S(2)}, u32[]{:S(2)}) collective-permute-start(bf16[32,48,128]{2,1,0:T(8,128)(2,1)S(1)} %collective-permute-done.8.refs_2_), channel_id=1, source_target_pairs={{0,2},{1,3},{2,0},{3,1},{4,6},{5,7},{6,4},{7,5},{8,10},{9,11},{10,... | collective-permute-start | bytes 1179656 | tf_op jit(solution)/shard_map/ppermute | solution.py:211
  103.4 21.1 %copy-start.10 = (bf16[32,48,128]{2,1,0:T(8,128)(2,1)}, bf16[32,48,128]{2,1,0:T(8,128)(2,1)S(1)}, u32[]{:S(2)}) copy-start(bf16[32,48,128]{2,1,0:T(8,128)(2,1)S(1)} %collective-permute-done.19.refs_2_) | copy-start | bytes 1179652
  103.4 19.1 %collective-permute-start.20 = (bf16[32,48,128]{2,1,0:T(8,128)(2,1)S(1)}, bf16[32,48,128]{2,1,0:T(8,128)(2,1)S(1)}, u32[]{:S(2)}, u32[]{:S(2)}) collective-permute-start(bf16[32,48,128]{2,1,0:T(8,128)(2,1)S(1)} %collective-permute-done.19.refs_2_), channel_id=1, source_target_pairs={{0,2},{1,3},{2,0},{3,1},{4,6},{5,7},{6,4},{7,5},{8,10},{9,11},{10,... | collective-permute-start | bytes 1179656 | tf_op jit(solution)/shard_map/ppermute | solution.py:211
  116.1 15.1 %copy-start.17 = (bf16[12,48,128]{2,1,0:T(8,128)(2,1)S(1)}, bf16[12,48,128]{2,1,0:T(8,128)(2,1)}, u32[]{:S(2)}) copy-start(bf16[12,48,128]{2,1,0:T(8,128)(2,1)} %get-tuple-element.68) | copy-start | bytes 442372
  116.1 16.4 %copy-start.18 = (bf16[12,48,128]{2,1,0:T(8,128)(2,1)S(1)}, bf16[12,48,128]{2,1,0:T(8,128)(2,1)}, u32[]{:S(2)}) copy-start(bf16[12,48,128]{2,1,0:T(8,128)(2,1)} %get-tuple-element.69) | copy-start | bytes 442372
  116.1 15.1 %collective-permute-start.11 = (bf16[12,48,128]{2,1,0:T(8,128)(2,1)}, bf16[12,48,128]{2,1,0:T(8,128)(2,1)S(1)}, u32[]{:S(2)}, u32[]{:S(2)}) collective-permute-start(bf16[12,48,128]{2,1,0:T(8,128)(2,1)} %get-tuple-element.63), channel_id=1, source_target_pairs={{0,1},{2,3},{4,5},{6,7},{1,0},{3,2},{5,4},{7,6},{8,9},{10,11},{12,... | collective-permute-start | bytes 442376 | tf_op jit(solution)/shard_map/ppermute | solution.py:269
  117.5 15.0 %collective-permute-start.12 = (bf16[12,48,128]{2,1,0:T(8,128)(2,1)}, bf16[12,48,128]{2,1,0:T(8,128)(2,1)S(1)}, u32[]{:S(2)}, u32[]{:S(2)}) collective-permute-start(bf16[12,48,128]{2,1,0:T(8,128)(2,1)} %get-tuple-element.64), channel_id=1, source_target_pairs={{0,8},{2,10},{4,12},{6,14},{1,9},{3,11},{5,13},{7,15},{8,16},{10,1... | collective-permute-start | bytes 442376 | tf_op jit(solution)/shard_map/ppermute | solution.py:269
  122.0 10.8 %collective-permute-start.13 = (bf16[12,48,128]{2,1,0:T(8,128)(2,1)}, bf16[12,48,128]{2,1,0:T(8,128)(2,1)S(1)}, u32[]{:S(2)}, u32[]{:S(2)}) collective-permute-start(bf16[12,48,128]{2,1,0:T(8,128)(2,1)} %get-tuple-element.65), channel_id=1, source_target_pairs={{0,9},{2,11},{4,13},{6,15},{1,8},{3,10},{5,12},{7,14},{8,17},{10,1... | collective-permute-start | bytes 442376 | tf_op jit(solution)/shard_map/ppermute | solution.py:269
  122.0 12.0 %collective-permute-start.14 = (bf16[12,48,128]{2,1,0:T(8,128)(2,1)}, bf16[12,48,128]{2,1,0:T(8,128)(2,1)S(1)}, u32[]{:S(2)}, u32[]{:S(2)}) collective-permute-start(bf16[12,48,128]{2,1,0:T(8,128)(2,1)} %get-tuple-element.66), channel_id=1, source_target_pairs={{0,16},{2,18},{4,20},{6,22},{1,17},{3,19},{5,21},{7,23},{8,24},{10... | collective-permute-start | bytes 442376 | tf_op jit(solution)/shard_map/ppermute | solution.py:269
  122.5 13.3 %collective-permute-start.15 = (bf16[12,48,128]{2,1,0:T(8,128)(2,1)}, bf16[12,48,128]{2,1,0:T(8,128)(2,1)S(1)}, u32[]{:S(2)}, u32[]{:S(2)}) collective-permute-start(bf16[12,48,128]{2,1,0:T(8,128)(2,1)} %get-tuple-element.67), channel_id=1, source_target_pairs={{0,17},{2,19},{4,21},{6,23},{1,16},{3,18},{5,20},{7,22},{8,25},{10... | collective-permute-start | bytes 442376 | tf_op jit(solution)/shard_map/ppermute | solution.py:269
  127.7 8.4 %copy-start.23 = (bf16[12,48,128]{2,1,0:T(8,128)(2,1)S(1)}, bf16[12,48,128]{2,1,0:T(8,128)(2,1)}, u32[]{:S(2)}) copy-start(bf16[12,48,128]{2,1,0:T(8,128)(2,1)} %get-tuple-element.87) | copy-start | bytes 442372
  127.7 11.9 %copy-start.22 = (bf16[12,48,128]{2,1,0:T(8,128)(2,1)S(1)}, bf16[12,48,128]{2,1,0:T(8,128)(2,1)}, u32[]{:S(2)}) copy-start(bf16[12,48,128]{2,1,0:T(8,128)(2,1)} %get-tuple-element.88) | copy-start | bytes 442372
  127.8 13.1 %copy-start.21 = (bf16[12,48,128]{2,1,0:T(8,128)(2,1)S(1)}, bf16[12,48,128]{2,1,0:T(8,128)(2,1)}, u32[]{:S(2)}) copy-start(bf16[12,48,128]{2,1,0:T(8,128)(2,1)} %get-tuple-element.89) | copy-start | bytes 442372
  127.8 14.8 %copy-start.20 = (bf16[12,48,128]{2,1,0:T(8,128)(2,1)S(1)}, bf16[12,48,128]{2,1,0:T(8,128)(2,1)}, u32[]{:S(2)}) copy-start(bf16[12,48,128]{2,1,0:T(8,128)(2,1)} %get-tuple-element.90) | copy-start | bytes 442372
  131.2 16.5 %copy-start = (bf16[12,48,128]{2,1,0:T(8,128)(2,1)S(1)}, bf16[12,48,128]{2,1,0:T(8,128)(2,1)}, u32[]{:S(2)}) copy-start(bf16[12,48,128]{2,1,0:T(8,128)(2,1)} %get-tuple-element.62.refs_0_) | copy-start | bytes 442372
  131.2 4.9 %collective-permute-start.16 = (bf16[12,48,128]{2,1,0:T(8,128)(2,1)S(1)}, bf16[12,48,128]{2,1,0:T(8,128)(2,1)S(1)}, u32[]{:S(2)}, u32[]{:S(2)}) collective-permute-start(bf16[12,48,128]{2,1,0:T(8,128)(2,1)S(1)} %copy-done.17), channel_id=1, source_target_pairs={{0,24},{2,26},{4,28},{6,30},{1,25},{3,27},{5,29},{7,31},{8,0},{10,... | collective-permute-start | bytes 442376 | tf_op jit(solution)/shard_map/ppermute | solution.py:269
  132.5 18.5 %copy-start.1 = (bf16[12,48,128]{2,1,0:T(8,128)(2,1)S(1)}, bf16[12,48,128]{2,1,0:T(8,128)(2,1)}, u32[]{:S(2)}) copy-start(bf16[12,48,128]{2,1,0:T(8,128)(2,1)} %get-tuple-element.83.refs_0_) | copy-start | bytes 442372
  132.5 7.1 %collective-permute-start.17 = (bf16[12,48,128]{2,1,0:T(8,128)(2,1)S(1)}, bf16[12,48,128]{2,1,0:T(8,128)(2,1)S(1)}, u32[]{:S(2)}, u32[]{:S(2)}) collective-permute-start(bf16[12,48,128]{2,1,0:T(8,128)(2,1)S(1)} %copy-done.18), channel_id=1, source_target_pairs={{0,25},{2,27},{4,29},{6,31},{1,24},{3,26},{5,28},{7,30},{8,1},{10,... | collective-permute-start | bytes 442376 | tf_op jit(solution)/shard_map/ppermute | solution.py:269
  132.8 8.1 %collective-permute-start.21 = (bf16[12,48,128]{2,1,0:T(8,128)(2,1)S(1)}, bf16[12,48,128]{2,1,0:T(8,128)(2,1)S(1)}, u32[]{:S(2)}, u32[]{:S(2)}) collective-permute-start(bf16[12,48,128]{2,1,0:T(8,128)(2,1)S(1)} %copy-done.26), channel_id=1, source_target_pairs={{0,1},{2,3},{4,5},{6,7},{1,0},{3,2},{5,4},{7,6},{8,9},{10,11},{12,... | collective-permute-start | bytes 442376 | tf_op jit(solution)/shard_map/ppermute | solution.py:269
  134.0 8.6 %collective-permute-start.22 = (bf16[12,48,128]{2,1,0:T(8,128)(2,1)S(1)}, bf16[12,48,128]{2,1,0:T(8,128)(2,1)S(1)}, u32[]{:S(2)}, u32[]{:S(2)}) collective-permute-start(bf16[12,48,128]{2,1,0:T(8,128)(2,1)S(1)} %copy-done.25), channel_id=1, source_target_pairs={{0,8},{2,10},{4,12},{6,14},{1,9},{3,11},{5,13},{7,15},{8,16},{10,1... | collective-permute-start | bytes 442376 | tf_op jit(solution)/shard_map/ppermute | solution.py:269
  135.8 12.7 %collective-permute-start.23 = (bf16[12,48,128]{2,1,0:T(8,128)(2,1)S(1)}, bf16[12,48,128]{2,1,0:T(8,128)(2,1)S(1)}, u32[]{:S(2)}, u32[]{:S(2)}) collective-permute-start(bf16[12,48,128]{2,1,0:T(8,128)(2,1)S(1)} %copy-done.24), channel_id=1, source_target_pairs={{0,9},{2,11},{4,13},{6,15},{1,8},{3,10},{5,12},{7,14},{8,17},{10,1... | collective-permute-start | bytes 442376 | tf_op jit(solution)/shard_map/ppermute | solution.py:269
  136.2 12.3 %collective-permute-start.24 = (bf16[12,48,128]{2,1,0:T(8,128)(2,1)S(1)}, bf16[12,48,128]{2,1,0:T(8,128)(2,1)S(1)}, u32[]{:S(2)}, u32[]{:S(2)}) collective-permute-start(bf16[12,48,128]{2,1,0:T(8,128)(2,1)S(1)} %copy-done.23), channel_id=1, source_target_pairs={{0,16},{2,18},{4,20},{6,22},{1,17},{3,19},{5,21},{7,23},{8,24},{10... | collective-permute-start | bytes 442376 | tf_op jit(solution)/shard_map/ppermute | solution.py:269
  139.7 8.8 %collective-permute-start.25 = (bf16[12,48,128]{2,1,0:T(8,128)(2,1)S(1)}, bf16[12,48,128]{2,1,0:T(8,128)(2,1)S(1)}, u32[]{:S(2)}, u32[]{:S(2)}) collective-permute-start(bf16[12,48,128]{2,1,0:T(8,128)(2,1)S(1)} %copy-done.22), channel_id=1, source_target_pairs={{0,17},{2,19},{4,21},{6,23},{1,16},{3,18},{5,20},{7,22},{8,25},{10... | collective-permute-start | bytes 442376 | tf_op jit(solution)/shard_map/ppermute | solution.py:269
  140.9 9.1 %collective-permute-start.26 = (bf16[12,48,128]{2,1,0:T(8,128)(2,1)S(1)}, bf16[12,48,128]{2,1,0:T(8,128)(2,1)S(1)}, u32[]{:S(2)}, u32[]{:S(2)}) collective-permute-start(bf16[12,48,128]{2,1,0:T(8,128)(2,1)S(1)} %copy-done.21), channel_id=1, source_target_pairs={{0,24},{2,26},{4,28},{6,30},{1,25},{3,27},{5,29},{7,31},{8,0},{10,... | collective-permute-start | bytes 442376 | tf_op jit(solution)/shard_map/ppermute | solution.py:269
  142.6 8.4 %collective-permute-start.27 = (bf16[12,48,128]{2,1,0:T(8,128)(2,1)S(1)}, bf16[12,48,128]{2,1,0:T(8,128)(2,1)S(1)}, u32[]{:S(2)}, u32[]{:S(2)}) collective-permute-start(bf16[12,48,128]{2,1,0:T(8,128)(2,1)S(1)} %copy-done.20), channel_id=1, source_target_pairs={{0,25},{2,27},{4,29},{6,31},{1,24},{3,26},{5,28},{7,30},{8,1},{10,... | collective-permute-start | bytes 442376 | tf_op jit(solution)/shard_map/ppermute | solution.py:269
  (8 other events, 26.3 us)

commit v5 on v4

--- a/solution.py
+++ b/solution.py
@@ -12,8 +12,10 @@
 SUM_LIMIT = 20 << 20
 
 
-def select_kernel(where, groups, outs, places_ref, table_ref, *refs):
-    pieces, out_refs, (held, stage, sems, out_sems) = refs[: -4 - outs], refs[-4 - outs : -4], refs[-4:]
+def select_kernel(where, groups, outs, late, places_ref, table_ref, *refs):
+    arrays = len(where)
+    pieces, out_refs, rest = refs[:arrays], refs[arrays : arrays + outs], refs[arrays + outs :]
+    list_ref, held, stage, sems, out_sems = rest
     per = held.shape[0] // places_ref.shape[0]
     copies = [
         pltpu.make_async_copy(
@@ -23,6 +25,15 @@
     ]
     for copy in copies:
         copy.start()
+    k, first, blocks = late
+    begin = places_ref[k] * per + first
+
+    def note(i, found):
+        slot = table_ref[i] - begin
+        list_ref[found + 1] = i
+        return found + jnp.logical_and(slot >= 0, slot < blocks).astype(jnp.int32)
+
+    list_ref[0] = lax.fori_loop(0, table_ref.shape[0], note, 0, unroll=4)
     for copy in copies:
         copy.wait()
     count = stage.shape[0] // groups
@@ -41,108 +52,122 @@
         copy.wait()
 
 
-def late_kernel(k, first, per, outs, places_ref, table_ref, piece, *refs):
+def late_kernel(k, first, per, outs, places_ref, table_ref, list_ref, piece, *refs):
     out_refs, (held, sem, out_sem) = refs[outs:-3], refs[-3:]
     load = pltpu.make_async_copy(piece, held, sem)
     load.start()
-    blocks = held.shape[0]
+    load.wait()
     begin = places_ref[k] * per + first
-    load.wait()
-    sent = 0
-    for g, out_ref in enumerate(out_refs):
-        count = out_ref.shape[0]
-
-        def put(i, sent, g=g, out_ref=out_ref, count=count):
-            slot = table_ref[g * count + i] - begin
-            mine = jnp.logical_and(slot >= 0, slot < blocks)
-
-            @pl.when(mine)
-            def _():
-                pltpu.make_async_copy(held.at[slot], out_ref.at[i], out_sem).start()
-
-            return sent + mine.astype(jnp.int32)
-
-        sent = lax.fori_loop(0, count, put, sent)
-
-    @pl.loop(0, sent)
-    def _(i):
+    count = out_refs[0].shape[0]
+    found = list_ref[0]
+
+    @pl.loop(0, found)
+    def _(n):
+        i = list_ref[n + 1]
+        source = held.at[table_ref[i] - begin]
+        if outs == 1:
+            pltpu.make_async_copy(source, out_refs[0].at[i], out_sem).start()
+        for g in range(outs if outs > 1 else 0):
+
+            @pl.when(i // count == g)
+            def _(g=g):
+                pltpu.make_async_copy(source, out_refs[g].at[i % count], out_sem).start()
+
+    @pl.loop(0, found)
+    def _(n):
         pltpu.make_async_copy(held.at[0], out_refs[0].at[0], out_sem).wait()
 
 
-def select_tiles(places, table, pieces, groups, apart, late=None):
-    early = pieces[:-1] if late else pieces
-    where, arrays = [w for w, _ in early], [array for _, array in early]
-    _, rows, blk = arrays[0].shape
-    dtype = arrays[0].dtype
+def select_early(places, table, pieces, groups, apart):
+    total = sum(array.shape[0] for _, array in pieces)
+    (k, first), last = pieces[-1]
+    where, arrays = [w for w, _ in pieces[:-1]], [array for _, array in pieces[:-1]]
+    blocks, rows, blk = last.shape
     count = table.shape[0]
     outs = groups if apart else 1
-    shapes = [jax.ShapeDtypeStruct((count // outs, rows, blk), dtype)] * outs
-    total = sum(array.shape[0] for _, array in pieces)
     picked = pl.pallas_call(
-        functools.partial(select_kernel, where, groups, outs),
-        out_shape=shapes,
+        functools.partial(select_kernel, where, groups, outs, (k, first, blocks)),
+        out_shape=[jax.ShapeDtypeStruct((count // outs, rows, blk), last.dtype)] * outs
+        + [jax.ShapeDtypeStruct((count + 2,), jnp.int32)],
         in_specs=[pl.BlockSpec(memory_space=pltpu.SMEM)] * 2
         + [pl.BlockSpec(memory_space=pl.ANY)] * len(arrays),
-        out_specs=[pl.BlockSpec(memory_space=pl.ANY)] * outs,
+        out_specs=[pl.BlockSpec(memory_space=pl.ANY)] * outs + [pl.BlockSpec(memory_space=pltpu.SMEM)],
         scratch_shapes=[
-            pltpu.VMEM((total, rows, blk), dtype),
-            pltpu.VMEM((count, rows, blk), dtype),
+            pltpu.VMEM((total, rows, blk), last.dtype),
+            pltpu.VMEM((count, rows, blk), last.dtype),
             pltpu.SemaphoreType.DMA((len(arrays),)),
             pltpu.SemaphoreType.DMA((groups,)),
         ],
         compiler_params=pltpu.CompilerParams(vmem_limit_bytes=SELECT_LIMIT),
         name="select_tiles",
     )(places, table, *arrays)
-    if not late:
-        return picked
+    return list(picked)
+
+
+def select_late(places, table, pieces, picked):
+    *picked, listed = picked
     (k, first), piece = pieces[-1]
+    outs = len(picked)
+    per = sum(array.shape[0] for _, array in pieces) // places.shape[0]
     return pl.pallas_call(
-        functools.partial(late_kernel, k, first, total // places.shape[0], outs),
-        out_shape=shapes,
-        in_specs=[pl.BlockSpec(memory_space=pltpu.SMEM)] * 2
+        functools.partial(late_kernel, k, first, per, outs),
+        out_shape=[jax.ShapeDtypeStruct(p.shape, p.dtype) for p in picked],
+        in_specs=[pl.BlockSpec(memory_space=pltpu.SMEM)] * 3
         + [pl.BlockSpec(memory_space=pl.ANY)] * (1 + outs),
         out_specs=[pl.BlockSpec(memory_space=pl.ANY)] * outs,
         scratch_shapes=[
-            pltpu.VMEM(piece.shape, dtype),
+            pltpu.VMEM(piece.shape, piece.dtype),
             pltpu.SemaphoreType.DMA,
             pltpu.SemaphoreType.DMA,
         ],
-        input_output_aliases={3 + i: i for i in range(outs)},
+        input_output_aliases={4 + i: i for i in range(outs)},
         compiler_params=pltpu.CompilerParams(vmem_limit_bytes=SELECT_LIMIT),
         name="late_tiles",
-    )(places, table, piece, *picked)
-
-
-def rows_in_order(order_ref, tiles, group, which, rows):
+    )(places, table, listed, piece, *picked)
+
+
+def rows_in_order(order_ref, tiles, p, rows):
     return jnp.concatenate(
-        [tiles[order_ref[d] * group + which, rows] for d in range(order_ref.shape[0])], 0
+        [tiles[order_ref[d], p, 0, rows] for d in range(order_ref.shape[0])], 0
     )
 
 
 def left_kernel(chunks, order_ref, tiles, *left_refs):
-    pairs = left_refs[0].shape[0]
-    chunk = tiles.shape[1] // chunks
-
-    @pl.loop(0, pairs, unroll=2)
-    def _(p):
+    chunk = tiles.shape[3] // chunks
+    for p in range(tiles.shape[1]):
         for c, left_ref in enumerate(left_refs):
-            rows = slice(c * chunk, (c + 1) * chunk)
-            left_ref[p] = rows_in_order(order_ref, tiles, 2 * pairs, 2 * p, rows).T
+            left_ref[p] = rows_in_order(order_ref, tiles, p, slice(c * chunk, (c + 1) * chunk)).T
 
 
 def gram_kernel(inverse, chunks, order_ref, *refs):
     lefts, (tiles, out_ref) = refs[:chunks], refs[chunks:]
-    pairs = out_ref.shape[0]
-    chunk = tiles.shape[1] // chunks
-
-    @pl.loop(0, pairs, unroll=2)
-    def _(p):
+    chunk = tiles.shape[3] // chunks
+    for p in range(tiles.shape[1]):
         total = jnp.zeros(out_ref.shape[1:], jnp.float32)
         for c, left_ref in enumerate(lefts):
-            rows = slice(c * chunk, (c + 1) * chunk)
-            right = rows_in_order(order_ref, tiles, 2 * pairs, 2 * p + 1, rows)
+            right = rows_in_order(order_ref, tiles, p, slice(c * chunk, (c + 1) * chunk))
             total += jnp.dot(left_ref[p], right, preferred_element_type=jnp.float32)
         out_ref[p] = total * inverse
+
+
+def pairs_call(kernel, order, lefts, tiles, which, outs, name):
+    groups, pairs, _, rows, blk = tiles.shape
+    step = pairs // 2 if pairs % 2 == 0 else pairs
+
+    def some(array):
+        return pl.BlockSpec((step,) + array.shape[1:], lambda p: (p, 0, 0))
+
+    return pl.pallas_call(
+        kernel,
+        grid=(pairs // step,),
+        out_shape=outs,
+        in_specs=[pl.BlockSpec(memory_space=pltpu.SMEM)]
+        + [some(left) for left in lefts]
+        + [pl.BlockSpec((groups, step, 1, rows, blk), lambda p: (0, p, which, 0, 0))],
+        out_specs=[some(out) for out in outs],
+        compiler_params=pltpu.CompilerParams(vmem_limit_bytes=SUM_LIMIT),
+        name=name,
+    )(order, *lefts, tiles)
 
 
 def cross_kernel(inverse, parts, left_ref, *refs):
@@ -268,9 +293,11 @@
             ]
         return lax.ppermute(tiles, ("tok", "feat"), perm)
 
+    own_in = blocks_of(span_input, side)
+    span_input, own_in = after(span_input, own_in)
+    others_in, others_out = from_sides(span_input), from_sides(span_output)
     own_out = blocks_of(span_output, side)
-    others_in, others_out = from_sides(span_input), from_sides(span_output)
-    streams_in = [far_hops(blocks_of(span_input, side))]
+    streams_in = [far_hops(own_in)]
     if sides > 1:
         others_in, streams_in[0][1] = after(others_in, streams_in[0][1])
         streams_in += [far_hops(other) for other in others_in]
@@ -281,26 +308,31 @@
     for held in streams_in[1:]:
         held.update(last_hops(held))
     chunks_out = [far_hops(unit) for unit in units]
-    (picked,) = select_tiles(places, slots.reshape(-1), pieces_of(streams_in), len(owners), False, True)
-    tiles_in = to_owners(picked)
+    pieces = pieces_of(streams_in)
+    picked = select_early(places, slots.reshape(-1), pieces, len(owners), False)
+    (picked,) = select_late(places, slots.reshape(-1), pieces, picked)
+    tiles_in = to_owners(picked).reshape(len(owners), pairs, 2, part, BLK)
     for held in chunks_out:
         held.update(last_hops(held))
 
     gram_shape = jax.ShapeDtypeStruct((pairs, BLK, BLK), jnp.float32)
     left_shape = jax.ShapeDtypeStruct((pairs, BLK, len(owners) * chunk), span_input.dtype)
-    lefts = sum_call(
-        functools.partial(left_kernel, chunks), [sources, tiles_in], [left_shape] * chunks, "left_tiles"
+    lefts = pairs_call(
+        functools.partial(left_kernel, chunks), sources, [], tiles_in, 0, [left_shape] * chunks, "left_tiles"
     )
+    pieces = [pieces_of([held]) for held in chunks_out]
+    early = [select_early(places, right_slots, p, len(owners), True) for p in pieces]
+    early[0], early[-1] = after(early[0], early[-1])
     cross = []
-    for c, held in enumerate(chunks_out):
+    for c in range(chunks):
         final = c + 1 == chunks
-        picked = select_tiles(places, right_slots, pieces_of([held]), len(owners), True, not final)
+        picked = select_late(places, right_slots, pieces[c], early[c])
         if final:
             picked, lefts = after(picked, lefts)
         got = [to_owner(tiles, d) for d, tiles in enumerate(picked)]
         if final:
-            (gram,) = sum_call(
-                functools.partial(gram_kernel, inverse, chunks), [sources] + list(lefts) + [tiles_in],
+            (gram,) = pairs_call(
+                functools.partial(gram_kernel, inverse, chunks), sources, lefts, tiles_in, 1,
                 [gram_shape], "gram_sum",
             )
             cross, gram = after(list(cross), gram)

time: 154 us -> 151 us (0.981)
    pallas_call x5 -> x8, Pallas kernels: 16.3 us -> 25 us  [the longest x3 12.5 us: select_early(): pl.pallas_call(functools.partial(select_kernel, where, groups, outs, (k,...]
    pallas_call x4 -> x2, Pallas kernels: 10.7 us -> 2.45 us  [sum_call(): pl.pallas_call(kernel, out_shape=outs, in_specs=[pl.BlockSpec(memory_spac...]
    ppermute x12, waiting for transfers between devices: 70.6 us -> 68.9 us  [hop(): lax.ppermute(piece, 'feat', [(f, at_place(f // sides, k) * sides + f % si...]
    unnamed x56 -> x48, local copies, waits for them, and re-layouts: 4.55 us -> 4.69 us
  transfers between devices with their start and end apart: 29 -> 29, of which waited for: 13 -> 13; matrix products, arithmetic and copies ran while one was open for 5% -> 3% of each run, Pallas kernels for 15% -> 15%
where the time goes in v5:
time: 151 us; the launch traced here: 150 us
  waiting for transfers between devices  83.6 us (55%)
  starting transfers between devices  29.4 us (19%)
  Pallas kernels  27.5 us (18%)
  local copies, waits for them, and re-layouts  7.37 us (5%)
    ppermute x12, waiting for transfers between devices, hop(): lax.ppermute(piece, 'feat', [(f, at_place(f // sides, k) * sides + f % si...  68.9 us
    ppermute x14, starting transfers between devices, to_owner(): return lax.ppermute(tiles, ('tok', 'feat'), perm)  17.1 us
    pallas_call x3, Pallas kernels, select_early(): pl.pallas_call(functools.partial(select_kernel, where, groups, outs, (k,...  12.5 us
    ppermute x14, waiting for transfers between devices, to_owner(): return lax.ppermute(tiles, ('tok', 'feat'), perm)  7.55 us
    pallas_call x3, Pallas kernels, select_late(): pl.pallas_call(functools.partial(late_kernel, k, first, per, outs), out_s...  7.3 us
    ppermute x2, waiting for transfers between devices, from_sides(): lax.ppermute(blocks_of(array, (side + d) % sides), 'feat', [(f, f // side...  7.13 us
    ppermute x12, starting transfers between devices, hop(): lax.ppermute(piece, 'feat', [(f, at_place(f // sides, k) * sides + f % si...  5.7 us
    pallas_call x2, Pallas kernels, pairs_call(): pl.pallas_call(kernel, grid=(pairs // step,), out_shape=outs, in_specs=[p...  5.21 us
  transfers between devices with their start and end apart: 29, of which 13 were waited for; matrix products, arithmetic and copies ran while one was open for 3% of the time, Pallas kernels for 15%

profile of v5, /device:TPU:25, one launch (start us, length us, event | category | flops | bytes accessed | tf_op | source)
XLA Modules:
  0.0 150.3 jit_solution(16600379535571693949)
XLA Ops:
  0.7 1.1 copy-done
  1.9 1.3 collective-permute-start
  3.4 1.2 dynamic-slice_bitcast_fusion
  5.0 7.1 %collective-permute-done.refs_4_ = bf16[16,96,128]{2,1,0:T(8,128)(2,1)S(1)} collective-permute-done((bf16[16,96,128]{2,1,0:T(8,128)(2,1)S(1)}, bf16[16,96,128]{2,1,0:T(8,128)(2,1)S(1)}, u32[]{:S(2)}, u32[]{:S(2)}) %collective-permute-start) | collective-permute-done | bytes 393248 | tf_op jit(solution)/shard_map/ppermute | solution.py:225
  12.1 8.3 %collective-permute-done.1.refs_1_ = bf16[16,96,128]{2,1,0:T(8,128)(2,1)S(1)} collective-permute-done((bf16[16,96,128]{2,1,0:T(8,128)(2,1)S(1)}, bf16[16,96,128]{2,1,0:T(8,128)(2,1)S(1)}, u32[]{:S(2)}, u32[]{:S(2)}) %collective-permute-start.1) | collective-permute-done | bytes 393248 | tf_op jit(solution)/shard_map/ppermute | solution.py:236
  20.4 1.1 collective-permute-start.6
  21.5 0.8 reshape.385
  22.4 0.4 collective-permute-start.3
  22.9 17.7 %collective-permute-done.5.refs_5_ = bf16[16,96,128]{2,1,0:T(8,128)(2,1)} collective-permute-done((bf16[16,96,128]{2,1,0:T(8,128)(2,1)S(1)}, bf16[16,96,128]{2,1,0:T(8,128)(2,1)}, u32[]{:S(2)}, u32[]{:S(2)}) %collective-permute-start.5) | collective-permute-done | bytes 393248 | tf_op jit(solution)/shard_map/ppermute | solution.py:236
  40.9 0.7 pad_add_fusion.places_ref
  41.6 0.5 fusion.13.table_ref
  42.1 7.0 %collective-permute-done.3.refs_3_ = bf16[16,96,128]{2,1,0:T(8,128)(2,1)} collective-permute-done((bf16[16,96,128]{2,1,0:T(8,128)(2,1)}, bf16[16,96,128]{2,1,0:T(8,128)(2,1)}, u32[]{:S(2)}, u32[]{:S(2)}) %collective-permute-start.3) | collective-permute-done | bytes 393248 | tf_op jit(solution)/shard_map/ppermute | solution.py:236
  49.1 5.4 %select_tiles.3 = (bf16[192,96,128]{2,1,0:T(8,128)(2,1)}, s32[194]{0:T(256)}) custom-call(s32[4]{0:T(128)} %pad_add_fusion.places_ref, s32[192]{0:T(256)} %fusion.13.table_ref, bf16[16,96,128]{2,1,0:T(8,128)(2,1)} %copy-done.5, bf16[16,96,128]{2,1,0:T(8,128)(2,1)} %copy-done.13, bf16[16,96,128]{2,1,0:T(8,128)(2,1)} %collective-permute-done.2.refs_2_, ...), custom_call_target="tpu_custom_call" | custom-call | tf_op jit(solution)/shard_map/select_tiles/pallas_call | solution.py:88
  54.5 2.9 %collective-permute-done.7.piece = bf16[16,96,128]{2,1,0:T(8,128)(2,1)S(1)} collective-permute-done((bf16[16,96,128]{2,1,0:T(8,128)(2,1)}, bf16[16,96,128]{2,1,0:T(8,128)(2,1)S(1)}, u32[]{:S(2)}, u32[]{:S(2)}) %collective-permute-start.7) | collective-permute-done | bytes 393248 | tf_op jit(solution)/shard_map/ppermute | solution.py:236
  57.4 0.7 copy-done.6
  58.1 2.5 %late_tiles.3 = bf16[192,96,128]{2,1,0:T(8,128)(2,1)} custom-call(s32[4]{0:T(128)} %pad_add_fusion.places_ref, s32[192]{0:T(256)} %fusion.13.table_ref, s32[194]{0:T(256)} %get-tuple-element.86.list_ref, bf16[16,96,128]{2,1,0:T(8,128)(2,1)} %copy-done.6, bf16[192,96,128]{2,1,0:T(8,128)(2,1)} %get-tuple-element.87.refs_0_), custom_call_target="tpu_custom_call", output_to_operand_aliasing={{}: (4, {})} | custom-call | tf_op jit(solution)/shard_map/late_tiles/pallas_call | solution.py:112
  60.7 5.1 %all-to-all-start = ((bf16[192,96,128]{2,1,0:T(8,128)(2,1)}), bf16[192,96,128]{2,1,0:T(8,128)(2,1)}, u32[]{:S(2)}, u32[]{:S(2)}) async-start(bf16[192,96,128]{2,1,0:T(8,128)(2,1)} %late_tiles.3), calls=%async_computation | async-start | bytes 9437184 | tf_op jit(solution)/shard_map/all_to_all | solution.py:281
  66.2 2.4 %collective-permute-start.11 = (bf16[32,48,128]{2,1,0:T(8,128)(2,1)S(1)}, bf16[32,48,128]{2,1,0:T(8,128)(2,1)S(1)}, u32[]{:S(2)}, u32[]{:S(2)}) collective-permute-start(bf16[32,48,128]{2,1,0:T(8,128)(2,1)S(1)} %get-tuple-element.99.refs_0_), channel_id=1, source_target_pairs={{0,4},{1,5},{2,6},{3,7},{4,0},{5,1},{6,2},{7,3},{8,12},{9,13},{10,... | collective-permute-start | bytes 1179656 | tf_op jit(solution)/shard_map/ppermute | solution.py:236
  68.6 1.5 collective-permute-start.10
  70.1 24.1 %collective-permute-done.9.refs_2_ = bf16[32,48,128]{2,1,0:T(8,128)(2,1)S(1)} collective-permute-done((bf16[32,48,128]{2,1,0:T(8,128)(2,1)S(1)}, bf16[32,48,128]{2,1,0:T(8,128)(2,1)S(1)}, u32[]{:S(2)}, u32[]{:S(2)}) %collective-permute-start.9) | collective-permute-done | bytes 393248 | tf_op jit(solution)/shard_map/ppermute | solution.py:236
  94.2 8.3 %collective-permute-done.11.refs_2_ = bf16[32,48,128]{2,1,0:T(8,128)(2,1)S(1)} collective-permute-done((bf16[32,48,128]{2,1,0:T(8,128)(2,1)S(1)}, bf16[32,48,128]{2,1,0:T(8,128)(2,1)S(1)}, u32[]{:S(2)}, u32[]{:S(2)}) %collective-permute-start.11) | collective-permute-done | bytes 393248 | tf_op jit(solution)/shard_map/ppermute | solution.py:236
  102.5 0.6 gather_fusion
  103.2 0.6 select_n.236.table_ref
  103.7 3.6 %select_tiles.4 = (bf16[12,48,128]{2,1,0:T(8,128)(2,1)}, bf16[12,48,128]{2,1,0:T(8,128)(2,1)}, bf16[12,48,128]{2,1,0:T(8,128)(2,1)}, bf16[12,48,128]{2,1,0:T(8,1...) custom-call(s32[4]{0:T(128)} %pad_add_fusion.places_ref, ...), custom_call_target="tpu_custom_call" | custom-call | tf_op jit(solution)/shard_map/select_tiles/pallas_call | solution.py:88
  107.4 0.7 copy-done.11
  108.1 3.6 %select_tiles.5 = (bf16[12,48,128]{2,1,0:T(8,128)(2,1)}, bf16[12,48,128]{2,1,0:T(8,128)(2,1)}, bf16[12,48,128]{2,1,0:T(8,128)(2,1)}, bf16[12,48,128]{2,1,0:T(8,1...) custom-call(s32[4]{0:T(128)} %pad_add_fusion.places_ref, ...), custom_call_target="tpu_custom_call" | custom-call | tf_op jit(solution)/shard_map/select_tiles/pallas_call | solution.py:88
  111.7 0.5 collective-permute-done.12.piece
  112.2 0.7 copy-done.10
  112.9 2.4 %late_tiles.4 = (bf16[12,48,128]{2,1,0:T(8,128)(2,1)}, bf16[12,48,128]{2,1,0:T(8,128)(2,1)}, bf16[12,48,128]{2,1,0:T(8,128)(2,1)}, bf16[12,48,128]{2,1,0:T(8,128...) custom-call(s32[4]{0:T(128)} %pad_add_fusion.places_ref, ...), custom_call_target="tpu_custom_call", output_to_operand_aliasing={{0}: (4, {}), {1}: (5, {}), {2}: (6, {}), {3}: (7, {}), {4}... | custom-call | tf_op jit(solution)/shard_map/late_tiles/pallas_call | solution.py:112
  115.3 1.3 collective-permute-start.13
  116.6 4.5 %collective-permute-start.14 = (bf16[12,48,128]{2,1,0:T(8,128)(2,1)}, bf16[12,48,128]{2,1,0:T(8,128)(2,1)S(1)}, u32[]{:S(2)}, u32[]{:S(2)}) collective-permute-start(bf16[12,48,128]{2,1,0:T(8,128)(2,1)} %get-tuple-element.120), channel_id=1, source_target_pairs={{0,8},{2,10},{4,12},{6,14},{1,9},{3,11},{5,13},{7,15},{8,16},{10,1... | collective-permute-start | bytes 442376 | tf_op jit(solution)/shard_map/ppermute | solution.py:294
  121.5 2.2 %collective-permute-start.17 = (bf16[12,48,128]{2,1,0:T(8,128)(2,1)}, bf16[12,48,128]{2,1,0:T(8,128)(2,1)S(1)}, u32[]{:S(2)}, u32[]{:S(2)}) collective-permute-start(bf16[12,48,128]{2,1,0:T(8,128)(2,1)} %get-tuple-element.123), channel_id=1, source_target_pairs={{0,17},{2,19},{4,21},{6,23},{1,16},{3,18},{5,20},{7,22},{8,25},{10... | collective-permute-start | bytes 442376 | tf_op jit(solution)/shard_map/ppermute | solution.py:294
  123.7 2.4 %late_tiles.5 = (bf16[12,48,128]{2,1,0:T(8,128)(2,1)}, bf16[12,48,128]{2,1,0:T(8,128)(2,1)}, bf16[12,48,128]{2,1,0:T(8,128)(2,1)}, bf16[12,48,128]{2,1,0:T(8,128...) custom-call(s32[4]{0:T(128)} %pad_add_fusion.places_ref, ...), custom_call_target="tpu_custom_call", output_to_operand_aliasing={{0}: (4, {}), {1}: (5, {}), {2}: (6, {}), {3}: (7, {}), {4}... | custom-call | tf_op jit(solution)/shard_map/late_tiles/pallas_call | solution.py:112
  126.2 2.2 %left_tiles.1 = (bf16[12,128,384]{2,1,0:T(8,128)(2,1)S(1)}, bf16[12,128,384]{2,1,0:T(8,128)(2,1)S(1)}) custom-call(s32[8]{0:T(128)S(1)} %stack.93.order_ref, bf16[8,12,2,96,128]{4,3,2,1,0:T(8,128)(2,1)} %bitcast.16.tiles.refs_2_), custom_call_target="tpu_custom_call" | custom-call | tf_op jit(solution)/shard_map/left_tiles/pallas_call | solution.py:160
  128.4 1.3 collective-permute-start.18
  130.0 1.2 collective-permute-start.21
  131.2 1.0 collective-permute-done.16.refs_4_
  132.2 1.1 collective-permute-start.22
  133.3 0.6 collective-permute-start.23
  133.9 2.2 %collective-permute-start.24 = (bf16[12,48,128]{2,1,0:T(8,128)(2,1)S(1)}, bf16[12,48,128]{2,1,0:T(8,128)(2,1)S(1)}, u32[]{:S(2)}, u32[]{:S(2)}) collective-permute-start(bf16[12,48,128]{2,1,0:T(8,128)(2,1)S(1)} %copy-done.17), channel_id=1, source_target_pairs={{0,16},{2,18},{4,20},{6,22},{1,17},{3,19},{5,21},{7,23},{8,24},{10... | collective-permute-start | bytes 442376 | tf_op jit(solution)/shard_map/ppermute | solution.py:294
  136.2 0.7 collective-permute-done.19.refs_7_
  137.2 1.0 collective-permute-done.21.refs_1_
  138.2 1.5 %collective-permute-start.26 = (bf16[12,48,128]{2,1,0:T(8,128)(2,1)S(1)}, bf16[12,48,128]{2,1,0:T(8,128)(2,1)S(1)}, u32[]{:S(2)}, u32[]{:S(2)}) collective-permute-start(bf16[12,48,128]{2,1,0:T(8,128)(2,1)S(1)} %copy-done.19), channel_id=1, source_target_pairs={{0,24},{2,26},{4,28},{6,30},{1,25},{3,27},{5,29},{7,31},{8,0},{10,... | collective-permute-start | bytes 442376 | tf_op jit(solution)/shard_map/ppermute | solution.py:294
  140.1 3.0 %gram_sum.1 = f32[12,128,128]{2,1,0:T(8,128)} custom-call(s32[8]{0:T(128)S(1)} %stack.93.order_ref, bf16[12,128,384]{2,1,0:T(8,128)(2,1)S(1)} %get-tuple-element.144.left_ref.refs_0_, bf16[12,128,384]{2,1,0:T(8,128)(2,1)S(1)} %get-tuple-element.145.refs_1_.left_ref, bf16[8,12,2,96,128]{4,3,2,1,0:T(8,128)(2,1)} %bitcast.16.tiles.refs_2_), custom_call_target="tpu_custom_call" | custom-call | tf_op jit(solution)/shard_map/gram_sum/pallas_call | solution.py:160
  143.1 0.8 cross_sum.2.refs_8_
  143.9 1.1 collective-permute-done.24.refs_4_
  145.0 3.6 %collective-permute-done.26.refs_6_ = bf16[12,48,128]{2,1,0:T(8,128)(2,1)S(1)} collective-permute-done((bf16[12,48,128]{2,1,0:T(8,128)(2,1)S(1)}, bf16[12,48,128]{2,1,0:T(8,128)(2,1)S(1)}, u32[]{:S(2)}, u32[]{:S(2)}) %collective-permute-start.26) | collective-permute-done | bytes 147488 | tf_op jit(solution)/shard_map/ppermute | solution.py:294
  148.6 1.7 %cross_sum.3 = f32[12,128,128]{2,1,0:T(8,128)} custom-call(bf16[12,128,384]{2,1,0:T(8,128)(2,1)S(1)} %get-tuple-element.145.refs_1_.left_ref, bf16[12,48,128]{2,1,0:T(8,128)(2,1)S(1)} %copy-done.1, bf16[12,48,128]{2,1,0:T(8,128)(2,1)S(1)} %collective-permute-done.21.refs_1_, bf16[12,48,128]{2,1,0:T(8,128)(2,1)S(1)} %collective-permute-done.22.refs_2_, ...), custom_call_target="tpu_custom_call" | custom-call | tf_op jit(solution)/shard_map/cross_sum/pallas_call | solution.py:185
  (91 shorter events, 2.9 us)
Async XLA Ops:
  1.8 47.2 %copy-start.5 = (bf16[16,96,128]{2,1,0:T(8,128)(2,1)}, bf16[16,96,128]{2,1,0:T(8,128)(2,1)S(1)}, u32[]{:S(2)}) copy-start(bf16[16,96,128]{2,1,0:T(8,128)(2,1)S(1)} %bitcast_bitcast_fusion.3.refs_0_) | copy-start | bytes 1179652
  1.9 10.2 %collective-permute-start = (bf16[16,96,128]{2,1,0:T(8,128)(2,1)S(1)}, bf16[16,96,128]{2,1,0:T(8,128)(2,1)S(1)}, u32[]{:S(2)}, u32[]{:S(2)}) collective-permute-start(bf16[16,96,128]{2,1,0:T(8,128)(2,1)S(1)} %bitcast_bitcast_fusion.2), channel_id=1, source_target_pairs={{0,1},{1,0},{2,3},{3,2},{4,5},{5,4},{6,7},{7,6},{8,9},{9,8},{10,11... | collective-permute-start | bytes 1179656 | tf_op jit(solution)/shard_map/ppermute | solution.py:225
  3.2 17.2 %collective-permute-start.1 = (bf16[16,96,128]{2,1,0:T(8,128)(2,1)S(1)}, bf16[16,96,128]{2,1,0:T(8,128)(2,1)S(1)}, u32[]{:S(2)}, u32[]{:S(2)}) collective-permute-start(bf16[16,96,128]{2,1,0:T(8,128)(2,1)S(1)} %bitcast_bitcast_fusion.3.refs_0_), channel_id=1, source_target_pairs={{0,2},{1,3},{2,0},{3,1},{4,6},{5,7},{6,4},{7,5},{8,10},{9,11},{10,... | collective-permute-start | bytes 1179656 | tf_op jit(solution)/shard_map/ppermute | solution.py:236
  3.4 19.0 %collective-permute-start.2 = (bf16[16,96,128]{2,1,0:T(8,128)(2,1)S(1)}, bf16[16,96,128]{2,1,0:T(8,128)(2,1)}, u32[]{:S(2)}, u32[]{:S(2)}) collective-permute-start(bf16[16,96,128]{2,1,0:T(8,128)(2,1)S(1)} %bitcast_bitcast_fusion.3.refs_0_), channel_id=1, source_target_pairs={{0,4},{1,5},{2,6},{3,7},{4,0},{5,1},{6,2},{7,3},{8,12},{9,13},{10,... | collective-permute-start | bytes 1179656 | tf_op jit(solution)/shard_map/ppermute | solution.py:236
  4.7 18.1 %collective-permute-start.4 = (bf16[16,96,128]{2,1,0:T(8,128)(2,1)S(1)}, bf16[16,96,128]{2,1,0:T(8,128)(2,1)S(1)}, u32[]{:S(2)}, u32[]{:S(2)}) collective-permute-start(bf16[16,96,128]{2,1,0:T(8,128)(2,1)S(1)} %bitcast.72), channel_id=1, source_target_pairs={{0,1},{1,0},{2,3},{3,2},{4,5},{5,4},{6,7},{7,6},{8,9},{9,8},{10,11... | collective-permute-start | bytes 1179656 | tf_op jit(solution)/shard_map/ppermute | solution.py:225
  12.1 37.0 %copy-start.12 = (bf16[16,96,128]{2,1,0:T(8,128)(2,1)}, bf16[16,96,128]{2,1,0:T(8,128)(2,1)S(1)}, u32[]{:S(2)}) copy-start(bf16[16,96,128]{2,1,0:T(8,128)(2,1)S(1)} %collective-permute-done.refs_4_) | copy-start | bytes 1179652
  20.4 28.7 %copy-start.13 = (bf16[16,96,128]{2,1,0:T(8,128)(2,1)}, bf16[16,96,128]{2,1,0:T(8,128)(2,1)S(1)}, u32[]{:S(2)}) copy-start(bf16[16,96,128]{2,1,0:T(8,128)(2,1)S(1)} %collective-permute-done.1.refs_1_) | copy-start | bytes 1179652
  20.4 20.2 %collective-permute-start.5 = (bf16[16,96,128]{2,1,0:T(8,128)(2,1)S(1)}, bf16[16,96,128]{2,1,0:T(8,128)(2,1)}, u32[]{:S(2)}, u32[]{:S(2)}) collective-permute-start(bf16[16,96,128]{2,1,0:T(8,128)(2,1)S(1)} %collective-permute-done.refs_4_), channel_id=1, source_target_pairs={{0,2},{1,3},{2,0},{3,1},{4,6},{5,7},{6,4},{7,5},{8,10},{9,11},{10,... | collective-permute-start | bytes 1179656 | tf_op jit(solution)/shard_map/ppermute | solution.py:236
  20.4 20.2 %collective-permute-start.6 = (bf16[16,96,128]{2,1,0:T(8,128)(2,1)S(1)}, bf16[16,96,128]{2,1,0:T(8,128)(2,1)}, u32[]{:S(2)}, u32[]{:S(2)}) collective-permute-start(bf16[16,96,128]{2,1,0:T(8,128)(2,1)S(1)} %collective-permute-done.refs_4_), channel_id=1, source_target_pairs={{0,4},{1,5},{2,6},{3,7},{4,0},{5,1},{6,2},{7,3},{8,12},{9,13},{10,... | collective-permute-start | bytes 1179656 | tf_op jit(solution)/shard_map/ppermute | solution.py:236
  22.4 26.7 %collective-permute-start.3 = (bf16[16,96,128]{2,1,0:T(8,128)(2,1)}, bf16[16,96,128]{2,1,0:T(8,128)(2,1)}, u32[]{:S(2)}, u32[]{:S(2)}) collective-permute-start(bf16[16,96,128]{2,1,0:T(8,128)(2,1)} %collective-permute-done.2.refs_2_), channel_id=1, source_target_pairs={{0,2},{1,3},{2,0},{3,1},{4,6},{5,7},{6,4},{7,5},{8,10},{9,11},{10,... | collective-permute-start | bytes 1179656 | tf_op jit(solution)/shard_map/ppermute | solution.py:236
  22.9 45.7 %copy-start.4 = (bf16[32,48,128]{2,1,0:T(8,128)(2,1)}, bf16[32,48,128]{2,1,0:T(8,128)(2,1)S(1)}, u32[]{:S(2)}) copy-start(bf16[32,48,128]{2,1,0:T(8,128)(2,1)S(1)} %get-tuple-element.89.refs_0_) | copy-start | bytes 1179652
  22.9 45.7 %copy-start.3 = (bf16[32,48,128]{2,1,0:T(8,128)(2,1)}, bf16[32,48,128]{2,1,0:T(8,128)(2,1)S(1)}, u32[]{:S(2)}) copy-start(bf16[32,48,128]{2,1,0:T(8,128)(2,1)S(1)} %get-tuple-element.99.refs_0_) | copy-start | bytes 1179652
  40.7 16.7 %collective-permute-start.7 = (bf16[16,96,128]{2,1,0:T(8,128)(2,1)}, bf16[16,96,128]{2,1,0:T(8,128)(2,1)S(1)}, u32[]{:S(2)}, u32[]{:S(2)}) collective-permute-start(bf16[16,96,128]{2,1,0:T(8,128)(2,1)} %collective-permute-done.6.refs_6_), channel_id=1, source_target_pairs={{0,2},{1,3},{2,0},{3,1},{4,6},{5,7},{6,4},{7,5},{8,10},{9,11},{10,... | collective-permute-start | bytes 1179656 | tf_op jit(solution)/shard_map/ppermute | solution.py:236
  60.7 65.5 %all-to-all-start = ((bf16[192,96,128]{2,1,0:T(8,128)(2,1)}), bf16[192,96,128]{2,1,0:T(8,128)(2,1)}, u32[]{:S(2)}, u32[]{:S(2)}) async-start(bf16[192,96,128]{2,1,0:T(8,128)(2,1)} %late_tiles.3), calls=%async_computation | async-start | bytes 9437184 | tf_op jit(solution)/shard_map/all_to_all | solution.py:281
  66.1 28.1 %collective-permute-start.9 = (bf16[32,48,128]{2,1,0:T(8,128)(2,1)S(1)}, bf16[32,48,128]{2,1,0:T(8,128)(2,1)S(1)}, u32[]{:S(2)}, u32[]{:S(2)}) collective-permute-start(bf16[32,48,128]{2,1,0:T(8,128)(2,1)S(1)} %get-tuple-element.89.refs_0_), channel_id=1, source_target_pairs={{0,4},{1,5},{2,6},{3,7},{4,0},{5,1},{6,2},{7,3},{8,12},{9,13},{10,... | collective-permute-start | bytes 1179656 | tf_op jit(solution)/shard_map/ppermute | solution.py:236
  66.2 36.3 %collective-permute-start.11 = (bf16[32,48,128]{2,1,0:T(8,128)(2,1)S(1)}, bf16[32,48,128]{2,1,0:T(8,128)(2,1)S(1)}, u32[]{:S(2)}, u32[]{:S(2)}) collective-permute-start(bf16[32,48,128]{2,1,0:T(8,128)(2,1)S(1)} %get-tuple-element.99.refs_0_), channel_id=1, source_target_pairs={{0,4},{1,5},{2,6},{3,7},{4,0},{5,1},{6,2},{7,3},{8,12},{9,13},{10,... | collective-permute-start | bytes 1179656 | tf_op jit(solution)/shard_map/ppermute | solution.py:236
  68.6 35.1 %collective-permute-start.8 = (bf16[32,48,128]{2,1,0:T(8,128)(2,1)S(1)}, bf16[32,48,128]{2,1,0:T(8,128)(2,1)}, u32[]{:S(2)}, u32[]{:S(2)}) collective-permute-start(bf16[32,48,128]{2,1,0:T(8,128)(2,1)S(1)} %get-tuple-element.89.refs_0_), channel_id=1, source_target_pairs={{0,2},{1,3},{2,0},{3,1},{4,6},{5,7},{6,4},{7,5},{8,10},{9,11},{10,... | collective-permute-start | bytes 1179656 | tf_op jit(solution)/shard_map/ppermute | solution.py:236
  68.6 38.7 %collective-permute-start.10 = (bf16[32,48,128]{2,1,0:T(8,128)(2,1)S(1)}, bf16[32,48,128]{2,1,0:T(8,128)(2,1)S(1)}, u32[]{:S(2)}, u32[]{:S(2)}) collective-permute-start(bf16[32,48,128]{2,1,0:T(8,128)(2,1)S(1)} %get-tuple-element.99.refs_0_), channel_id=1, source_target_pairs={{0,2},{1,3},{2,0},{3,1},{4,6},{5,7},{6,4},{7,5},{8,10},{9,11},{10,... | collective-permute-start | bytes 1179656 | tf_op jit(solution)/shard_map/ppermute | solution.py:236
  94.2 9.6 %copy-start.9 = (bf16[32,48,128]{2,1,0:T(8,128)(2,1)}, bf16[32,48,128]{2,1,0:T(8,128)(2,1)S(1)}, u32[]{:S(2)}) copy-start(bf16[32,48,128]{2,1,0:T(8,128)(2,1)S(1)} %collective-permute-done.9.refs_2_) | copy-start | bytes 1179652
  94.2 18.0 %collective-permute-start.12 = (bf16[32,48,128]{2,1,0:T(8,128)(2,1)S(1)}, bf16[32,48,128]{2,1,0:T(8,128)(2,1)S(1)}, u32[]{:S(2)}, u32[]{:S(2)}) collective-permute-start(bf16[32,48,128]{2,1,0:T(8,128)(2,1)S(1)} %collective-permute-done.9.refs_2_), channel_id=1, source_target_pairs={{0,2},{1,3},{2,0},{3,1},{4,6},{5,7},{6,4},{7,5},{8,10},{9,11},{10,... | collective-permute-start | bytes 1179656 | tf_op jit(solution)/shard_map/ppermute | solution.py:236
  102.5 4.9 %copy-start.7 = (bf16[32,48,128]{2,1,0:T(8,128)(2,1)}, bf16[32,48,128]{2,1,0:T(8,128)(2,1)S(1)}, u32[]{:S(2)}) copy-start(bf16[32,48,128]{2,1,0:T(8,128)(2,1)S(1)} %collective-permute-done.11.refs_2_) | copy-start | bytes 1179652
  102.5 19.0 %collective-permute-start.20 = (bf16[32,48,128]{2,1,0:T(8,128)(2,1)S(1)}, bf16[32,48,128]{2,1,0:T(8,128)(2,1)S(1)}, u32[]{:S(2)}, u32[]{:S(2)}) collective-permute-start(bf16[32,48,128]{2,1,0:T(8,128)(2,1)S(1)} %collective-permute-done.11.refs_2_), channel_id=1, source_target_pairs={{0,2},{1,3},{2,0},{3,1},{4,6},{5,7},{6,4},{7,5},{8,10},{9,11},{10,... | collective-permute-start | bytes 1179656 | tf_op jit(solution)/shard_map/ppermute | solution.py:236
  115.3 13.1 %copy-start.21 = (bf16[12,48,128]{2,1,0:T(8,128)(2,1)S(1)}, bf16[12,48,128]{2,1,0:T(8,128)(2,1)}, u32[]{:S(2)}) copy-start(bf16[12,48,128]{2,1,0:T(8,128)(2,1)} %get-tuple-element.124) | copy-start | bytes 442372
  115.3 14.4 %copy-start.22 = (bf16[12,48,128]{2,1,0:T(8,128)(2,1)S(1)}, bf16[12,48,128]{2,1,0:T(8,128)(2,1)}, u32[]{:S(2)}) copy-start(bf16[12,48,128]{2,1,0:T(8,128)(2,1)} %get-tuple-element.125) | copy-start | bytes 442372
  115.3 13.1 %collective-permute-start.13 = (bf16[12,48,128]{2,1,0:T(8,128)(2,1)}, bf16[12,48,128]{2,1,0:T(8,128)(2,1)S(1)}, u32[]{:S(2)}, u32[]{:S(2)}) collective-permute-start(bf16[12,48,128]{2,1,0:T(8,128)(2,1)} %get-tuple-element.119), channel_id=1, source_target_pairs={{0,1},{2,3},{4,5},{6,7},{1,0},{3,2},{5,4},{7,6},{8,9},{10,11},{12,... | collective-permute-start | bytes 442376 | tf_op jit(solution)/shard_map/ppermute | solution.py:294
  116.6 13.1 %collective-permute-start.14 = (bf16[12,48,128]{2,1,0:T(8,128)(2,1)}, bf16[12,48,128]{2,1,0:T(8,128)(2,1)S(1)}, u32[]{:S(2)}, u32[]{:S(2)}) collective-permute-start(bf16[12,48,128]{2,1,0:T(8,128)(2,1)} %get-tuple-element.120), channel_id=1, source_target_pairs={{0,8},{2,10},{4,12},{6,14},{1,9},{3,11},{5,13},{7,15},{8,16},{10,1... | collective-permute-start | bytes 442376 | tf_op jit(solution)/shard_map/ppermute | solution.py:294
  121.2 8.8 %collective-permute-start.15 = (bf16[12,48,128]{2,1,0:T(8,128)(2,1)}, bf16[12,48,128]{2,1,0:T(8,128)(2,1)S(1)}, u32[]{:S(2)}, u32[]{:S(2)}) collective-permute-start(bf16[12,48,128]{2,1,0:T(8,128)(2,1)} %get-tuple-element.121), channel_id=1, source_target_pairs={{0,9},{2,11},{4,13},{6,15},{1,8},{3,10},{5,12},{7,14},{8,17},{10,1... | collective-permute-start | bytes 442376 | tf_op jit(solution)/shard_map/ppermute | solution.py:294
  121.2 11.0 %collective-permute-start.16 = (bf16[12,48,128]{2,1,0:T(8,128)(2,1)}, bf16[12,48,128]{2,1,0:T(8,128)(2,1)S(1)}, u32[]{:S(2)}, u32[]{:S(2)}) collective-permute-start(bf16[12,48,128]{2,1,0:T(8,128)(2,1)} %get-tuple-element.122), channel_id=1, source_target_pairs={{0,16},{2,18},{4,20},{6,22},{1,17},{3,19},{5,21},{7,23},{8,24},{10... | collective-permute-start | bytes 442376 | tf_op jit(solution)/shard_map/ppermute | solution.py:294
  121.5 2.2 %copy-start.8 = (bf16[32,48,128]{2,1,0:T(8,128)(2,1)}, bf16[32,48,128]{2,1,0:T(8,128)(2,1)S(1)}, u32[]{:S(2)}) copy-start(bf16[32,48,128]{2,1,0:T(8,128)(2,1)S(1)} %collective-permute-done.20.piece) | copy-start | bytes 1179652
  121.5 11.8 %collective-permute-start.17 = (bf16[12,48,128]{2,1,0:T(8,128)(2,1)}, bf16[12,48,128]{2,1,0:T(8,128)(2,1)S(1)}, u32[]{:S(2)}, u32[]{:S(2)}) collective-permute-start(bf16[12,48,128]{2,1,0:T(8,128)(2,1)} %get-tuple-element.123), channel_id=1, source_target_pairs={{0,17},{2,19},{4,21},{6,23},{1,16},{3,18},{5,20},{7,22},{8,25},{10... | collective-permute-start | bytes 442376 | tf_op jit(solution)/shard_map/ppermute | solution.py:294
  126.1 3.9 %copy-start.14 = (bf16[12,48,128]{2,1,0:T(8,128)(2,1)S(1)}, bf16[12,48,128]{2,1,0:T(8,128)(2,1)}, u32[]{:S(2)}) copy-start(bf16[12,48,128]{2,1,0:T(8,128)(2,1)} %get-tuple-element.148) | copy-start | bytes 442372
  126.1 6.1 %copy-start.15 = (bf16[12,48,128]{2,1,0:T(8,128)(2,1)S(1)}, bf16[12,48,128]{2,1,0:T(8,128)(2,1)}, u32[]{:S(2)}) copy-start(bf16[12,48,128]{2,1,0:T(8,128)(2,1)} %get-tuple-element.149) | copy-start | bytes 442372
  126.1 7.2 %copy-start.16 = (bf16[12,48,128]{2,1,0:T(8,128)(2,1)S(1)}, bf16[12,48,128]{2,1,0:T(8,128)(2,1)}, u32[]{:S(2)}) copy-start(bf16[12,48,128]{2,1,0:T(8,128)(2,1)} %get-tuple-element.150) | copy-start | bytes 442372
  126.1 7.8 %copy-start.17 = (bf16[12,48,128]{2,1,0:T(8,128)(2,1)S(1)}, bf16[12,48,128]{2,1,0:T(8,128)(2,1)}, u32[]{:S(2)}) copy-start(bf16[12,48,128]{2,1,0:T(8,128)(2,1)} %get-tuple-element.151) | copy-start | bytes 442372
  126.1 10.7 %copy-start.18 = (bf16[12,48,128]{2,1,0:T(8,128)(2,1)S(1)}, bf16[12,48,128]{2,1,0:T(8,128)(2,1)}, u32[]{:S(2)}) copy-start(bf16[12,48,128]{2,1,0:T(8,128)(2,1)} %get-tuple-element.152) | copy-start | bytes 442372
  126.2 12.0 %copy-start.19 = (bf16[12,48,128]{2,1,0:T(8,128)(2,1)S(1)}, bf16[12,48,128]{2,1,0:T(8,128)(2,1)}, u32[]{:S(2)}) copy-start(bf16[12,48,128]{2,1,0:T(8,128)(2,1)} %get-tuple-element.153) | copy-start | bytes 442372
  126.2 13.5 %copy-start.20 = (bf16[12,48,128]{2,1,0:T(8,128)(2,1)S(1)}, bf16[12,48,128]{2,1,0:T(8,128)(2,1)}, u32[]{:S(2)}) copy-start(bf16[12,48,128]{2,1,0:T(8,128)(2,1)} %get-tuple-element.154) | copy-start | bytes 442372
  128.4 14.7 %copy-start.2 = (bf16[12,48,128]{2,1,0:T(8,128)(2,1)S(1)}, bf16[12,48,128]{2,1,0:T(8,128)(2,1)}, u32[]{:S(2)}) copy-start(bf16[12,48,128]{2,1,0:T(8,128)(2,1)} %get-tuple-element.118.refs_0_) | copy-start | bytes 442372
  128.4 5.5 %collective-permute-start.18 = (bf16[12,48,128]{2,1,0:T(8,128)(2,1)S(1)}, bf16[12,48,128]{2,1,0:T(8,128)(2,1)S(1)}, u32[]{:S(2)}, u32[]{:S(2)}) collective-permute-start(bf16[12,48,128]{2,1,0:T(8,128)(2,1)S(1)} %copy-done.21), channel_id=1, source_target_pairs={{0,24},{2,26},{4,28},{6,30},{1,25},{3,27},{5,29},{7,31},{8,0},{10,... | collective-permute-start | bytes 442376 | tf_op jit(solution)/shard_map/ppermute | solution.py:294
  129.8 18.9 %copy-start.1 = (bf16[12,48,128]{2,1,0:T(8,128)(2,1)S(1)}, bf16[12,48,128]{2,1,0:T(8,128)(2,1)}, u32[]{:S(2)}) copy-start(bf16[12,48,128]{2,1,0:T(8,128)(2,1)} %get-tuple-element.147.refs_0_) | copy-start | bytes 442372
  129.8 7.1 %collective-permute-start.19 = (bf16[12,48,128]{2,1,0:T(8,128)(2,1)S(1)}, bf16[12,48,128]{2,1,0:T(8,128)(2,1)S(1)}, u32[]{:S(2)}, u32[]{:S(2)}) collective-permute-start(bf16[12,48,128]{2,1,0:T(8,128)(2,1)S(1)} %copy-done.22), channel_id=1, source_target_pairs={{0,25},{2,27},{4,29},{6,31},{1,24},{3,26},{5,28},{7,30},{8,1},{10,... | collective-permute-start | bytes 442376 | tf_op jit(solution)/shard_map/ppermute | solution.py:294
  130.0 8.2 %collective-permute-start.21 = (bf16[12,48,128]{2,1,0:T(8,128)(2,1)S(1)}, bf16[12,48,128]{2,1,0:T(8,128)(2,1)S(1)}, u32[]{:S(2)}, u32[]{:S(2)}) collective-permute-start(bf16[12,48,128]{2,1,0:T(8,128)(2,1)S(1)} %copy-done.14), channel_id=1, source_target_pairs={{0,1},{2,3},{4,5},{6,7},{1,0},{3,2},{5,4},{7,6},{8,9},{10,11},{12,... | collective-permute-start | bytes 442376 | tf_op jit(solution)/shard_map/ppermute | solution.py:294
  132.2 7.5 %collective-permute-start.22 = (bf16[12,48,128]{2,1,0:T(8,128)(2,1)S(1)}, bf16[12,48,128]{2,1,0:T(8,128)(2,1)S(1)}, u32[]{:S(2)}, u32[]{:S(2)}) collective-permute-start(bf16[12,48,128]{2,1,0:T(8,128)(2,1)S(1)} %copy-done.15), channel_id=1, source_target_pairs={{0,8},{2,10},{4,12},{6,14},{1,9},{3,11},{5,13},{7,15},{8,16},{10,1... | collective-permute-start | bytes 442376 | tf_op jit(solution)/shard_map/ppermute | solution.py:294
  133.3 10.6 %collective-permute-start.23 = (bf16[12,48,128]{2,1,0:T(8,128)(2,1)S(1)}, bf16[12,48,128]{2,1,0:T(8,128)(2,1)S(1)}, u32[]{:S(2)}, u32[]{:S(2)}) collective-permute-start(bf16[12,48,128]{2,1,0:T(8,128)(2,1)S(1)} %copy-done.16), channel_id=1, source_target_pairs={{0,9},{2,11},{4,13},{6,15},{1,8},{3,10},{5,12},{7,14},{8,17},{10,1... | collective-permute-start | bytes 442376 | tf_op jit(solution)/shard_map/ppermute | solution.py:294
  133.9 11.1 %collective-permute-start.24 = (bf16[12,48,128]{2,1,0:T(8,128)(2,1)S(1)}, bf16[12,48,128]{2,1,0:T(8,128)(2,1)S(1)}, u32[]{:S(2)}, u32[]{:S(2)}) collective-permute-start(bf16[12,48,128]{2,1,0:T(8,128)(2,1)S(1)} %copy-done.17), channel_id=1, source_target_pairs={{0,16},{2,18},{4,20},{6,22},{1,17},{3,19},{5,21},{7,23},{8,24},{10... | collective-permute-start | bytes 442376 | tf_op jit(solution)/shard_map/ppermute | solution.py:294
  136.9 8.1 %collective-permute-start.25 = (bf16[12,48,128]{2,1,0:T(8,128)(2,1)S(1)}, bf16[12,48,128]{2,1,0:T(8,128)(2,1)S(1)}, u32[]{:S(2)}, u32[]{:S(2)}) collective-permute-start(bf16[12,48,128]{2,1,0:T(8,128)(2,1)S(1)} %copy-done.18), channel_id=1, source_target_pairs={{0,17},{2,19},{4,21},{6,23},{1,16},{3,18},{5,20},{7,22},{8,25},{10... | collective-permute-start | bytes 442376 | tf_op jit(solution)/shard_map/ppermute | solution.py:294
  138.2 10.4 %collective-permute-start.26 = (bf16[12,48,128]{2,1,0:T(8,128)(2,1)S(1)}, bf16[12,48,128]{2,1,0:T(8,128)(2,1)S(1)}, u32[]{:S(2)}, u32[]{:S(2)}) collective-permute-start(bf16[12,48,128]{2,1,0:T(8,128)(2,1)S(1)} %copy-done.19), channel_id=1, source_target_pairs={{0,24},{2,26},{4,28},{6,30},{1,25},{3,27},{5,29},{7,31},{8,0},{10,... | collective-permute-start | bytes 442376 | tf_op jit(solution)/shard_map/ppermute | solution.py:294
  139.7 8.9 %collective-permute-start.27 = (bf16[12,48,128]{2,1,0:T(8,128)(2,1)S(1)}, bf16[12,48,128]{2,1,0:T(8,128)(2,1)S(1)}, u32[]{:S(2)}, u32[]{:S(2)}) collective-permute-start(bf16[12,48,128]{2,1,0:T(8,128)(2,1)S(1)} %copy-done.20), channel_id=1, source_target_pairs={{0,25},{2,27},{4,29},{6,31},{1,24},{3,26},{5,28},{7,30},{8,1},{10,... | collective-permute-start | bytes 442376 | tf_op jit(solution)/shard_map/ppermute | solution.py:294
  (4 other events, 3.4 us)

commit v6 on v5

--- a/solution.py
+++ b/solution.py
@@ -53,10 +53,7 @@
 
 
 def late_kernel(k, first, per, outs, places_ref, table_ref, list_ref, piece, *refs):
-    out_refs, (held, sem, out_sem) = refs[outs:-3], refs[-3:]
-    load = pltpu.make_async_copy(piece, held, sem)
-    load.start()
-    load.wait()
+    out_refs, out_sem = refs[outs:-1], refs[-1]
     begin = places_ref[k] * per + first
     count = out_refs[0].shape[0]
     found = list_ref[0]
@@ -64,7 +61,7 @@
     @pl.loop(0, found)
     def _(n):
         i = list_ref[n + 1]
-        source = held.at[table_ref[i] - begin]
+        source = piece.at[table_ref[i] - begin]
         if outs == 1:
             pltpu.make_async_copy(source, out_refs[0].at[i], out_sem).start()
         for g in range(outs if outs > 1 else 0):
@@ -75,7 +72,7 @@
 
     @pl.loop(0, found)
     def _(n):
-        pltpu.make_async_copy(held.at[0], out_refs[0].at[0], out_sem).wait()
+        pltpu.make_async_copy(piece.at[0], out_refs[0].at[0], out_sem).wait()
 
 
 def select_early(places, table, pieces, groups, apart):
@@ -113,13 +110,10 @@
         functools.partial(late_kernel, k, first, per, outs),
         out_shape=[jax.ShapeDtypeStruct(p.shape, p.dtype) for p in picked],
         in_specs=[pl.BlockSpec(memory_space=pltpu.SMEM)] * 3
-        + [pl.BlockSpec(memory_space=pl.ANY)] * (1 + outs),
+        + [pl.BlockSpec(memory_space=pltpu.VMEM)]
+        + [pl.BlockSpec(memory_space=pl.ANY)] * outs,
         out_specs=[pl.BlockSpec(memory_space=pl.ANY)] * outs,
-        scratch_shapes=[
-            pltpu.VMEM(piece.shape, piece.dtype),
-            pltpu.SemaphoreType.DMA,
-            pltpu.SemaphoreType.DMA,
-        ],
+        scratch_shapes=[pltpu.SemaphoreType.DMA],
         input_output_aliases={4 + i: i for i in range(outs)},
         compiler_params=pltpu.CompilerParams(vmem_limit_bytes=SELECT_LIMIT),
         name="late_tiles",

time: 151 us -> 150 us (level)
  transfers between devices with their start and end apart: 29 -> 29, of which waited for: 13 -> 14; matrix products, arithmetic and copies ran while one was open for 3% -> 3% of each run, Pallas kernels for 15% -> 15%
where the time goes in v6:
time: 150 us; the launch traced here: 149 us
  waiting for transfers between devices  83.2 us (55%)
  starting transfers between devices  29.8 us (20%)
  Pallas kernels  26.5 us (18%)
  local copies, waits for them, and re-layouts  7.37 us (5%)
    ppermute x12, waiting for transfers between devices, hop(): lax.ppermute(piece, 'feat', [(f, at_place(f // sides, k) * sides + f % si...  68.9 us
    ppermute x14, starting transfers between devices, to_owner(): return lax.ppermute(tiles, ('tok', 'feat'), perm)  17.5 us
    pallas_call x3, Pallas kernels, select_early(): pl.pallas_call(functools.partial(select_kernel, where, groups, outs, (k,...  12.5 us
    ppermute x14, waiting for transfers between devices, to_owner(): return lax.ppermute(tiles, ('tok', 'feat'), perm)  7.21 us
    ppermute x2, waiting for transfers between devices, from_sides(): lax.ppermute(blocks_of(array, (side + d) % sides), 'feat', [(f, f // side...  7.13 us
    pallas_call x3, Pallas kernels, select_late(): pl.pallas_call(functools.partial(late_kernel, k, first, per, outs), out_s...  6.31 us
    ppermute x12, starting transfers between devices, hop(): lax.ppermute(piece, 'feat', [(f, at_place(f // sides, k) * sides + f % si...  5.7 us
    pallas_call x2, Pallas kernels, pairs_call(): pl.pallas_call(kernel, grid=(pairs // step,), out_shape=outs, in_specs=[p...  5.2 us
  transfers between devices with their start and end apart: 29, of which 14 were waited for; matrix products, arithmetic and copies ran while one was open for 3% of the time, Pallas kernels for 15%

profile of v6, /device:TPU:25, one launch (start us, length us, event | category | flops | bytes accessed | tf_op | source)
XLA Modules:
  0.0 149.4 jit_solution(1624495143701398937)
XLA Ops:
  0.7 1.1 copy-done
  1.9 1.3 collective-permute-start
  3.4 1.2 dynamic-slice_bitcast_fusion
  5.0 7.1 %collective-permute-done.refs_4_ = bf16[16,96,128]{2,1,0:T(8,128)(2,1)S(1)} collective-permute-done((bf16[16,96,128]{2,1,0:T(8,128)(2,1)S(1)}, bf16[16,96,128]{2,1,0:T(8,128)(2,1)S(1)}, u32[]{:S(2)}, u32[]{:S(2)}) %collective-permute-start) | collective-permute-done | bytes 393248 | tf_op jit(solution)/shard_map/ppermute | solution.py:219
  12.1 8.3 %collective-permute-done.1.refs_1_ = bf16[16,96,128]{2,1,0:T(8,128)(2,1)S(1)} collective-permute-done((bf16[16,96,128]{2,1,0:T(8,128)(2,1)S(1)}, bf16[16,96,128]{2,1,0:T(8,128)(2,1)S(1)}, u32[]{:S(2)}, u32[]{:S(2)}) %collective-permute-start.1) | collective-permute-done | bytes 393248 | tf_op jit(solution)/shard_map/ppermute | solution.py:230
  20.4 1.1 collective-permute-start.6
  21.5 0.8 reshape.385
  22.4 0.4 collective-permute-start.3
  22.9 17.7 %collective-permute-done.5.refs_5_ = bf16[16,96,128]{2,1,0:T(8,128)(2,1)} collective-permute-done((bf16[16,96,128]{2,1,0:T(8,128)(2,1)S(1)}, bf16[16,96,128]{2,1,0:T(8,128)(2,1)}, u32[]{:S(2)}, u32[]{:S(2)}) %collective-permute-start.5) | collective-permute-done | bytes 393248 | tf_op jit(solution)/shard_map/ppermute | solution.py:230
  40.9 0.7 pad_add_fusion.places_ref
  41.6 0.5 fusion.13.table_ref
  42.1 7.0 %collective-permute-done.3.refs_3_ = bf16[16,96,128]{2,1,0:T(8,128)(2,1)} collective-permute-done((bf16[16,96,128]{2,1,0:T(8,128)(2,1)}, bf16[16,96,128]{2,1,0:T(8,128)(2,1)}, u32[]{:S(2)}, u32[]{:S(2)}) %collective-permute-start.3) | collective-permute-done | bytes 393248 | tf_op jit(solution)/shard_map/ppermute | solution.py:230
  49.1 5.4 %select_tiles.3 = (bf16[192,96,128]{2,1,0:T(8,128)(2,1)}, s32[194]{0:T(256)}) custom-call(s32[4]{0:T(128)} %pad_add_fusion.places_ref, s32[192]{0:T(256)} %fusion.13.table_ref, bf16[16,96,128]{2,1,0:T(8,128)(2,1)} %copy-done.5, bf16[16,96,128]{2,1,0:T(8,128)(2,1)} %copy-done.13, bf16[16,96,128]{2,1,0:T(8,128)(2,1)} %collective-permute-done.2.refs_2_, ...), custom_call_target="tpu_custom_call" | custom-call | tf_op jit(solution)/shard_map/select_tiles/pallas_call | solution.py:85
  54.5 2.9 %collective-permute-done.7.piece = bf16[16,96,128]{2,1,0:T(8,128)(2,1)S(1)} collective-permute-done((bf16[16,96,128]{2,1,0:T(8,128)(2,1)}, bf16[16,96,128]{2,1,0:T(8,128)(2,1)S(1)}, u32[]{:S(2)}, u32[]{:S(2)}) %collective-permute-start.7) | collective-permute-done | bytes 393248 | tf_op jit(solution)/shard_map/ppermute | solution.py:230
  57.4 0.7 copy-done.6
  58.1 1.9 %late_tiles.3 = bf16[192,96,128]{2,1,0:T(8,128)(2,1)} custom-call(s32[4]{0:T(128)} %pad_add_fusion.places_ref, s32[192]{0:T(256)} %fusion.13.table_ref, s32[194]{0:T(256)} %get-tuple-element.86.list_ref, bf16[16,96,128]{2,1,0:T(8,128)(2,1)} %copy-done.6, bf16[192,96,128]{2,1,0:T(8,128)(2,1)} %get-tuple-element.87.refs_0_), custom_call_target="tpu_custom_call", output_to_operand_aliasing={{}: (4, {})} | custom-call | tf_op jit(solution)/shard_map/late_tiles/pallas_call | solution.py:109
  60.0 5.1 %all-to-all-start = ((bf16[192,96,128]{2,1,0:T(8,128)(2,1)}), bf16[192,96,128]{2,1,0:T(8,128)(2,1)}, u32[]{:S(2)}, u32[]{:S(2)}) async-start(bf16[192,96,128]{2,1,0:T(8,128)(2,1)} %late_tiles.3), calls=%async_computation | async-start | bytes 9437184 | tf_op jit(solution)/shard_map/all_to_all | solution.py:275
  65.5 2.4 %collective-permute-start.11 = (bf16[32,48,128]{2,1,0:T(8,128)(2,1)S(1)}, bf16[32,48,128]{2,1,0:T(8,128)(2,1)S(1)}, u32[]{:S(2)}, u32[]{:S(2)}) collective-permute-start(bf16[32,48,128]{2,1,0:T(8,128)(2,1)S(1)} %get-tuple-element.99.refs_0_), channel_id=1, source_target_pairs={{0,4},{1,5},{2,6},{3,7},{4,0},{5,1},{6,2},{7,3},{8,12},{9,13},{10,... | collective-permute-start | bytes 1179656 | tf_op jit(solution)/shard_map/ppermute | solution.py:230
  68.0 1.5 collective-permute-start.10
  69.4 24.2 %collective-permute-done.9.refs_2_ = bf16[32,48,128]{2,1,0:T(8,128)(2,1)S(1)} collective-permute-done((bf16[32,48,128]{2,1,0:T(8,128)(2,1)S(1)}, bf16[32,48,128]{2,1,0:T(8,128)(2,1)S(1)}, u32[]{:S(2)}, u32[]{:S(2)}) %collective-permute-start.9) | collective-permute-done | bytes 393248 | tf_op jit(solution)/shard_map/ppermute | solution.py:230
  93.6 8.3 %collective-permute-done.11.refs_2_ = bf16[32,48,128]{2,1,0:T(8,128)(2,1)S(1)} collective-permute-done((bf16[32,48,128]{2,1,0:T(8,128)(2,1)S(1)}, bf16[32,48,128]{2,1,0:T(8,128)(2,1)S(1)}, u32[]{:S(2)}, u32[]{:S(2)}) %collective-permute-start.11) | collective-permute-done | bytes 393248 | tf_op jit(solution)/shard_map/ppermute | solution.py:230
  101.9 0.6 gather_fusion
  102.6 0.6 select_n.236.table_ref
  103.1 3.6 %select_tiles.4 = (bf16[12,48,128]{2,1,0:T(8,128)(2,1)}, bf16[12,48,128]{2,1,0:T(8,128)(2,1)}, bf16[12,48,128]{2,1,0:T(8,128)(2,1)}, bf16[12,48,128]{2,1,0:T(8,1...) custom-call(s32[4]{0:T(128)} %pad_add_fusion.places_ref, ...), custom_call_target="tpu_custom_call" | custom-call | tf_op jit(solution)/shard_map/select_tiles/pallas_call | solution.py:85
  106.8 0.7 copy-done.11
  107.5 3.6 %select_tiles.5 = (bf16[12,48,128]{2,1,0:T(8,128)(2,1)}, bf16[12,48,128]{2,1,0:T(8,128)(2,1)}, bf16[12,48,128]{2,1,0:T(8,128)(2,1)}, bf16[12,48,128]{2,1,0:T(8,1...) custom-call(s32[4]{0:T(128)} %pad_add_fusion.places_ref, ...), custom_call_target="tpu_custom_call" | custom-call | tf_op jit(solution)/shard_map/select_tiles/pallas_call | solution.py:85
  111.1 0.4 collective-permute-done.12.piece
  111.5 0.7 copy-done.10
  112.3 2.2 %late_tiles.4 = (bf16[12,48,128]{2,1,0:T(8,128)(2,1)}, bf16[12,48,128]{2,1,0:T(8,128)(2,1)}, bf16[12,48,128]{2,1,0:T(8,128)(2,1)}, bf16[12,48,128]{2,1,0:T(8,128...) custom-call(s32[4]{0:T(128)} %pad_add_fusion.places_ref, ...), custom_call_target="tpu_custom_call", output_to_operand_aliasing={{0}: (4, {}), {1}: (5, {}), {2}: (6, {}), {3}: (7, {}), {4}... | custom-call | tf_op jit(solution)/shard_map/late_tiles/pallas_call | solution.py:109
  114.5 1.3 collective-permute-start.13
  115.8 4.5 %collective-permute-start.14 = (bf16[12,48,128]{2,1,0:T(8,128)(2,1)}, bf16[12,48,128]{2,1,0:T(8,128)(2,1)S(1)}, u32[]{:S(2)}, u32[]{:S(2)}) collective-permute-start(bf16[12,48,128]{2,1,0:T(8,128)(2,1)} %get-tuple-element.120), channel_id=1, source_target_pairs={{0,8},{2,10},{4,12},{6,14},{1,9},{3,11},{5,13},{7,15},{8,16},{10,1... | collective-permute-start | bytes 442376 | tf_op jit(solution)/shard_map/ppermute | solution.py:288
  120.7 2.2 %collective-permute-start.17 = (bf16[12,48,128]{2,1,0:T(8,128)(2,1)}, bf16[12,48,128]{2,1,0:T(8,128)(2,1)S(1)}, u32[]{:S(2)}, u32[]{:S(2)}) collective-permute-start(bf16[12,48,128]{2,1,0:T(8,128)(2,1)} %get-tuple-element.123), channel_id=1, source_target_pairs={{0,17},{2,19},{4,21},{6,23},{1,16},{3,18},{5,20},{7,22},{8,25},{10... | collective-permute-start | bytes 442376 | tf_op jit(solution)/shard_map/ppermute | solution.py:288
  122.9 2.2 %late_tiles.5 = (bf16[12,48,128]{2,1,0:T(8,128)(2,1)}, bf16[12,48,128]{2,1,0:T(8,128)(2,1)}, bf16[12,48,128]{2,1,0:T(8,128)(2,1)}, bf16[12,48,128]{2,1,0:T(8,128...) custom-call(s32[4]{0:T(128)} %pad_add_fusion.places_ref, ...), custom_call_target="tpu_custom_call", output_to_operand_aliasing={{0}: (4, {}), {1}: (5, {}), {2}: (6, {}), {3}: (7, {}), {4}... | custom-call | tf_op jit(solution)/shard_map/late_tiles/pallas_call | solution.py:109
  125.2 2.2 %left_tiles.1 = (bf16[12,128,384]{2,1,0:T(8,128)(2,1)S(1)}, bf16[12,128,384]{2,1,0:T(8,128)(2,1)S(1)}) custom-call(s32[8]{0:T(128)S(1)} %stack.93.order_ref, bf16[8,12,2,96,128]{4,3,2,1,0:T(8,128)(2,1)} %bitcast.16.tiles.refs_2_), custom_call_target="tpu_custom_call" | custom-call | tf_op jit(solution)/shard_map/left_tiles/pallas_call | solution.py:154
  127.4 1.3 collective-permute-start.18
  129.0 1.2 collective-permute-start.21
  130.2 1.2 collective-permute-done.16.refs_4_
  131.4 1.0 collective-permute-start.22
  132.5 0.6 collective-permute-start.23
  133.2 2.5 %collective-permute-start.24 = (bf16[12,48,128]{2,1,0:T(8,128)(2,1)S(1)}, bf16[12,48,128]{2,1,0:T(8,128)(2,1)S(1)}, u32[]{:S(2)}, u32[]{:S(2)}) collective-permute-start(bf16[12,48,128]{2,1,0:T(8,128)(2,1)S(1)} %copy-done.17), channel_id=1, source_target_pairs={{0,16},{2,18},{4,20},{6,22},{1,17},{3,19},{5,21},{7,23},{8,24},{10... | collective-permute-start | bytes 442376 | tf_op jit(solution)/shard_map/ppermute | solution.py:288
  136.3 0.9 collective-permute-done.21.refs_1_
  137.2 1.5 %collective-permute-start.26 = (bf16[12,48,128]{2,1,0:T(8,128)(2,1)S(1)}, bf16[12,48,128]{2,1,0:T(8,128)(2,1)S(1)}, u32[]{:S(2)}, u32[]{:S(2)}) collective-permute-start(bf16[12,48,128]{2,1,0:T(8,128)(2,1)S(1)} %copy-done.19), channel_id=1, source_target_pairs={{0,24},{2,26},{4,28},{6,30},{1,25},{3,27},{5,29},{7,31},{8,0},{10,... | collective-permute-start | bytes 442376 | tf_op jit(solution)/shard_map/ppermute | solution.py:288
  138.7 0.5 collective-permute-start.27
  139.2 3.0 %gram_sum.1 = f32[12,128,128]{2,1,0:T(8,128)} custom-call(s32[8]{0:T(128)S(1)} %stack.93.order_ref, bf16[12,128,384]{2,1,0:T(8,128)(2,1)S(1)} %get-tuple-element.144.left_ref.refs_0_, bf16[12,128,384]{2,1,0:T(8,128)(2,1)S(1)} %get-tuple-element.145.refs_1_.left_ref, bf16[8,12,2,96,128]{4,3,2,1,0:T(8,128)(2,1)} %bitcast.16.tiles.refs_2_), custom_call_target="tpu_custom_call" | custom-call | tf_op jit(solution)/shard_map/gram_sum/pallas_call | solution.py:154
  142.2 0.8 cross_sum.2.refs_8_
  143.0 1.2 collective-permute-done.24.refs_4_
  144.2 3.5 %collective-permute-done.26.refs_6_ = bf16[12,48,128]{2,1,0:T(8,128)(2,1)S(1)} collective-permute-done((bf16[12,48,128]{2,1,0:T(8,128)(2,1)S(1)}, bf16[12,48,128]{2,1,0:T(8,128)(2,1)S(1)}, u32[]{:S(2)}, u32[]{:S(2)}) %collective-permute-start.26) | collective-permute-done | bytes 147488 | tf_op jit(solution)/shard_map/ppermute | solution.py:288
  147.7 1.7 %cross_sum.3 = f32[12,128,128]{2,1,0:T(8,128)} custom-call(bf16[12,128,384]{2,1,0:T(8,128)(2,1)S(1)} %get-tuple-element.145.refs_1_.left_ref, bf16[12,48,128]{2,1,0:T(8,128)(2,1)S(1)} %copy-done.1, bf16[12,48,128]{2,1,0:T(8,128)(2,1)S(1)} %collective-permute-done.21.refs_1_, bf16[12,48,128]{2,1,0:T(8,128)(2,1)S(1)} %collective-permute-done.22.refs_2_, ...), custom_call_target="tpu_custom_call" | custom-call | tf_op jit(solution)/shard_map/cross_sum/pallas_call | solution.py:179
  (91 shorter events, 3.0 us)
Async XLA Ops:
  1.8 47.2 %copy-start.5 = (bf16[16,96,128]{2,1,0:T(8,128)(2,1)}, bf16[16,96,128]{2,1,0:T(8,128)(2,1)S(1)}, u32[]{:S(2)}) copy-start(bf16[16,96,128]{2,1,0:T(8,128)(2,1)S(1)} %bitcast_bitcast_fusion.3.refs_0_) | copy-start | bytes 1179652
  1.9 10.2 %collective-permute-start = (bf16[16,96,128]{2,1,0:T(8,128)(2,1)S(1)}, bf16[16,96,128]{2,1,0:T(8,128)(2,1)S(1)}, u32[]{:S(2)}, u32[]{:S(2)}) collective-permute-start(bf16[16,96,128]{2,1,0:T(8,128)(2,1)S(1)} %bitcast_bitcast_fusion.2), channel_id=1, source_target_pairs={{0,1},{1,0},{2,3},{3,2},{4,5},{5,4},{6,7},{7,6},{8,9},{9,8},{10,11... | collective-permute-start | bytes 1179656 | tf_op jit(solution)/shard_map/ppermute | solution.py:219
  3.2 17.2 %collective-permute-start.1 = (bf16[16,96,128]{2,1,0:T(8,128)(2,1)S(1)}, bf16[16,96,128]{2,1,0:T(8,128)(2,1)S(1)}, u32[]{:S(2)}, u32[]{:S(2)}) collective-permute-start(bf16[16,96,128]{2,1,0:T(8,128)(2,1)S(1)} %bitcast_bitcast_fusion.3.refs_0_), channel_id=1, source_target_pairs={{0,2},{1,3},{2,0},{3,1},{4,6},{5,7},{6,4},{7,5},{8,10},{9,11},{10,... | collective-permute-start | bytes 1179656 | tf_op jit(solution)/shard_map/ppermute | solution.py:230
  3.4 19.0 %collective-permute-start.2 = (bf16[16,96,128]{2,1,0:T(8,128)(2,1)S(1)}, bf16[16,96,128]{2,1,0:T(8,128)(2,1)}, u32[]{:S(2)}, u32[]{:S(2)}) collective-permute-start(bf16[16,96,128]{2,1,0:T(8,128)(2,1)S(1)} %bitcast_bitcast_fusion.3.refs_0_), channel_id=1, source_target_pairs={{0,4},{1,5},{2,6},{3,7},{4,0},{5,1},{6,2},{7,3},{8,12},{9,13},{10,... | collective-permute-start | bytes 1179656 | tf_op jit(solution)/shard_map/ppermute | solution.py:230
  4.7 18.1 %collective-permute-start.4 = (bf16[16,96,128]{2,1,0:T(8,128)(2,1)S(1)}, bf16[16,96,128]{2,1,0:T(8,128)(2,1)S(1)}, u32[]{:S(2)}, u32[]{:S(2)}) collective-permute-start(bf16[16,96,128]{2,1,0:T(8,128)(2,1)S(1)} %bitcast.72), channel_id=1, source_target_pairs={{0,1},{1,0},{2,3},{3,2},{4,5},{5,4},{6,7},{7,6},{8,9},{9,8},{10,11... | collective-permute-start | bytes 1179656 | tf_op jit(solution)/shard_map/ppermute | solution.py:219
  12.1 37.0 %copy-start.12 = (bf16[16,96,128]{2,1,0:T(8,128)(2,1)}, bf16[16,96,128]{2,1,0:T(8,128)(2,1)S(1)}, u32[]{:S(2)}) copy-start(bf16[16,96,128]{2,1,0:T(8,128)(2,1)S(1)} %collective-permute-done.refs_4_) | copy-start | bytes 1179652
  20.4 28.7 %copy-start.13 = (bf16[16,96,128]{2,1,0:T(8,128)(2,1)}, bf16[16,96,128]{2,1,0:T(8,128)(2,1)S(1)}, u32[]{:S(2)}) copy-start(bf16[16,96,128]{2,1,0:T(8,128)(2,1)S(1)} %collective-permute-done.1.refs_1_) | copy-start | bytes 1179652
  20.4 20.2 %collective-permute-start.5 = (bf16[16,96,128]{2,1,0:T(8,128)(2,1)S(1)}, bf16[16,96,128]{2,1,0:T(8,128)(2,1)}, u32[]{:S(2)}, u32[]{:S(2)}) collective-permute-start(bf16[16,96,128]{2,1,0:T(8,128)(2,1)S(1)} %collective-permute-done.refs_4_), channel_id=1, source_target_pairs={{0,2},{1,3},{2,0},{3,1},{4,6},{5,7},{6,4},{7,5},{8,10},{9,11},{10,... | collective-permute-start | bytes 1179656 | tf_op jit(solution)/shard_map/ppermute | solution.py:230
  20.4 20.2 %collective-permute-start.6 = (bf16[16,96,128]{2,1,0:T(8,128)(2,1)S(1)}, bf16[16,96,128]{2,1,0:T(8,128)(2,1)}, u32[]{:S(2)}, u32[]{:S(2)}) collective-permute-start(bf16[16,96,128]{2,1,0:T(8,128)(2,1)S(1)} %collective-permute-done.refs_4_), channel_id=1, source_target_pairs={{0,4},{1,5},{2,6},{3,7},{4,0},{5,1},{6,2},{7,3},{8,12},{9,13},{10,... | collective-permute-start | bytes 1179656 | tf_op jit(solution)/shard_map/ppermute | solution.py:230
  22.4 26.7 %collective-permute-start.3 = (bf16[16,96,128]{2,1,0:T(8,128)(2,1)}, bf16[16,96,128]{2,1,0:T(8,128)(2,1)}, u32[]{:S(2)}, u32[]{:S(2)}) collective-permute-start(bf16[16,96,128]{2,1,0:T(8,128)(2,1)} %collective-permute-done.2.refs_2_), channel_id=1, source_target_pairs={{0,2},{1,3},{2,0},{3,1},{4,6},{5,7},{6,4},{7,5},{8,10},{9,11},{10,... | collective-permute-start | bytes 1179656 | tf_op jit(solution)/shard_map/ppermute | solution.py:230
  22.9 45.1 %copy-start.4 = (bf16[32,48,128]{2,1,0:T(8,128)(2,1)}, bf16[32,48,128]{2,1,0:T(8,128)(2,1)S(1)}, u32[]{:S(2)}) copy-start(bf16[32,48,128]{2,1,0:T(8,128)(2,1)S(1)} %get-tuple-element.89.refs_0_) | copy-start | bytes 1179652
  22.9 45.1 %copy-start.3 = (bf16[32,48,128]{2,1,0:T(8,128)(2,1)}, bf16[32,48,128]{2,1,0:T(8,128)(2,1)S(1)}, u32[]{:S(2)}) copy-start(bf16[32,48,128]{2,1,0:T(8,128)(2,1)S(1)} %get-tuple-element.99.refs_0_) | copy-start | bytes 1179652
  40.7 16.7 %collective-permute-start.7 = (bf16[16,96,128]{2,1,0:T(8,128)(2,1)}, bf16[16,96,128]{2,1,0:T(8,128)(2,1)S(1)}, u32[]{:S(2)}, u32[]{:S(2)}) collective-permute-start(bf16[16,96,128]{2,1,0:T(8,128)(2,1)} %collective-permute-done.6.refs_6_), channel_id=1, source_target_pairs={{0,2},{1,3},{2,0},{3,1},{4,6},{5,7},{6,4},{7,5},{8,10},{9,11},{10,... | collective-permute-start | bytes 1179656 | tf_op jit(solution)/shard_map/ppermute | solution.py:230
  60.0 65.1 %all-to-all-start = ((bf16[192,96,128]{2,1,0:T(8,128)(2,1)}), bf16[192,96,128]{2,1,0:T(8,128)(2,1)}, u32[]{:S(2)}, u32[]{:S(2)}) async-start(bf16[192,96,128]{2,1,0:T(8,128)(2,1)} %late_tiles.3), calls=%async_computation | async-start | bytes 9437184 | tf_op jit(solution)/shard_map/all_to_all | solution.py:275
  65.5 28.1 %collective-permute-start.9 = (bf16[32,48,128]{2,1,0:T(8,128)(2,1)S(1)}, bf16[32,48,128]{2,1,0:T(8,128)(2,1)S(1)}, u32[]{:S(2)}, u32[]{:S(2)}) collective-permute-start(bf16[32,48,128]{2,1,0:T(8,128)(2,1)S(1)} %get-tuple-element.89.refs_0_), channel_id=1, source_target_pairs={{0,4},{1,5},{2,6},{3,7},{4,0},{5,1},{6,2},{7,3},{8,12},{9,13},{10,... | collective-permute-start | bytes 1179656 | tf_op jit(solution)/shard_map/ppermute | solution.py:230
  65.5 36.4 %collective-permute-start.11 = (bf16[32,48,128]{2,1,0:T(8,128)(2,1)S(1)}, bf16[32,48,128]{2,1,0:T(8,128)(2,1)S(1)}, u32[]{:S(2)}, u32[]{:S(2)}) collective-permute-start(bf16[32,48,128]{2,1,0:T(8,128)(2,1)S(1)} %get-tuple-element.99.refs_0_), channel_id=1, source_target_pairs={{0,4},{1,5},{2,6},{3,7},{4,0},{5,1},{6,2},{7,3},{8,12},{9,13},{10,... | collective-permute-start | bytes 1179656 | tf_op jit(solution)/shard_map/ppermute | solution.py:230
  68.0 35.2 %collective-permute-start.8 = (bf16[32,48,128]{2,1,0:T(8,128)(2,1)S(1)}, bf16[32,48,128]{2,1,0:T(8,128)(2,1)}, u32[]{:S(2)}, u32[]{:S(2)}) collective-permute-start(bf16[32,48,128]{2,1,0:T(8,128)(2,1)S(1)} %get-tuple-element.89.refs_0_), channel_id=1, source_target_pairs={{0,2},{1,3},{2,0},{3,1},{4,6},{5,7},{6,4},{7,5},{8,10},{9,11},{10,... | collective-permute-start | bytes 1179656 | tf_op jit(solution)/shard_map/ppermute | solution.py:230
  68.0 38.8 %collective-permute-start.10 = (bf16[32,48,128]{2,1,0:T(8,128)(2,1)S(1)}, bf16[32,48,128]{2,1,0:T(8,128)(2,1)S(1)}, u32[]{:S(2)}, u32[]{:S(2)}) collective-permute-start(bf16[32,48,128]{2,1,0:T(8,128)(2,1)S(1)} %get-tuple-element.99.refs_0_), channel_id=1, source_target_pairs={{0,2},{1,3},{2,0},{3,1},{4,6},{5,7},{6,4},{7,5},{8,10},{9,11},{10,... | collective-permute-start | bytes 1179656 | tf_op jit(solution)/shard_map/ppermute | solution.py:230
  93.6 9.6 %copy-start.9 = (bf16[32,48,128]{2,1,0:T(8,128)(2,1)}, bf16[32,48,128]{2,1,0:T(8,128)(2,1)S(1)}, u32[]{:S(2)}) copy-start(bf16[32,48,128]{2,1,0:T(8,128)(2,1)S(1)} %collective-permute-done.9.refs_2_) | copy-start | bytes 1179652
  93.6 17.9 %collective-permute-start.12 = (bf16[32,48,128]{2,1,0:T(8,128)(2,1)S(1)}, bf16[32,48,128]{2,1,0:T(8,128)(2,1)S(1)}, u32[]{:S(2)}, u32[]{:S(2)}) collective-permute-start(bf16[32,48,128]{2,1,0:T(8,128)(2,1)S(1)} %collective-permute-done.9.refs_2_), channel_id=1, source_target_pairs={{0,2},{1,3},{2,0},{3,1},{4,6},{5,7},{6,4},{7,5},{8,10},{9,11},{10,... | collective-permute-start | bytes 1179656 | tf_op jit(solution)/shard_map/ppermute | solution.py:230
  101.9 4.9 %copy-start.7 = (bf16[32,48,128]{2,1,0:T(8,128)(2,1)}, bf16[32,48,128]{2,1,0:T(8,128)(2,1)S(1)}, u32[]{:S(2)}) copy-start(bf16[32,48,128]{2,1,0:T(8,128)(2,1)S(1)} %collective-permute-done.11.refs_2_) | copy-start | bytes 1179652
  101.9 18.8 %collective-permute-start.20 = (bf16[32,48,128]{2,1,0:T(8,128)(2,1)S(1)}, bf16[32,48,128]{2,1,0:T(8,128)(2,1)S(1)}, u32[]{:S(2)}, u32[]{:S(2)}) collective-permute-start(bf16[32,48,128]{2,1,0:T(8,128)(2,1)S(1)} %collective-permute-done.11.refs_2_), channel_id=1, source_target_pairs={{0,2},{1,3},{2,0},{3,1},{4,6},{5,7},{6,4},{7,5},{8,10},{9,11},{10,... | collective-permute-start | bytes 1179656 | tf_op jit(solution)/shard_map/ppermute | solution.py:230
  114.5 12.9 %copy-start.21 = (bf16[12,48,128]{2,1,0:T(8,128)(2,1)S(1)}, bf16[12,48,128]{2,1,0:T(8,128)(2,1)}, u32[]{:S(2)}) copy-start(bf16[12,48,128]{2,1,0:T(8,128)(2,1)} %get-tuple-element.124) | copy-start | bytes 442372
  114.5 14.2 %copy-start.22 = (bf16[12,48,128]{2,1,0:T(8,128)(2,1)S(1)}, bf16[12,48,128]{2,1,0:T(8,128)(2,1)}, u32[]{:S(2)}) copy-start(bf16[12,48,128]{2,1,0:T(8,128)(2,1)} %get-tuple-element.125) | copy-start | bytes 442372
  114.5 12.9 %collective-permute-start.13 = (bf16[12,48,128]{2,1,0:T(8,128)(2,1)}, bf16[12,48,128]{2,1,0:T(8,128)(2,1)S(1)}, u32[]{:S(2)}, u32[]{:S(2)}) collective-permute-start(bf16[12,48,128]{2,1,0:T(8,128)(2,1)} %get-tuple-element.119), channel_id=1, source_target_pairs={{0,1},{2,3},{4,5},{6,7},{1,0},{3,2},{5,4},{7,6},{8,9},{10,11},{12,... | collective-permute-start | bytes 442376 | tf_op jit(solution)/shard_map/ppermute | solution.py:288
  115.8 12.9 %collective-permute-start.14 = (bf16[12,48,128]{2,1,0:T(8,128)(2,1)}, bf16[12,48,128]{2,1,0:T(8,128)(2,1)S(1)}, u32[]{:S(2)}, u32[]{:S(2)}) collective-permute-start(bf16[12,48,128]{2,1,0:T(8,128)(2,1)} %get-tuple-element.120), channel_id=1, source_target_pairs={{0,8},{2,10},{4,12},{6,14},{1,9},{3,11},{5,13},{7,15},{8,16},{10,1... | collective-permute-start | bytes 442376 | tf_op jit(solution)/shard_map/ppermute | solution.py:288
  120.3 8.6 %collective-permute-start.15 = (bf16[12,48,128]{2,1,0:T(8,128)(2,1)}, bf16[12,48,128]{2,1,0:T(8,128)(2,1)S(1)}, u32[]{:S(2)}, u32[]{:S(2)}) collective-permute-start(bf16[12,48,128]{2,1,0:T(8,128)(2,1)} %get-tuple-element.121), channel_id=1, source_target_pairs={{0,9},{2,11},{4,13},{6,15},{1,8},{3,10},{5,12},{7,14},{8,17},{10,1... | collective-permute-start | bytes 442376 | tf_op jit(solution)/shard_map/ppermute | solution.py:288
  120.3 11.1 %collective-permute-start.16 = (bf16[12,48,128]{2,1,0:T(8,128)(2,1)}, bf16[12,48,128]{2,1,0:T(8,128)(2,1)S(1)}, u32[]{:S(2)}, u32[]{:S(2)}) collective-permute-start(bf16[12,48,128]{2,1,0:T(8,128)(2,1)} %get-tuple-element.122), channel_id=1, source_target_pairs={{0,16},{2,18},{4,20},{6,22},{1,17},{3,19},{5,21},{7,23},{8,24},{10... | collective-permute-start | bytes 442376 | tf_op jit(solution)/shard_map/ppermute | solution.py:288
  120.7 2.2 %copy-start.8 = (bf16[32,48,128]{2,1,0:T(8,128)(2,1)}, bf16[32,48,128]{2,1,0:T(8,128)(2,1)S(1)}, u32[]{:S(2)}) copy-start(bf16[32,48,128]{2,1,0:T(8,128)(2,1)S(1)} %collective-permute-done.20.piece) | copy-start | bytes 1179652
  120.7 11.8 %collective-permute-start.17 = (bf16[12,48,128]{2,1,0:T(8,128)(2,1)}, bf16[12,48,128]{2,1,0:T(8,128)(2,1)S(1)}, u32[]{:S(2)}, u32[]{:S(2)}) collective-permute-start(bf16[12,48,128]{2,1,0:T(8,128)(2,1)} %get-tuple-element.123), channel_id=1, source_target_pairs={{0,17},{2,19},{4,21},{6,23},{1,16},{3,18},{5,20},{7,22},{8,25},{10... | collective-permute-start | bytes 442376 | tf_op jit(solution)/shard_map/ppermute | solution.py:288
  125.1 3.9 %copy-start.14 = (bf16[12,48,128]{2,1,0:T(8,128)(2,1)S(1)}, bf16[12,48,128]{2,1,0:T(8,128)(2,1)}, u32[]{:S(2)}) copy-start(bf16[12,48,128]{2,1,0:T(8,128)(2,1)} %get-tuple-element.148) | copy-start | bytes 442372
  125.1 6.3 %copy-start.15 = (bf16[12,48,128]{2,1,0:T(8,128)(2,1)S(1)}, bf16[12,48,128]{2,1,0:T(8,128)(2,1)}, u32[]{:S(2)}) copy-start(bf16[12,48,128]{2,1,0:T(8,128)(2,1)} %get-tuple-element.149) | copy-start | bytes 442372
  125.1 7.3 %copy-start.16 = (bf16[12,48,128]{2,1,0:T(8,128)(2,1)S(1)}, bf16[12,48,128]{2,1,0:T(8,128)(2,1)}, u32[]{:S(2)}) copy-start(bf16[12,48,128]{2,1,0:T(8,128)(2,1)} %get-tuple-element.150) | copy-start | bytes 442372
  125.1 8.1 %copy-start.17 = (bf16[12,48,128]{2,1,0:T(8,128)(2,1)S(1)}, bf16[12,48,128]{2,1,0:T(8,128)(2,1)}, u32[]{:S(2)}) copy-start(bf16[12,48,128]{2,1,0:T(8,128)(2,1)} %get-tuple-element.151) | copy-start | bytes 442372
  125.1 10.7 %copy-start.18 = (bf16[12,48,128]{2,1,0:T(8,128)(2,1)S(1)}, bf16[12,48,128]{2,1,0:T(8,128)(2,1)}, u32[]{:S(2)}) copy-start(bf16[12,48,128]{2,1,0:T(8,128)(2,1)} %get-tuple-element.152) | copy-start | bytes 442372
  125.2 12.0 %copy-start.19 = (bf16[12,48,128]{2,1,0:T(8,128)(2,1)S(1)}, bf16[12,48,128]{2,1,0:T(8,128)(2,1)}, u32[]{:S(2)}) copy-start(bf16[12,48,128]{2,1,0:T(8,128)(2,1)} %get-tuple-element.153) | copy-start | bytes 442372
  125.2 13.5 %copy-start.20 = (bf16[12,48,128]{2,1,0:T(8,128)(2,1)S(1)}, bf16[12,48,128]{2,1,0:T(8,128)(2,1)}, u32[]{:S(2)}) copy-start(bf16[12,48,128]{2,1,0:T(8,128)(2,1)} %get-tuple-element.154) | copy-start | bytes 442372
  127.4 14.8 %copy-start.2 = (bf16[12,48,128]{2,1,0:T(8,128)(2,1)S(1)}, bf16[12,48,128]{2,1,0:T(8,128)(2,1)}, u32[]{:S(2)}) copy-start(bf16[12,48,128]{2,1,0:T(8,128)(2,1)} %get-tuple-element.118.refs_0_) | copy-start | bytes 442372
  127.4 5.8 %collective-permute-start.18 = (bf16[12,48,128]{2,1,0:T(8,128)(2,1)S(1)}, bf16[12,48,128]{2,1,0:T(8,128)(2,1)S(1)}, u32[]{:S(2)}, u32[]{:S(2)}) collective-permute-start(bf16[12,48,128]{2,1,0:T(8,128)(2,1)S(1)} %copy-done.21), channel_id=1, source_target_pairs={{0,24},{2,26},{4,28},{6,30},{1,25},{3,27},{5,29},{7,31},{8,0},{10,... | collective-permute-start | bytes 442376 | tf_op jit(solution)/shard_map/ppermute | solution.py:288
  128.7 19.0 %copy-start.1 = (bf16[12,48,128]{2,1,0:T(8,128)(2,1)S(1)}, bf16[12,48,128]{2,1,0:T(8,128)(2,1)}, u32[]{:S(2)}) copy-start(bf16[12,48,128]{2,1,0:T(8,128)(2,1)} %get-tuple-element.147.refs_0_) | copy-start | bytes 442372
  128.7 7.1 %collective-permute-start.19 = (bf16[12,48,128]{2,1,0:T(8,128)(2,1)S(1)}, bf16[12,48,128]{2,1,0:T(8,128)(2,1)S(1)}, u32[]{:S(2)}, u32[]{:S(2)}) collective-permute-start(bf16[12,48,128]{2,1,0:T(8,128)(2,1)S(1)} %copy-done.22), channel_id=1, source_target_pairs={{0,25},{2,27},{4,29},{6,31},{1,24},{3,26},{5,28},{7,30},{8,1},{10,... | collective-permute-start | bytes 442376 | tf_op jit(solution)/shard_map/ppermute | solution.py:288
  129.0 8.2 %collective-permute-start.21 = (bf16[12,48,128]{2,1,0:T(8,128)(2,1)S(1)}, bf16[12,48,128]{2,1,0:T(8,128)(2,1)S(1)}, u32[]{:S(2)}, u32[]{:S(2)}) collective-permute-start(bf16[12,48,128]{2,1,0:T(8,128)(2,1)S(1)} %copy-done.14), channel_id=1, source_target_pairs={{0,1},{2,3},{4,5},{6,7},{1,0},{3,2},{5,4},{7,6},{8,9},{10,11},{12,... | collective-permute-start | bytes 442376 | tf_op jit(solution)/shard_map/ppermute | solution.py:288
  131.4 7.3 %collective-permute-start.22 = (bf16[12,48,128]{2,1,0:T(8,128)(2,1)S(1)}, bf16[12,48,128]{2,1,0:T(8,128)(2,1)S(1)}, u32[]{:S(2)}, u32[]{:S(2)}) collective-permute-start(bf16[12,48,128]{2,1,0:T(8,128)(2,1)S(1)} %copy-done.15), channel_id=1, source_target_pairs={{0,8},{2,10},{4,12},{6,14},{1,9},{3,11},{5,13},{7,15},{8,16},{10,1... | collective-permute-start | bytes 442376 | tf_op jit(solution)/shard_map/ppermute | solution.py:288
  132.5 10.5 %collective-permute-start.23 = (bf16[12,48,128]{2,1,0:T(8,128)(2,1)S(1)}, bf16[12,48,128]{2,1,0:T(8,128)(2,1)S(1)}, u32[]{:S(2)}, u32[]{:S(2)}) collective-permute-start(bf16[12,48,128]{2,1,0:T(8,128)(2,1)S(1)} %copy-done.16), channel_id=1, source_target_pairs={{0,9},{2,11},{4,13},{6,15},{1,8},{3,10},{5,12},{7,14},{8,17},{10,1... | collective-permute-start | bytes 442376 | tf_op jit(solution)/shard_map/ppermute | solution.py:288
  133.2 11.0 %collective-permute-start.24 = (bf16[12,48,128]{2,1,0:T(8,128)(2,1)S(1)}, bf16[12,48,128]{2,1,0:T(8,128)(2,1)S(1)}, u32[]{:S(2)}, u32[]{:S(2)}) collective-permute-start(bf16[12,48,128]{2,1,0:T(8,128)(2,1)S(1)} %copy-done.17), channel_id=1, source_target_pairs={{0,16},{2,18},{4,20},{6,22},{1,17},{3,19},{5,21},{7,23},{8,24},{10... | collective-permute-start | bytes 442376 | tf_op jit(solution)/shard_map/ppermute | solution.py:288
  135.9 8.3 %collective-permute-start.25 = (bf16[12,48,128]{2,1,0:T(8,128)(2,1)S(1)}, bf16[12,48,128]{2,1,0:T(8,128)(2,1)S(1)}, u32[]{:S(2)}, u32[]{:S(2)}) collective-permute-start(bf16[12,48,128]{2,1,0:T(8,128)(2,1)S(1)} %copy-done.18), channel_id=1, source_target_pairs={{0,17},{2,19},{4,21},{6,23},{1,16},{3,18},{5,20},{7,22},{8,25},{10... | collective-permute-start | bytes 442376 | tf_op jit(solution)/shard_map/ppermute | solution.py:288
  137.2 10.5 %collective-permute-start.26 = (bf16[12,48,128]{2,1,0:T(8,128)(2,1)S(1)}, bf16[12,48,128]{2,1,0:T(8,128)(2,1)S(1)}, u32[]{:S(2)}, u32[]{:S(2)}) collective-permute-start(bf16[12,48,128]{2,1,0:T(8,128)(2,1)S(1)} %copy-done.19), channel_id=1, source_target_pairs={{0,24},{2,26},{4,28},{6,30},{1,25},{3,27},{5,29},{7,31},{8,0},{10,... | collective-permute-start | bytes 442376 | tf_op jit(solution)/shard_map/ppermute | solution.py:288
  138.7 9.0 %collective-permute-start.27 = (bf16[12,48,128]{2,1,0:T(8,128)(2,1)S(1)}, bf16[12,48,128]{2,1,0:T(8,128)(2,1)S(1)}, u32[]{:S(2)}, u32[]{:S(2)}) collective-permute-start(bf16[12,48,128]{2,1,0:T(8,128)(2,1)S(1)} %copy-done.20), channel_id=1, source_target_pairs={{0,25},{2,27},{4,29},{6,31},{1,24},{3,26},{5,28},{7,30},{8,1},{10,... | collective-permute-start | bytes 442376 | tf_op jit(solution)/shard_map/ppermute | solution.py:288
  (4 other events, 3.4 us)

commit v7 on v6

--- a/solution.py
+++ b/solution.py
@@ -320,9 +320,9 @@
     cross = []
     for c in range(chunks):
         final = c + 1 == chunks
+        if final:
+            early[c], lefts = after(early[c], lefts)
         picked = select_late(places, right_slots, pieces[c], early[c])
-        if final:
-            picked, lefts = after(picked, lefts)
         got = [to_owner(tiles, d) for d, tiles in enumerate(picked)]
         if final:
             (gram,) = pairs_call(

time: 150 us -> 150 us (level)
    unnamed x48 -> x36, local copies, waits for them, and re-layouts: 4.69 us -> 4.66 us
  transfers between devices with their start and end apart: 29 -> 29, of which waited for: 14 -> 13; matrix products, arithmetic and copies ran while one was open for 3% -> 4% of each run, Pallas kernels for 15% -> 15%
where the time goes in v7:
time: 150 us; the launch traced here: 149 us
  waiting for transfers between devices  83.6 us (56%)
  starting transfers between devices  29.8 us (20%)
  Pallas kernels  26 us (17%)
  local copies, waits for them, and re-layouts  7.36 us (5%)
    ppermute x12, waiting for transfers between devices, hop(): lax.ppermute(piece, 'feat', [(f, at_place(f // sides, k) * sides + f % si...  68.9 us
    ppermute x14, starting transfers between devices, to_owner(): return lax.ppermute(tiles, ('tok', 'feat'), perm)  17.5 us
    pallas_call x3, Pallas kernels, select_early(): pl.pallas_call(functools.partial(select_kernel, where, groups, outs, (k,...  12.5 us
    ppermute x14, waiting for transfers between devices, to_owner(): return lax.ppermute(tiles, ('tok', 'feat'), perm)  7.66 us
    ppermute x2, waiting for transfers between devices, from_sides(): lax.ppermute(blocks_of(array, (side + d) % sides), 'feat', [(f, f // side...  7.13 us
    pallas_call x3, Pallas kernels, select_late(): pl.pallas_call(functools.partial(late_kernel, k, first, per, outs), out_s...  5.95 us
    ppermute x12, starting transfers between devices, hop(): lax.ppermute(piece, 'feat', [(f, at_place(f // sides, k) * sides + f % si...  5.7 us
    all_to_all x1, starting transfers between devices, to_owners(): lax.all_to_all(tiles, ('tok', 'feat'), split_axis=0, concat_axis=0, axis_...  5.11 us
  transfers between devices with their start and end apart: 29, of which 13 were waited for; matrix products, arithmetic and copies ran while one was open for 4% of the time, Pallas kernels for 15%

profile of v7, /device:TPU:25, one launch (start us, length us, event | category | flops | bytes accessed | tf_op | source)
XLA Modules:
  0.0 149.2 jit_solution(17201893396659259676)
XLA Ops:
  0.7 1.1 copy-done
  1.9 1.3 collective-permute-start
  3.4 1.2 dynamic-slice_bitcast_fusion
  5.0 7.1 %collective-permute-done.refs_4_ = bf16[16,96,128]{2,1,0:T(8,128)(2,1)S(1)} collective-permute-done((bf16[16,96,128]{2,1,0:T(8,128)(2,1)S(1)}, bf16[16,96,128]{2,1,0:T(8,128)(2,1)S(1)}, u32[]{:S(2)}, u32[]{:S(2)}) %collective-permute-start) | collective-permute-done | bytes 393248 | tf_op jit(solution)/shard_map/ppermute | solution.py:219
  12.1 8.3 %collective-permute-done.1.refs_1_ = bf16[16,96,128]{2,1,0:T(8,128)(2,1)S(1)} collective-permute-done((bf16[16,96,128]{2,1,0:T(8,128)(2,1)S(1)}, bf16[16,96,128]{2,1,0:T(8,128)(2,1)S(1)}, u32[]{:S(2)}, u32[]{:S(2)}) %collective-permute-start.1) | collective-permute-done | bytes 393248 | tf_op jit(solution)/shard_map/ppermute | solution.py:230
  20.4 1.1 collective-permute-start.6
  21.5 0.8 reshape.385
  22.4 0.4 collective-permute-start.3
  22.9 17.7 %collective-permute-done.5.refs_5_ = bf16[16,96,128]{2,1,0:T(8,128)(2,1)} collective-permute-done((bf16[16,96,128]{2,1,0:T(8,128)(2,1)S(1)}, bf16[16,96,128]{2,1,0:T(8,128)(2,1)}, u32[]{:S(2)}, u32[]{:S(2)}) %collective-permute-start.5) | collective-permute-done | bytes 393248 | tf_op jit(solution)/shard_map/ppermute | solution.py:230
  40.9 0.6 pad_add_fusion.places_ref
  41.5 0.6 fusion.13.table_ref
  42.1 7.0 %collective-permute-done.3.refs_3_ = bf16[16,96,128]{2,1,0:T(8,128)(2,1)} collective-permute-done((bf16[16,96,128]{2,1,0:T(8,128)(2,1)}, bf16[16,96,128]{2,1,0:T(8,128)(2,1)}, u32[]{:S(2)}, u32[]{:S(2)}) %collective-permute-start.3) | collective-permute-done | bytes 393248 | tf_op jit(solution)/shard_map/ppermute | solution.py:230
  49.1 5.3 %select_tiles.3 = (bf16[192,96,128]{2,1,0:T(8,128)(2,1)}, s32[194]{0:T(256)}) custom-call(s32[4]{0:T(128)} %pad_add_fusion.places_ref, s32[192]{0:T(256)} %fusion.13.table_ref, bf16[16,96,128]{2,1,0:T(8,128)(2,1)} %copy-done.5, bf16[16,96,128]{2,1,0:T(8,128)(2,1)} %copy-done.13, bf16[16,96,128]{2,1,0:T(8,128)(2,1)} %collective-permute-done.2.refs_2_, ...), custom_call_target="tpu_custom_call" | custom-call | tf_op jit(solution)/shard_map/select_tiles/pallas_call | solution.py:85
  54.4 3.0 %collective-permute-done.7.piece = bf16[16,96,128]{2,1,0:T(8,128)(2,1)S(1)} collective-permute-done((bf16[16,96,128]{2,1,0:T(8,128)(2,1)}, bf16[16,96,128]{2,1,0:T(8,128)(2,1)S(1)}, u32[]{:S(2)}, u32[]{:S(2)}) %collective-permute-start.7) | collective-permute-done | bytes 393248 | tf_op jit(solution)/shard_map/ppermute | solution.py:230
  57.4 0.7 copy-done.6
  58.1 1.8 %late_tiles.3 = bf16[192,96,128]{2,1,0:T(8,128)(2,1)} custom-call(s32[4]{0:T(128)} %pad_add_fusion.places_ref, s32[192]{0:T(256)} %fusion.13.table_ref, s32[194]{0:T(256)} %get-tuple-element.87.list_ref, bf16[16,96,128]{2,1,0:T(8,128)(2,1)} %copy-done.6, bf16[192,96,128]{2,1,0:T(8,128)(2,1)} %get-tuple-element.88.refs_0_), custom_call_target="tpu_custom_call", output_to_operand_aliasing={{}: (4, {})} | custom-call | tf_op jit(solution)/shard_map/late_tiles/pallas_call | solution.py:109
  60.0 5.1 %all-to-all-start = ((bf16[192,96,128]{2,1,0:T(8,128)(2,1)}), bf16[192,96,128]{2,1,0:T(8,128)(2,1)}, u32[]{:S(2)}, u32[]{:S(2)}) async-start(bf16[192,96,128]{2,1,0:T(8,128)(2,1)} %late_tiles.3), calls=%async_computation | async-start | bytes 9437184 | tf_op jit(solution)/shard_map/all_to_all | solution.py:275
  65.5 2.4 %collective-permute-start.11 = (bf16[32,48,128]{2,1,0:T(8,128)(2,1)S(1)}, bf16[32,48,128]{2,1,0:T(8,128)(2,1)S(1)}, u32[]{:S(2)}, u32[]{:S(2)}) collective-permute-start(bf16[32,48,128]{2,1,0:T(8,128)(2,1)S(1)} %get-tuple-element.100.refs_0_), channel_id=1, source_target_pairs={{0,4},{1,5},{2,6},{3,7},{4,0},{5,1},{6,2},{7,3},{8,12},{9,13},{10,... | collective-permute-start | bytes 1179656 | tf_op jit(solution)/shard_map/ppermute | solution.py:230
  68.0 1.5 collective-permute-start.10
  69.4 24.3 %collective-permute-done.9.refs_2_ = bf16[32,48,128]{2,1,0:T(8,128)(2,1)S(1)} collective-permute-done((bf16[32,48,128]{2,1,0:T(8,128)(2,1)S(1)}, bf16[32,48,128]{2,1,0:T(8,128)(2,1)S(1)}, u32[]{:S(2)}, u32[]{:S(2)}) %collective-permute-start.9) | collective-permute-done | bytes 393248 | tf_op jit(solution)/shard_map/ppermute | solution.py:230
  93.7 8.3 %collective-permute-done.11.refs_2_ = bf16[32,48,128]{2,1,0:T(8,128)(2,1)S(1)} collective-permute-done((bf16[32,48,128]{2,1,0:T(8,128)(2,1)S(1)}, bf16[32,48,128]{2,1,0:T(8,128)(2,1)S(1)}, u32[]{:S(2)}, u32[]{:S(2)}) %collective-permute-start.11) | collective-permute-done | bytes 393248 | tf_op jit(solution)/shard_map/ppermute | solution.py:230
  102.0 0.6 gather_fusion
  102.6 0.6 select_n.236.table_ref
  103.3 3.6 %select_tiles.4 = (bf16[12,48,128]{2,1,0:T(8,128)(2,1)}, bf16[12,48,128]{2,1,0:T(8,128)(2,1)}, bf16[12,48,128]{2,1,0:T(8,128)(2,1)}, bf16[12,48,128]{2,1,0:T(8,1...) custom-call(s32[4]{0:T(128)} %pad_add_fusion.places_ref, ...), custom_call_target="tpu_custom_call" | custom-call | tf_op jit(solution)/shard_map/select_tiles/pallas_call | solution.py:85
  106.9 0.7 copy-done.11
  107.6 3.6 %select_tiles.5 = (bf16[12,48,128]{2,1,0:T(8,128)(2,1)}, bf16[12,48,128]{2,1,0:T(8,128)(2,1)}, bf16[12,48,128]{2,1,0:T(8,128)(2,1)}, bf16[12,48,128]{2,1,0:T(8,1...) custom-call(s32[4]{0:T(128)} %pad_add_fusion.places_ref, ...), custom_call_target="tpu_custom_call" | custom-call | tf_op jit(solution)/shard_map/select_tiles/pallas_call | solution.py:85
  111.5 0.7 copy-done.10
  112.2 2.1 %late_tiles.4 = (bf16[12,48,128]{2,1,0:T(8,128)(2,1)}, bf16[12,48,128]{2,1,0:T(8,128)(2,1)}, bf16[12,48,128]{2,1,0:T(8,128)(2,1)}, bf16[12,48,128]{2,1,0:T(8,128...) custom-call(s32[4]{0:T(128)} %pad_add_fusion.places_ref, ...), custom_call_target="tpu_custom_call", output_to_operand_aliasing={{0}: (4, {}), {1}: (5, {}), {2}: (6, {}), {3}: (7, {}), {4}... | custom-call | tf_op jit(solution)/shard_map/late_tiles/pallas_call | solution.py:109
  114.3 1.3 collective-permute-start.13
  115.7 4.5 %collective-permute-start.14 = (bf16[12,48,128]{2,1,0:T(8,128)(2,1)}, bf16[12,48,128]{2,1,0:T(8,128)(2,1)S(1)}, u32[]{:S(2)}, u32[]{:S(2)}) collective-permute-start(bf16[12,48,128]{2,1,0:T(8,128)(2,1)} %get-tuple-element.121), channel_id=1, source_target_pairs={{0,8},{2,10},{4,12},{6,14},{1,9},{3,11},{5,13},{7,15},{8,16},{10,1... | collective-permute-start | bytes 442376 | tf_op jit(solution)/shard_map/ppermute | solution.py:288
  120.5 2.1 %left_tiles.1 = (bf16[12,128,384]{2,1,0:T(8,128)(2,1)S(1)}, bf16[12,128,384]{2,1,0:T(8,128)(2,1)S(1)}) custom-call(s32[8]{0:T(128)S(1)} %stack.93.order_ref, bf16[8,12,2,96,128]{4,3,2,1,0:T(8,128)(2,1)} %bitcast.16.tiles.refs_2_), custom_call_target="tpu_custom_call" | custom-call | tf_op jit(solution)/shard_map/left_tiles/pallas_call | solution.py:154
  122.6 2.2 %collective-permute-start.17 = (bf16[12,48,128]{2,1,0:T(8,128)(2,1)S(1)}, bf16[12,48,128]{2,1,0:T(8,128)(2,1)S(1)}, u32[]{:S(2)}, u32[]{:S(2)}) collective-permute-start(bf16[12,48,128]{2,1,0:T(8,128)(2,1)S(1)} %copy-done.14), channel_id=1, source_target_pairs={{0,17},{2,19},{4,21},{6,23},{1,16},{3,18},{5,20},{7,22},{8,25},{10... | collective-permute-start | bytes 442376 | tf_op jit(solution)/shard_map/ppermute | solution.py:288
  124.8 2.1 %late_tiles.5 = (bf16[12,48,128]{2,1,0:T(8,128)(2,1)}, bf16[12,48,128]{2,1,0:T(8,128)(2,1)}, bf16[12,48,128]{2,1,0:T(8,128)(2,1)}, bf16[12,48,128]{2,1,0:T(8,128...) custom-call(s32[4]{0:T(128)} %pad_add_fusion.places_ref, ...), custom_call_target="tpu_custom_call", output_to_operand_aliasing={{0}: (4, {}), {1}: (5, {}), {2}: (6, {}), {3}: (7, {}), {4}... | custom-call | tf_op jit(solution)/shard_map/late_tiles/pallas_call | solution.py:109
  126.9 1.3 collective-permute-start.18
  128.4 1.2 collective-permute-start.21
  129.6 1.6 %collective-permute-done.16.refs_4_ = bf16[12,48,128]{2,1,0:T(8,128)(2,1)S(1)} collective-permute-done((bf16[12,48,128]{2,1,0:T(8,128)(2,1)}, bf16[12,48,128]{2,1,0:T(8,128)(2,1)S(1)}, u32[]{:S(2)}, u32[]{:S(2)}) %collective-permute-start.16) | collective-permute-done | bytes 147488 | tf_op jit(solution)/shard_map/ppermute | solution.py:288
  131.3 1.0 collective-permute-start.22
  132.3 0.6 collective-permute-start.23
  132.9 0.6 collective-permute-done.18.refs_6_
  133.5 2.4 %collective-permute-start.24 = (bf16[12,48,128]{2,1,0:T(8,128)(2,1)}, bf16[12,48,128]{2,1,0:T(8,128)(2,1)S(1)}, u32[]{:S(2)}, u32[]{:S(2)}) collective-permute-start(bf16[12,48,128]{2,1,0:T(8,128)(2,1)} %get-tuple-element.153), channel_id=1, source_target_pairs={{0,16},{2,18},{4,20},{6,22},{1,17},{3,19},{5,21},{7,23},{8,24},{10... | collective-permute-start | bytes 442376 | tf_op jit(solution)/shard_map/ppermute | solution.py:288
  136.2 0.5 collective-permute-done.21.refs_1_
  136.7 1.5 collective-permute-start.26
  138.1 0.7 collective-permute-start.27
  138.9 3.0 %gram_sum.1 = f32[12,128,128]{2,1,0:T(8,128)} custom-call(s32[8]{0:T(128)S(1)} %stack.93.order_ref, bf16[12,128,384]{2,1,0:T(8,128)(2,1)S(1)} %get-tuple-element.137.left_ref.refs_0_, bf16[12,128,384]{2,1,0:T(8,128)(2,1)S(1)} %get-tuple-element.138.refs_1_.left_ref, bf16[8,12,2,96,128]{4,3,2,1,0:T(8,128)(2,1)} %bitcast.16.tiles.refs_2_), custom_call_target="tpu_custom_call" | custom-call | tf_op jit(solution)/shard_map/gram_sum/pallas_call | solution.py:154
  141.9 0.8 cross_sum.2.refs_8_
  142.7 2.2 %collective-permute-done.24.refs_4_ = bf16[12,48,128]{2,1,0:T(8,128)(2,1)S(1)} collective-permute-done((bf16[12,48,128]{2,1,0:T(8,128)(2,1)}, bf16[12,48,128]{2,1,0:T(8,128)(2,1)S(1)}, u32[]{:S(2)}, u32[]{:S(2)}) %collective-permute-start.24) | collective-permute-done | bytes 147488 | tf_op jit(solution)/shard_map/ppermute | solution.py:288
  144.9 2.7 %collective-permute-done.26.refs_6_ = bf16[12,48,128]{2,1,0:T(8,128)(2,1)S(1)} collective-permute-done((bf16[12,48,128]{2,1,0:T(8,128)(2,1)}, bf16[12,48,128]{2,1,0:T(8,128)(2,1)S(1)}, u32[]{:S(2)}, u32[]{:S(2)}) %collective-permute-start.26) | collective-permute-done | bytes 147488 | tf_op jit(solution)/shard_map/ppermute | solution.py:288
  147.6 1.7 %cross_sum.3 = f32[12,128,128]{2,1,0:T(8,128)} custom-call(bf16[12,128,384]{2,1,0:T(8,128)(2,1)S(1)} %get-tuple-element.138.refs_1_.left_ref, bf16[12,48,128]{2,1,0:T(8,128)(2,1)S(1)} %copy-done.1, bf16[12,48,128]{2,1,0:T(8,128)(2,1)S(1)} %collective-permute-done.21.refs_1_, bf16[12,48,128]{2,1,0:T(8,128)(2,1)S(1)} %collective-permute-done.22.refs_2_, ...), custom_call_target="tpu_custom_call" | custom-call | tf_op jit(solution)/shard_map/cross_sum/pallas_call | solution.py:179
  (79 shorter events, 2.8 us)
Async XLA Ops:
  0.6 1.1 copy-start
  1.8 47.2 %copy-start.5 = (bf16[16,96,128]{2,1,0:T(8,128)(2,1)}, bf16[16,96,128]{2,1,0:T(8,128)(2,1)S(1)}, u32[]{:S(2)}) copy-start(bf16[16,96,128]{2,1,0:T(8,128)(2,1)S(1)} %bitcast_bitcast_fusion.3.refs_0_) | copy-start | bytes 1179652
  1.9 10.2 %collective-permute-start = (bf16[16,96,128]{2,1,0:T(8,128)(2,1)S(1)}, bf16[16,96,128]{2,1,0:T(8,128)(2,1)S(1)}, u32[]{:S(2)}, u32[]{:S(2)}) collective-permute-start(bf16[16,96,128]{2,1,0:T(8,128)(2,1)S(1)} %bitcast_bitcast_fusion.2), channel_id=1, source_target_pairs={{0,1},{1,0},{2,3},{3,2},{4,5},{5,4},{6,7},{7,6},{8,9},{9,8},{10,11... | collective-permute-start | bytes 1179656 | tf_op jit(solution)/shard_map/ppermute | solution.py:219
  3.2 17.2 %collective-permute-start.1 = (bf16[16,96,128]{2,1,0:T(8,128)(2,1)S(1)}, bf16[16,96,128]{2,1,0:T(8,128)(2,1)S(1)}, u32[]{:S(2)}, u32[]{:S(2)}) collective-permute-start(bf16[16,96,128]{2,1,0:T(8,128)(2,1)S(1)} %bitcast_bitcast_fusion.3.refs_0_), channel_id=1, source_target_pairs={{0,2},{1,3},{2,0},{3,1},{4,6},{5,7},{6,4},{7,5},{8,10},{9,11},{10,... | collective-permute-start | bytes 1179656 | tf_op jit(solution)/shard_map/ppermute | solution.py:230
  3.4 19.0 %collective-permute-start.2 = (bf16[16,96,128]{2,1,0:T(8,128)(2,1)S(1)}, bf16[16,96,128]{2,1,0:T(8,128)(2,1)}, u32[]{:S(2)}, u32[]{:S(2)}) collective-permute-start(bf16[16,96,128]{2,1,0:T(8,128)(2,1)S(1)} %bitcast_bitcast_fusion.3.refs_0_), channel_id=1, source_target_pairs={{0,4},{1,5},{2,6},{3,7},{4,0},{5,1},{6,2},{7,3},{8,12},{9,13},{10,... | collective-permute-start | bytes 1179656 | tf_op jit(solution)/shard_map/ppermute | solution.py:230
  4.7 18.1 %collective-permute-start.4 = (bf16[16,96,128]{2,1,0:T(8,128)(2,1)S(1)}, bf16[16,96,128]{2,1,0:T(8,128)(2,1)S(1)}, u32[]{:S(2)}, u32[]{:S(2)}) collective-permute-start(bf16[16,96,128]{2,1,0:T(8,128)(2,1)S(1)} %bitcast.72), channel_id=1, source_target_pairs={{0,1},{1,0},{2,3},{3,2},{4,5},{5,4},{6,7},{7,6},{8,9},{9,8},{10,11... | collective-permute-start | bytes 1179656 | tf_op jit(solution)/shard_map/ppermute | solution.py:219
  12.1 37.0 %copy-start.12 = (bf16[16,96,128]{2,1,0:T(8,128)(2,1)}, bf16[16,96,128]{2,1,0:T(8,128)(2,1)S(1)}, u32[]{:S(2)}) copy-start(bf16[16,96,128]{2,1,0:T(8,128)(2,1)S(1)} %collective-permute-done.refs_4_) | copy-start | bytes 1179652
  20.4 28.7 %copy-start.13 = (bf16[16,96,128]{2,1,0:T(8,128)(2,1)}, bf16[16,96,128]{2,1,0:T(8,128)(2,1)S(1)}, u32[]{:S(2)}) copy-start(bf16[16,96,128]{2,1,0:T(8,128)(2,1)S(1)} %collective-permute-done.1.refs_1_) | copy-start | bytes 1179652
  20.4 20.2 %collective-permute-start.5 = (bf16[16,96,128]{2,1,0:T(8,128)(2,1)S(1)}, bf16[16,96,128]{2,1,0:T(8,128)(2,1)}, u32[]{:S(2)}, u32[]{:S(2)}) collective-permute-start(bf16[16,96,128]{2,1,0:T(8,128)(2,1)S(1)} %collective-permute-done.refs_4_), channel_id=1, source_target_pairs={{0,2},{1,3},{2,0},{3,1},{4,6},{5,7},{6,4},{7,5},{8,10},{9,11},{10,... | collective-permute-start | bytes 1179656 | tf_op jit(solution)/shard_map/ppermute | solution.py:230
  20.4 20.2 %collective-permute-start.6 = (bf16[16,96,128]{2,1,0:T(8,128)(2,1)S(1)}, bf16[16,96,128]{2,1,0:T(8,128)(2,1)}, u32[]{:S(2)}, u32[]{:S(2)}) collective-permute-start(bf16[16,96,128]{2,1,0:T(8,128)(2,1)S(1)} %collective-permute-done.refs_4_), channel_id=1, source_target_pairs={{0,4},{1,5},{2,6},{3,7},{4,0},{5,1},{6,2},{7,3},{8,12},{9,13},{10,... | collective-permute-start | bytes 1179656 | tf_op jit(solution)/shard_map/ppermute | solution.py:230
  22.4 26.7 %collective-permute-start.3 = (bf16[16,96,128]{2,1,0:T(8,128)(2,1)}, bf16[16,96,128]{2,1,0:T(8,128)(2,1)}, u32[]{:S(2)}, u32[]{:S(2)}) collective-permute-start(bf16[16,96,128]{2,1,0:T(8,128)(2,1)} %collective-permute-done.2.refs_2_), channel_id=1, source_target_pairs={{0,2},{1,3},{2,0},{3,1},{4,6},{5,7},{6,4},{7,5},{8,10},{9,11},{10,... | collective-permute-start | bytes 1179656 | tf_op jit(solution)/shard_map/ppermute | solution.py:230
  22.9 45.1 %copy-start.4 = (bf16[32,48,128]{2,1,0:T(8,128)(2,1)}, bf16[32,48,128]{2,1,0:T(8,128)(2,1)S(1)}, u32[]{:S(2)}) copy-start(bf16[32,48,128]{2,1,0:T(8,128)(2,1)S(1)} %get-tuple-element.90.refs_0_) | copy-start | bytes 1179652
  22.9 45.1 %copy-start.3 = (bf16[32,48,128]{2,1,0:T(8,128)(2,1)}, bf16[32,48,128]{2,1,0:T(8,128)(2,1)S(1)}, u32[]{:S(2)}) copy-start(bf16[32,48,128]{2,1,0:T(8,128)(2,1)S(1)} %get-tuple-element.100.refs_0_) | copy-start | bytes 1179652
  40.7 16.7 %collective-permute-start.7 = (bf16[16,96,128]{2,1,0:T(8,128)(2,1)}, bf16[16,96,128]{2,1,0:T(8,128)(2,1)S(1)}, u32[]{:S(2)}, u32[]{:S(2)}) collective-permute-start(bf16[16,96,128]{2,1,0:T(8,128)(2,1)} %collective-permute-done.6.refs_6_), channel_id=1, source_target_pairs={{0,2},{1,3},{2,0},{3,1},{4,6},{5,7},{6,4},{7,5},{8,10},{9,11},{10,... | collective-permute-start | bytes 1179656 | tf_op jit(solution)/shard_map/ppermute | solution.py:230
  57.4 0.7 copy-start.6
  60.0 60.5 %all-to-all-start = ((bf16[192,96,128]{2,1,0:T(8,128)(2,1)}), bf16[192,96,128]{2,1,0:T(8,128)(2,1)}, u32[]{:S(2)}, u32[]{:S(2)}) async-start(bf16[192,96,128]{2,1,0:T(8,128)(2,1)} %late_tiles.3), calls=%async_computation | async-start | bytes 9437184 | tf_op jit(solution)/shard_map/all_to_all | solution.py:275
  65.4 28.2 %collective-permute-start.9 = (bf16[32,48,128]{2,1,0:T(8,128)(2,1)S(1)}, bf16[32,48,128]{2,1,0:T(8,128)(2,1)S(1)}, u32[]{:S(2)}, u32[]{:S(2)}) collective-permute-start(bf16[32,48,128]{2,1,0:T(8,128)(2,1)S(1)} %get-tuple-element.90.refs_0_), channel_id=1, source_target_pairs={{0,4},{1,5},{2,6},{3,7},{4,0},{5,1},{6,2},{7,3},{8,12},{9,13},{10,... | collective-permute-start | bytes 1179656 | tf_op jit(solution)/shard_map/ppermute | solution.py:230
  65.5 36.5 %collective-permute-start.11 = (bf16[32,48,128]{2,1,0:T(8,128)(2,1)S(1)}, bf16[32,48,128]{2,1,0:T(8,128)(2,1)S(1)}, u32[]{:S(2)}, u32[]{:S(2)}) collective-permute-start(bf16[32,48,128]{2,1,0:T(8,128)(2,1)S(1)} %get-tuple-element.100.refs_0_), channel_id=1, source_target_pairs={{0,4},{1,5},{2,6},{3,7},{4,0},{5,1},{6,2},{7,3},{8,12},{9,13},{10,... | collective-permute-start | bytes 1179656 | tf_op jit(solution)/shard_map/ppermute | solution.py:230
  67.9 35.3 %collective-permute-start.8 = (bf16[32,48,128]{2,1,0:T(8,128)(2,1)S(1)}, bf16[32,48,128]{2,1,0:T(8,128)(2,1)}, u32[]{:S(2)}, u32[]{:S(2)}) collective-permute-start(bf16[32,48,128]{2,1,0:T(8,128)(2,1)S(1)} %get-tuple-element.90.refs_0_), channel_id=1, source_target_pairs={{0,2},{1,3},{2,0},{3,1},{4,6},{5,7},{6,4},{7,5},{8,10},{9,11},{10,... | collective-permute-start | bytes 1179656 | tf_op jit(solution)/shard_map/ppermute | solution.py:230
  68.0 38.9 %collective-permute-start.10 = (bf16[32,48,128]{2,1,0:T(8,128)(2,1)S(1)}, bf16[32,48,128]{2,1,0:T(8,128)(2,1)S(1)}, u32[]{:S(2)}, u32[]{:S(2)}) collective-permute-start(bf16[32,48,128]{2,1,0:T(8,128)(2,1)S(1)} %get-tuple-element.100.refs_0_), channel_id=1, source_target_pairs={{0,2},{1,3},{2,0},{3,1},{4,6},{5,7},{6,4},{7,5},{8,10},{9,11},{10,... | collective-permute-start | bytes 1179656 | tf_op jit(solution)/shard_map/ppermute | solution.py:230
  93.7 9.6 %copy-start.9 = (bf16[32,48,128]{2,1,0:T(8,128)(2,1)}, bf16[32,48,128]{2,1,0:T(8,128)(2,1)S(1)}, u32[]{:S(2)}) copy-start(bf16[32,48,128]{2,1,0:T(8,128)(2,1)S(1)} %collective-permute-done.9.refs_2_) | copy-start | bytes 1179652
  93.7 17.8 %collective-permute-start.12 = (bf16[32,48,128]{2,1,0:T(8,128)(2,1)S(1)}, bf16[32,48,128]{2,1,0:T(8,128)(2,1)S(1)}, u32[]{:S(2)}, u32[]{:S(2)}) collective-permute-start(bf16[32,48,128]{2,1,0:T(8,128)(2,1)S(1)} %collective-permute-done.9.refs_2_), channel_id=1, source_target_pairs={{0,2},{1,3},{2,0},{3,1},{4,6},{5,7},{6,4},{7,5},{8,10},{9,11},{10,... | collective-permute-start | bytes 1179656 | tf_op jit(solution)/shard_map/ppermute | solution.py:230
  102.0 4.9 %copy-start.7 = (bf16[32,48,128]{2,1,0:T(8,128)(2,1)}, bf16[32,48,128]{2,1,0:T(8,128)(2,1)S(1)}, u32[]{:S(2)}) copy-start(bf16[32,48,128]{2,1,0:T(8,128)(2,1)S(1)} %collective-permute-done.11.refs_2_) | copy-start | bytes 1179652
  102.0 20.6 %collective-permute-start.20 = (bf16[32,48,128]{2,1,0:T(8,128)(2,1)S(1)}, bf16[32,48,128]{2,1,0:T(8,128)(2,1)S(1)}, u32[]{:S(2)}, u32[]{:S(2)}) collective-permute-start(bf16[32,48,128]{2,1,0:T(8,128)(2,1)S(1)} %collective-permute-done.11.refs_2_), channel_id=1, source_target_pairs={{0,2},{1,3},{2,0},{3,1},{4,6},{5,7},{6,4},{7,5},{8,10},{9,11},{10,... | collective-permute-start | bytes 1179656 | tf_op jit(solution)/shard_map/ppermute | solution.py:230
  106.9 0.7 copy-start.11
  111.5 0.7 copy-start.10
  114.3 8.3 %copy-start.14 = (bf16[12,48,128]{2,1,0:T(8,128)(2,1)S(1)}, bf16[12,48,128]{2,1,0:T(8,128)(2,1)}, u32[]{:S(2)}) copy-start(bf16[12,48,128]{2,1,0:T(8,128)(2,1)} %get-tuple-element.124) | copy-start | bytes 442372
  114.3 12.6 %copy-start.15 = (bf16[12,48,128]{2,1,0:T(8,128)(2,1)S(1)}, bf16[12,48,128]{2,1,0:T(8,128)(2,1)}, u32[]{:S(2)}) copy-start(bf16[12,48,128]{2,1,0:T(8,128)(2,1)} %get-tuple-element.125) | copy-start | bytes 442372
  114.3 13.9 %copy-start.16 = (bf16[12,48,128]{2,1,0:T(8,128)(2,1)S(1)}, bf16[12,48,128]{2,1,0:T(8,128)(2,1)}, u32[]{:S(2)}) copy-start(bf16[12,48,128]{2,1,0:T(8,128)(2,1)} %get-tuple-element.126) | copy-start | bytes 442372
  114.3 12.6 %collective-permute-start.13 = (bf16[12,48,128]{2,1,0:T(8,128)(2,1)}, bf16[12,48,128]{2,1,0:T(8,128)(2,1)S(1)}, u32[]{:S(2)}, u32[]{:S(2)}) collective-permute-start(bf16[12,48,128]{2,1,0:T(8,128)(2,1)} %get-tuple-element.120), channel_id=1, source_target_pairs={{0,1},{2,3},{4,5},{6,7},{1,0},{3,2},{5,4},{7,6},{8,9},{10,11},{12,... | collective-permute-start | bytes 442376 | tf_op jit(solution)/shard_map/ppermute | solution.py:288
  115.7 12.5 %collective-permute-start.14 = (bf16[12,48,128]{2,1,0:T(8,128)(2,1)}, bf16[12,48,128]{2,1,0:T(8,128)(2,1)S(1)}, u32[]{:S(2)}, u32[]{:S(2)}) collective-permute-start(bf16[12,48,128]{2,1,0:T(8,128)(2,1)} %get-tuple-element.121), channel_id=1, source_target_pairs={{0,8},{2,10},{4,12},{6,14},{1,9},{3,11},{5,13},{7,15},{8,16},{10,1... | collective-permute-start | bytes 442376 | tf_op jit(solution)/shard_map/ppermute | solution.py:288
  120.2 8.3 %collective-permute-start.15 = (bf16[12,48,128]{2,1,0:T(8,128)(2,1)}, bf16[12,48,128]{2,1,0:T(8,128)(2,1)S(1)}, u32[]{:S(2)}, u32[]{:S(2)}) collective-permute-start(bf16[12,48,128]{2,1,0:T(8,128)(2,1)} %get-tuple-element.122), channel_id=1, source_target_pairs={{0,9},{2,11},{4,13},{6,15},{1,8},{3,10},{5,12},{7,14},{8,17},{10,1... | collective-permute-start | bytes 442376 | tf_op jit(solution)/shard_map/ppermute | solution.py:288
  120.2 11.1 %collective-permute-start.16 = (bf16[12,48,128]{2,1,0:T(8,128)(2,1)}, bf16[12,48,128]{2,1,0:T(8,128)(2,1)S(1)}, u32[]{:S(2)}, u32[]{:S(2)}) collective-permute-start(bf16[12,48,128]{2,1,0:T(8,128)(2,1)} %get-tuple-element.123), channel_id=1, source_target_pairs={{0,16},{2,18},{4,20},{6,22},{1,17},{3,19},{5,21},{7,23},{8,24},{10... | collective-permute-start | bytes 442376 | tf_op jit(solution)/shard_map/ppermute | solution.py:288
  122.6 2.2 %copy-start.8 = (bf16[32,48,128]{2,1,0:T(8,128)(2,1)}, bf16[32,48,128]{2,1,0:T(8,128)(2,1)S(1)}, u32[]{:S(2)}) copy-start(bf16[32,48,128]{2,1,0:T(8,128)(2,1)S(1)} %collective-permute-done.20.piece) | copy-start | bytes 1179652
  122.6 19.2 %copy-start.2 = (bf16[12,48,128]{2,1,0:T(8,128)(2,1)S(1)}, bf16[12,48,128]{2,1,0:T(8,128)(2,1)}, u32[]{:S(2)}) copy-start(bf16[12,48,128]{2,1,0:T(8,128)(2,1)} %get-tuple-element.119.refs_0_) | copy-start | bytes 442372
  122.6 9.6 %collective-permute-start.17 = (bf16[12,48,128]{2,1,0:T(8,128)(2,1)S(1)}, bf16[12,48,128]{2,1,0:T(8,128)(2,1)S(1)}, u32[]{:S(2)}, u32[]{:S(2)}) collective-permute-start(bf16[12,48,128]{2,1,0:T(8,128)(2,1)S(1)} %copy-done.14), channel_id=1, source_target_pairs={{0,17},{2,19},{4,21},{6,23},{1,16},{3,18},{5,20},{7,22},{8,25},{10... | collective-permute-start | bytes 442376 | tf_op jit(solution)/shard_map/ppermute | solution.py:288
  126.9 6.6 %collective-permute-start.18 = (bf16[12,48,128]{2,1,0:T(8,128)(2,1)S(1)}, bf16[12,48,128]{2,1,0:T(8,128)(2,1)S(1)}, u32[]{:S(2)}, u32[]{:S(2)}) collective-permute-start(bf16[12,48,128]{2,1,0:T(8,128)(2,1)S(1)} %copy-done.15), channel_id=1, source_target_pairs={{0,24},{2,26},{4,28},{6,30},{1,25},{3,27},{5,29},{7,31},{8,0},{10,... | collective-permute-start | bytes 442376 | tf_op jit(solution)/shard_map/ppermute | solution.py:288
  128.2 7.7 %collective-permute-start.19 = (bf16[12,48,128]{2,1,0:T(8,128)(2,1)S(1)}, bf16[12,48,128]{2,1,0:T(8,128)(2,1)S(1)}, u32[]{:S(2)}, u32[]{:S(2)}) collective-permute-start(bf16[12,48,128]{2,1,0:T(8,128)(2,1)S(1)} %copy-done.16), channel_id=1, source_target_pairs={{0,25},{2,27},{4,29},{6,31},{1,24},{3,26},{5,28},{7,30},{8,1},{10,... | collective-permute-start | bytes 442376 | tf_op jit(solution)/shard_map/ppermute | solution.py:288
  128.4 8.2 %collective-permute-start.21 = (bf16[12,48,128]{2,1,0:T(8,128)(2,1)}, bf16[12,48,128]{2,1,0:T(8,128)(2,1)S(1)}, u32[]{:S(2)}, u32[]{:S(2)}) collective-permute-start(bf16[12,48,128]{2,1,0:T(8,128)(2,1)} %get-tuple-element.150), channel_id=1, source_target_pairs={{0,1},{2,3},{4,5},{6,7},{1,0},{3,2},{5,4},{7,6},{8,9},{10,11},{12,... | collective-permute-start | bytes 442376 | tf_op jit(solution)/shard_map/ppermute | solution.py:288
  131.3 6.8 %collective-permute-start.22 = (bf16[12,48,128]{2,1,0:T(8,128)(2,1)}, bf16[12,48,128]{2,1,0:T(8,128)(2,1)S(1)}, u32[]{:S(2)}, u32[]{:S(2)}) collective-permute-start(bf16[12,48,128]{2,1,0:T(8,128)(2,1)} %get-tuple-element.151), channel_id=1, source_target_pairs={{0,8},{2,10},{4,12},{6,14},{1,9},{3,11},{5,13},{7,15},{8,16},{10,1... | collective-permute-start | bytes 442376 | tf_op jit(solution)/shard_map/ppermute | solution.py:288
  132.3 10.4 %collective-permute-start.23 = (bf16[12,48,128]{2,1,0:T(8,128)(2,1)}, bf16[12,48,128]{2,1,0:T(8,128)(2,1)S(1)}, u32[]{:S(2)}, u32[]{:S(2)}) collective-permute-start(bf16[12,48,128]{2,1,0:T(8,128)(2,1)} %get-tuple-element.152), channel_id=1, source_target_pairs={{0,9},{2,11},{4,13},{6,15},{1,8},{3,10},{5,12},{7,14},{8,17},{10,1... | collective-permute-start | bytes 442376 | tf_op jit(solution)/shard_map/ppermute | solution.py:288
  133.5 11.4 %collective-permute-start.24 = (bf16[12,48,128]{2,1,0:T(8,128)(2,1)}, bf16[12,48,128]{2,1,0:T(8,128)(2,1)S(1)}, u32[]{:S(2)}, u32[]{:S(2)}) collective-permute-start(bf16[12,48,128]{2,1,0:T(8,128)(2,1)} %get-tuple-element.153), channel_id=1, source_target_pairs={{0,16},{2,18},{4,20},{6,22},{1,17},{3,19},{5,21},{7,23},{8,24},{10... | collective-permute-start | bytes 442376 | tf_op jit(solution)/shard_map/ppermute | solution.py:288
  135.9 8.9 %collective-permute-start.25 = (bf16[12,48,128]{2,1,0:T(8,128)(2,1)}, bf16[12,48,128]{2,1,0:T(8,128)(2,1)S(1)}, u32[]{:S(2)}, u32[]{:S(2)}) collective-permute-start(bf16[12,48,128]{2,1,0:T(8,128)(2,1)} %get-tuple-element.154), channel_id=1, source_target_pairs={{0,17},{2,19},{4,21},{6,23},{1,16},{3,18},{5,20},{7,22},{8,25},{10... | collective-permute-start | bytes 442376 | tf_op jit(solution)/shard_map/ppermute | solution.py:288
  136.7 10.9 %collective-permute-start.26 = (bf16[12,48,128]{2,1,0:T(8,128)(2,1)}, bf16[12,48,128]{2,1,0:T(8,128)(2,1)S(1)}, u32[]{:S(2)}, u32[]{:S(2)}) collective-permute-start(bf16[12,48,128]{2,1,0:T(8,128)(2,1)} %get-tuple-element.155), channel_id=1, source_target_pairs={{0,24},{2,26},{4,28},{6,30},{1,25},{3,27},{5,29},{7,31},{8,0},{10,... | collective-permute-start | bytes 442376 | tf_op jit(solution)/shard_map/ppermute | solution.py:288
  138.1 9.4 %copy-start.1 = (bf16[12,48,128]{2,1,0:T(8,128)(2,1)S(1)}, bf16[12,48,128]{2,1,0:T(8,128)(2,1)}, u32[]{:S(2)}) copy-start(bf16[12,48,128]{2,1,0:T(8,128)(2,1)} %get-tuple-element.149.refs_0_) | copy-start | bytes 442372
  138.1 9.4 %collective-permute-start.27 = (bf16[12,48,128]{2,1,0:T(8,128)(2,1)}, bf16[12,48,128]{2,1,0:T(8,128)(2,1)S(1)}, u32[]{:S(2)}, u32[]{:S(2)}) collective-permute-start(bf16[12,48,128]{2,1,0:T(8,128)(2,1)} %get-tuple-element.156), channel_id=1, source_target_pairs={{0,25},{2,27},{4,29},{6,31},{1,24},{3,26},{5,28},{7,30},{8,1},{10,... | collective-permute-start | bytes 442376 | tf_op jit(solution)/shard_map/ppermute | solution.py:288
